TPU v7x, 128 devices: a whole 4x4x4 slice. The times are simulated.
128 devices in a mesh: dp: 8 (over y, z_lo), tensor: 16 (over x, z_hi, core).
Axes of the slice: x: 4, y: 4, z: 4 (z_hi: 2, z_lo: 2; z = z_hi * 2 + z_lo), core: 2. Of those that a mesh axis runs over, the one named last changes fastest.
Arguments:
- attn_out: bfloat16 [8192, 2048], P('tensor', 'dp'), may hold values from -6 to 6
- o_proj: bfloat16 [4096, 8192], P(None, 'tensor'), may hold values from -0.0625 to 0.0625
- high_resid: bfloat16 [4096, 2048], P('tensor', 'dp'), may hold values from -6 to 6
- low_hidden: bfloat16 [4096, 2048], P('tensor', 'dp'), may hold values from -6 to 6
- mid_hidden: bfloat16 [4096, 2048], P('tensor', 'dp'), may hold values from -6 to 6
- route_list: int32 [2048], P('dp'), may hold values from 0 to 7, as said below
- fc_weight: bfloat16 [8, 4096, 3, 4096], P('dp', None, None, 'tensor'), may hold values from -0.0546875 to 0.0546875
- norm_gain: float32 [8, 4096], P('dp', 'tensor'), may hold values from 0.25 to 1.75
- cotangent: bfloat16 [4096, 2048], P('tensor', 'dp'), may hold values from -0.29882812 to 0.29882812
Outputs:
- draft_hidden: bfloat16 [4096, 2048], P('tensor', 'dp')
- fc_grad: float32 [8, 4096, 3, 4096], P('dp', None, None, 'tensor')
- gain_grad: float32 [8, 4096], P('dp', 'tensor')
Inputs may be any that keep to these rules, and one draw needn't show every extreme that they name: `route_list`: in each replica's block of 256 tokens every trainer is named at most 128 times, and in every draw one trainer is named exactly 128 times in every block.
All inputs are finite; a program needn't handle non-finite values.
Results may differ from a plain program's by a relative error of at most 0.004.
Values may be sent and summed in bfloat16 or wider, within the bound.
No kernel may reach another device: no remote copies, remote signals or barrier semaphores. Data moves between devices by JAX's collectives and lax.ppermute only.
A program may use at most 128 MiB of HBM per device.

v0:
```python
import jax
import jax.numpy as jnp
from jax import lax
from jax.sharding import PartitionSpec as P

DOUT = 4096


epsilon = 1e-05


def local(
    attn_out,
    o_proj,
    high_resid,
    low_hidden,
    mid_hidden,
    route_list,
    fc_weight,
    norm_gain,
    cotangent,
):
    trainers = lax.axis_size("dp")
    tok_rows = route_list.shape[0]
    capacity = tok_rows // 2
    slots = trainers * capacity
    onehot = (route_list[:, None] == jnp.arange(trainers, dtype=jnp.int32)[None, :]).astype(
        jnp.int32
    )
    earlier = jnp.cumsum(onehot, axis=0) - onehot
    within = jnp.sum(earlier * onehot, axis=1)
    slot_of_token = route_list * capacity + within
    token_of_slot = (
        jnp.zeros((slots,), jnp.int32).at[slot_of_token].set(jnp.arange(tok_rows, dtype=jnp.int32))
    )
    filled = jnp.zeros((slots,), jnp.bool_).at[slot_of_token].set(True)

    def packed(values):
        picked = jnp.take(values, token_of_slot, axis=-1)
        return jnp.where(filled, picked, jnp.zeros((), values.dtype))

    block = o_proj
    high_part = lax.psum_scatter(
        jnp.dot(block, attn_out, preferred_element_type=jnp.float32),
        "tensor",
        scatter_dimension=0,
        tiled=True,
    )
    high_hidden = (high_resid.astype(jnp.float32) + high_part).astype(jnp.bfloat16)
    rows_in, grad_in = (
        lax.all_to_all(
            packed(jnp.stack([low_hidden, mid_hidden, high_hidden])),
            "dp",
            split_axis=2,
            concat_axis=2,
            tiled=True,
        ),
        lax.all_to_all(packed(cotangent)[None], "dp", split_axis=2, concat_axis=2, tiled=True),
    )
    weight = fc_weight.reshape(fc_weight.shape[1], -1)
    rows_flat = rows_in.reshape(-1, slots)
    block = weight
    draft_pre = lax.psum_scatter(
        jnp.dot(block, rows_flat, preferred_element_type=jnp.float32),
        "tensor",
        scatter_dimension=0,
        tiled=True,
    )
    gain = norm_gain[0][:, None]
    upstream_raw = grad_in[0].astype(jnp.float32)
    upstream = gain * upstream_raw
    square_total = lax.psum(jnp.sum(draft_pre * draft_pre, axis=0), "tensor")
    root_mean = jnp.sqrt(square_total / DOUT + epsilon)
    normed = draft_pre / root_mean
    slope = lax.psum(jnp.sum(upstream * normed, axis=0), "tensor")
    outputs = (gain * normed).astype(jnp.bfloat16)
    gain_grad = jnp.sum(upstream_raw * normed, axis=1)[None, :]
    pre_grad = ((upstream - normed * slope / DOUT) / root_mean).astype(jnp.bfloat16)
    weight_grad = lax.dot_general(
        lax.all_gather(pre_grad, "tensor", axis=0, tiled=True),
        rows_flat,
        (((1,), (1,)), ((), ())),
        preferred_element_type=jnp.float32,
    )
    returned = lax.all_to_all(outputs, "dp", split_axis=1, concat_axis=1, tiled=True)
    draft_hidden = jnp.take(returned, slot_of_token, axis=1)
    fc_grad = weight_grad.reshape(fc_weight.shape)
    return (draft_hidden, fc_grad, gain_grad)


def solution(mesh):
    return jax.shard_map(
        local,
        mesh=mesh,
        in_specs=(
            P("tensor", "dp"),
            P(None, "tensor"),
            P("tensor", "dp"),
            P("tensor", "dp"),
            P("tensor", "dp"),
            P("dp"),
            P("dp", None, None, "tensor"),
            P("dp", "tensor"),
            P("tensor", "dp"),
        ),
        out_specs=(P("tensor", "dp"), P("dp", None, None, "tensor"), P("dp", "tensor")),
        check_vma=False,
    )
```

profile of v0, /device:TPU:1, one launch (start us, length us, event | category | flops | bytes accessed | tf_op | source)
XLA Modules:
  0.0 471.8 jit_solution(8461513535569712851)
XLA Ops:
  7.2 0.9 copy-done
  8.1 5.4 %fusion.21 = f32[4096,256]{1,0:T(8,128)} fusion(bf16[4096,512]{1,0:T(8,128)(2,1)} %param.10, bf16[512,256]{1,0:T(8,128)(2,1)S(1)} %copy-done), kind=kOutput, calls=%fused_computation.46 | convolution fusion | flops 1073741824 | bytes 8650752 | tf_op jit(solution)/shard_map/dot_general | solution.py:44
  13.6 0.6 copy-done.7
  14.3 0.6 reduce-window.6
  15.2 1.4 scatter_custom_fusion.1
  16.6 1.5 scatter_custom_fusion
  18.1 77.9 %reduce-scatter.3.cloned.1.call-done = f32[256,256]{1,0:T(8,128)} async-done(((f32[4096,256]{1,0:T(8,128)}), f32[256,256]{1,0:T(8,128)}) %reduce-scatter.3.cloned.1.call-update) | async-done | bytes 262160 | tf_op jit(solution)/shard_map/reduce_scatter | solution.py:43
  96.0 1.0 fusion.12
  97.4 3.9 gather_fusion
  101.3 6.6 %select_bitcast_fusion = bf16[3,256,1024]{1,0,2:T(4,128)(2,1)} fusion(bf16[1024,3,256]{2,1,0:T(4,128)(2,1)S(1)} %gather_fusion, pred[1024]{0:T(1024)(128)(4,1)S(1)} %scatter_custom_fusion, pred[1024]{0:T(1024)(128)(4,1)S(1)} %compare_and_fusion), kind=kLoop, calls=%fused_computation.9 | loop fusion | flops 1572864 | bytes 3147776 | tf_op jit(solution)/shard_map/jit(_where)/select_n | solution.py:40
  107.9 4.1 all-to-all-start
  112.1 8.6 %copy.31 = bf16[1,4096,3,256]{1,3,2,0:T(8,128)(2,1)} copy(bf16[1,4096,3,256]{3,1,2,0:T(8,128)(2,1)} %param.15) | data formatting | bytes 12582912 | tf_op args[6]
  120.7 20.1 %all-to-all-done = bf16[3,256,1024]{1,0,2:T(4,128)(2,1)S(1)} async-done(((bf16[3,256,1024]{1,0,2:T(4,128)(2,1)}), bf16[3,256,1024]{1,0,2:T(4,128)(2,1)S(1)}, u32[]{:S(2)}, u32[]{:S(2)}) %all-to-all-start) | async-done | bytes 1572896 | tf_op jit(solution)/shard_map/all_to_all | solution.py:51
  140.8 2.9 copy.30
  143.7 12.5 %convolution_bitcast_fusion = f32[4096,1024]{0,1:T(8,128)} fusion(bf16[768,1024]{1,0:T(8,128)(2,1)} %bitcast.55, bf16[4096,768]{0,1:T(8,128)(2,1)} %bitcast.52), kind=kOutput, calls=%fused_computation.5 | convolution fusion | flops 6442450944 | bytes 24641536 | tf_op jit(solution)/shard_map/dot_general | solution.py:64
  156.5 0.6 copy-done.3
  157.3 3.9 gather_fusion.2
  161.6 0.8 copy.44
  162.9 3.8 reduce.2
  166.9 9.8 %all_to_all.22 = bf16[8,2,16384]{2,1,0:T(2,128)(2,1)S(1)} all-to-all(bf16[8,2,16384]{2,1,0:T(2,128)(2,1)S(1)} %reshape.157), channel_id=1, replica_groups=mesh['dp'=8,'tensor'=16] {'dp'}, dimensions={0} | all-to-all | bytes 1048576 | tf_op jit(solution)/shard_map/all_to_all | solution.py:58
  177.2 124.4 %reduce-scatter.5.cloned.1.call-done = f32[256,1024]{0,1:T(8,128)} async-done(((f32[4096,1024]{0,1:T(8,128)}), f32[256,1024]{0,1:T(8,128)}) %reduce-scatter.5.cloned.1.call-update) | async-done | bytes 1048592 | tf_op jit(solution)/shard_map/reduce_scatter | solution.py:63
  301.6 1.4 multiply_reduce_fusion
  303.0 33.7 %psum.14 = f32[1024]{0:T(1024)S(1)} all-reduce(f32[1024]{0:T(1024)S(1)} %multiply_reduce_fusion), channel_id=1, replica_groups=mesh['dp'=8,'tensor'=16] {'tensor'}, use_global_device_ids=true, to_apply=%region_8.9 | all-reduce | flops 1024 | bytes 8192 | tf_op jit(solution)/shard_map/psum | solution.py:72
  336.8 2.3 fusion.10
  339.1 33.1 %psum.15 = f32[1024]{0:T(1024)S(1)} all-reduce(f32[1024]{0:T(1024)S(1)} %get-tuple-element.16), channel_id=1, replica_groups=mesh['dp'=8,'tensor'=16] {'tensor'}, use_global_device_ids=true, to_apply=%region_10.11 | all-reduce | flops 1024 | bytes 8192 | tf_op jit(solution)/shard_map/psum | solution.py:75
  372.2 2.6 fusion.9
  374.8 4.6 all-to-all-start.1
  379.4 9.0 %all-to-all-done.1 = bf16[256,8,128]{0,2,1:T(8,128)(2,1)S(1)} async-done(((bf16[256,8,128]{0,2,1:T(8,128)(2,1)}), bf16[256,8,128]{0,2,1:T(8,128)(2,1)S(1)}, u32[]{:S(2)}, u32[]{:S(2)}) %all-to-all-start.1) | async-done | bytes 524320 | tf_op jit(solution)/shard_map/all_to_all | solution.py:85
  388.4 1.2 gather_fusion.1
  389.6 0.8 copy.37
  390.4 62.0 %all-gather.2.cloned.1.call-done = bf16[4096,1024]{0,1:T(8,128)(2,1)} async-done(((bf16[256,1024]{0,1:T(8,128)(2,1)}), bf16[4096,1024]{0,1:T(8,128)(2,1)}) %all-gather.2.cloned.1.call-update) | async-done | bytes 8388624 | tf_op jit(solution)/shard_map/all_gather | solution.py:80
  452.4 12.8 %fusion.2 = f32[1,4096,3,256]{3,1,2,0:T(8,128)} fusion(bf16[3,256,1024]{2,1,0:T(8,128)(2,1)S(1)} %copy-done.2, bf16[4096,1024]{0,1:T(8,128)(2,1)} %all-gather.2.cloned.1.call-done), kind=kOutput, calls=%fused_computation.8 | convolution fusion | flops 6442450944 | bytes 22544384 | tf_op jit(solution)/shard_map/dot_general | solution.py:79
  (41 shorter events, 2.8 us)
Async XLA Ops:
  7.2 1.0 copy-start
  7.2 88.8 %reduce-scatter.3.cloned.1.call-start = ((), (), s32[]{:S(2)}) async-start(), calls=%async_computation.5 | async-start | bytes 4456448 | tf_op jit(solution)/shard_map/reduce_scatter | solution.py:43
  13.6 0.7 copy-start.7
  13.6 82.4 %copy-start.4 = (bf16[256,256]{1,0:T(8,128)(2,1)S(1)}, bf16[256,256]{1,0:T(8,128)(2,1)}, u32[]{:S(2)}) copy-start(bf16[256,256]{1,0:T(8,128)(2,1)} %param.11) | copy-start | bytes 393220
  13.6 83.4 %copy-start.5 = (bf16[256,256]{1,0:T(8,128)(2,1)S(1)}, bf16[256,256]{1,0:T(8,128)(2,1)}, u32[]{:S(2)}) copy-start(bf16[256,256]{1,0:T(8,128)(2,1)} %param.13) | copy-start | bytes 393220
  13.6 83.4 %copy-start.6 = (bf16[256,256]{1,0:T(8,128)(2,1)S(1)}, bf16[256,256]{1,0:T(8,128)(2,1)}, u32[]{:S(2)}) copy-start(bf16[256,256]{1,0:T(8,128)(2,1)} %param.12) | copy-start | bytes 393220
  107.9 32.9 %all-to-all-start = ((bf16[3,256,1024]{1,0,2:T(4,128)(2,1)}), bf16[3,256,1024]{1,0,2:T(4,128)(2,1)S(1)}, u32[]{:S(2)}, u32[]{:S(2)}) async-start(bf16[3,256,1024]{1,0,2:T(4,128)(2,1)} %select_bitcast_fusion), calls=%async_computation.1 | async-start | bytes 4194304 | tf_op jit(solution)/shard_map/all_to_all | solution.py:51
  112.0 189.5 %reduce-scatter.5.cloned.1.call-start = ((), (), s32[]{:S(2)}) async-start(), calls=%async_computation.6 | async-start | bytes 17825792 | tf_op jit(solution)/shard_map/reduce_scatter | solution.py:63
  156.2 0.9 copy-start.3
  156.3 296.1 %all-gather.2.cloned.1.call-start = ((), (), s32[]{:S(2)}) async-start(), calls=%async_computation.7 | async-start | bytes 8912896 | tf_op jit(solution)/shard_map/all_gather | solution.py:80
  161.6 175.2 %copy-start.8 = (f32[1,256]{1,0:T(1,128)S(1)}, f32[1,256]{1,0:T(1,128)}, u32[]{:S(2)}) copy-start(f32[1,256]{1,0:T(1,128)} %param.16) | copy-start | bytes 3076
  336.7 115.7 %copy-start.2 = (bf16[3,256,1024]{2,1,0:T(8,128)(2,1)S(1)}, bf16[3,256,1024]{2,1,0:T(8,128)(2,1)}, u32[]{:S(2)}) copy-start(bf16[3,256,1024]{2,1,0:T(8,128)(2,1)} %copy.30) | copy-start | bytes 4718596
  374.8 13.6 %all-to-all-start.1 = ((bf16[256,8,128]{0,2,1:T(8,128)(2,1)}), bf16[256,8,128]{0,2,1:T(8,128)(2,1)S(1)}, u32[]{:S(2)}, u32[]{:S(2)}) async-start(bf16[256,8,128]{0,2,1:T(8,128)(2,1)} %bitcast.11), calls=%async_computation.3 | async-start | bytes 1048576 | tf_op jit(solution)/shard_map/all_to_all | solution.py:85
  452.4 12.8 %copy-start.1 = (bf16[512,256]{1,0:T(8,128)(2,1)S(1)}, bf16[512,256]{1,0:T(8,128)(2,1)}, u32[]{:S(2)}) copy-start(bf16[512,256]{1,0:T(8,128)(2,1)} %param.9) | copy-start | bytes 786436
Sparse Core Ops, SparseCore 0:
  13.7 82.2 reduce-scatter.2
  156.4 145.1 reduce-scatter.4
  374.9 77.4 all-gather.1
where the time goes:
time: 473 us; the launch traced here: 472 us
  waiting for transfers between devices  293 us (62%)
  blocking collectives  76.6 us (16%)
  matrix products  30.8 us (7%)
  local copies, waits for them, and re-layouts  29 us (6%)
  other arithmetic  19 us (4%)
  between operations  14 us (3%)
  starting transfers between devices  9.01 us (2%)
    reduce_scatter x1, waiting for transfers between devices, local(): lax.psum_scatter(jnp.dot(block, rows_flat, preferred_element_type=jnp.flo...  124 us
    reduce_scatter x1, waiting for transfers between devices, local(): lax.psum_scatter(jnp.dot(block, attn_out, preferred_element_type=jnp.floa...  77.9 us
    all_gather x1, waiting for transfers between devices, local(): lax.all_gather(pre_grad, 'tensor', axis=0, tiled=True)  62 us
    psum x1, blocking collectives, local(): square_total = lax.psum(jnp.sum(draft_pre * draft_pre, axis=0), 'tensor')  33.7 us
    psum x1, blocking collectives, local(): slope = lax.psum(jnp.sum(upstream * normed, axis=0), 'tensor')  33.1 us
    all_to_all x1, waiting for transfers between devices, local(): lax.all_to_all(packed(jnp.stack([low_hidden, mid_hidden, high_hidden])),...  20.1 us
    unnamed x24, local copies, waits for them, and re-layouts  12.9 us
    dot_general x1, matrix products, local(): lax.dot_general(lax.all_gather(pre_grad, 'tensor', axis=0, tiled=True), r...  12.8 us
  transfers between devices with their start and end apart: 5, of which 5 were waited for; matrix products, arithmetic and copies ran while one was open for 5% of the time, Pallas kernels for 0%

commit v1 on v0

v1 whole, which is shorter than its diff:
```python
import functools

import jax
import jax.numpy as jnp
from jax import lax
from jax.experimental import pallas as pl
from jax.experimental.pallas import tpu as pltpu
from jax.sharding import PartitionSpec as P

NX, NZ, NC = 4, 2, 2
NT = NX * NZ * NC
DOUT = 4096
HALF = DOUT // 2
EPS = 1e-05
F32, BF16 = jnp.float32, jnp.bfloat16
VMEM = 48 * 1024 * 1024


def shift(dx, dz, dc):
    pairs = []
    for x in range(NX):
        for z in range(NZ):
            for c in range(NC):
                pairs.append((x * 4 + z * 2 + c, (x + dx) % NX * 4 + (z ^ dz) * 2 + (c ^ dc)))
    return pairs


def send(v, dx=0, dz=0, dc=0):
    return lax.ppermute(v, "tensor", shift(dx, dz, dc))


def params():
    return pltpu.CompilerParams(vmem_limit_bytes=VMEM)


def nt(a, b):
    return lax.dot_general(a, b, (((1,), (1,)), ((), ())), preferred_element_type=F32)


def tn(a, b):
    return lax.dot_general(a, b, (((0,), (0,)), ((), ())), preferred_element_type=F32)


def oproj_kernel(pos, o_ref, a_ref, own_ref, oth_ref):
    z, c = pos[1], pos[2]
    for dz in range(NZ):
        for dc, out in ((0, own_ref), (1, oth_ref)):
            block = (z ^ dz) * 2 + (c ^ dc)
            rows = o_ref[pl.ds(pl.multiple_of(block * 256, 256), 256), :]
            out[0, dz] = jnp.dot(rows, a_ref[...], preferred_element_type=F32).astype(out.dtype)


def oproj_partial(pos, o_proj, attn):
    k, n = attn.shape
    part = lambda i, p: (i, 0, 0, 0)
    return pl.pallas_call(
        oproj_kernel,
        grid_spec=pltpu.PrefetchScalarGridSpec(
            num_scalar_prefetch=1,
            grid=(NX,),
            in_specs=[
                pl.BlockSpec((1024, k), lambda i, p: ((p[0] + i) % NX, 0)),
                pl.BlockSpec((k, n), lambda i, p: (0, 0)),
            ],
            out_specs=[pl.BlockSpec((1, NZ, 256, n), part)] * 2,
        ),
        out_shape=[jax.ShapeDtypeStruct((NX, NZ, 256, n), F32)] * 2,
        compiler_params=params(),
        name="oproj_partial",
    )(pos, o_proj, attn)


def reorder_kernel(pos, v_ref, own_ref, oth_ref):
    x, z, c = pos[0], pos[1], pos[2]
    for dx in range(NX):
        for dz in range(NZ):
            for dc, out in ((0, own_ref), (1, oth_ref)):
                t = ((x + dx) % NX) * 4 + (z ^ dz) * 2 + (c ^ dc)
                out[(dx * NZ + dz) * 64 : (dx * NZ + dz + 1) * 64, :] = v_ref[t]


def reorder(pos, v):
    f = v.shape[-1]
    whole = pl.BlockSpec(memory_space=pltpu.VMEM)
    return pl.pallas_call(
        reorder_kernel,
        in_specs=[pl.BlockSpec(memory_space=pltpu.SMEM), whole],
        out_specs=[whole] * 2,
        out_shape=[jax.ShapeDtypeStruct((512, f), v.dtype)] * 2,
        compiler_params=params(),
        name="reorder",
    )(pos, v.reshape(NT, 64, f))


def join_kernel(which, xo_ref, xp_ref, ho_ref, hp_ref, w_ref, v_ref, *outs):
    acc = nt(ho_ref[...], w_ref[2]) + nt(hp_ref[...], v_ref[2])
    for s in range(2):
        cols = slice(s * 256, (s + 1) * 256)
        acc += nt(xo_ref[:, cols], w_ref[s]) + nt(xp_ref[:, cols], v_ref[s])
    if which == 0:
        for dx in range(NX):
            outs[dx][...] = acc[dx * 128 : (dx + 1) * 128].astype(outs[dx].dtype)
    else:
        for dx in range(NX):
            for dz in range(NZ):
                at = dx * 128 + dz * 64
                outs[dz][dx * 64 : (dx + 1) * 64, :] = acc[at : at + 64].astype(outs[dz].dtype)


def join(which, xo, xp, ho, hp, w, v):
    tile = 512
    steps = HALF // tile
    base = which * steps
    whole = lambda a: pl.BlockSpec(a.shape, lambda j: (0, 0))
    wspec = pl.BlockSpec((3, tile, 256), lambda j: (0, base + j, 0))
    if which == 0:
        shapes = [(128, F32)] + [(128, BF16)] * 3
    else:
        shapes = [(256, F32), (256, BF16)]
    return pl.pallas_call(
        functools.partial(join_kernel, which),
        grid=(steps,),
        in_specs=[whole(xo), whole(xp), whole(ho), whole(hp), wspec, wspec],
        out_specs=[pl.BlockSpec((n, tile), lambda j: (0, j)) for n, _ in shapes],
        out_shape=[jax.ShapeDtypeStruct((n, HALF), t) for n, t in shapes],
        compiler_params=params(),
        name="join",
    )(xo, xp, ho, hp, w, v)


def norm_kernel(
    ka, ra, kb, rb1, rb2, rb3, cot_ref, gain_ref, out_ref, pga_ref, pgb_ref, pre
):
    per = HALF // 256
    square = jnp.zeros((64, 1), F32)
    inner = jnp.zeros((64, 1), F32)
    for t in range(NT):
        cols = slice(t % per * 256, (t % per + 1) * 256)
        if t < per:
            d = ka[:, cols] + ra[:, cols].astype(F32)
        else:
            d = kb[:, cols] + rb1[:, cols].astype(F32)
            d += rb2[:, cols].astype(F32) + rb3[:, cols].astype(F32)
        pre[t] = d
        up = gain_ref[t : t + 1, :] * cot_ref[t].astype(F32)
        square += jnp.sum(d * d, axis=1, keepdims=True)
        inner += jnp.sum(up * d, axis=1, keepdims=True)
    inv = 1.0 / jnp.sqrt(square / DOUT + EPS)
    slope = inner * inv
    for t in range(NT):
        cols = slice(t % per * 256, (t % per + 1) * 256)
        raw = cot_ref[t].astype(F32)
        gain = gain_ref[t : t + 1, :]
        normed = pre[t] * inv
        grad = ((gain * raw - normed * (slope / DOUT)) * inv).astype(BF16)
        if t < per:
            pga_ref[:, cols] = grad
        else:
            pgb_ref[:, cols] = grad
        total = jnp.sum(raw * normed, axis=0, keepdims=True)
        hi = total.astype(BF16)
        lo = (total - hi.astype(F32)).astype(BF16)
        row = lax.broadcasted_iota(jnp.int32, (16, 256), 0)
        extra = jnp.where(row == 0, hi.astype(F32), jnp.where(row == 1, lo.astype(F32), 0.0))
        out_ref[t, :64, :] = (gain * normed).astype(BF16)
        out_ref[t, 64:, :] = extra.astype(BF16)


def norm(ka, ra, kb, rb, cot, gain):
    whole = pl.BlockSpec(memory_space=pltpu.VMEM)
    return pl.pallas_call(
        norm_kernel,
        in_specs=[whole] * 8,
        out_specs=[whole] * 3,
        out_shape=[
            jax.ShapeDtypeStruct((NT, 80, 256), BF16),
            jax.ShapeDtypeStruct((64, HALF), BF16),
            jax.ShapeDtypeStruct((64, HALF), BF16),
        ],
        scratch_shapes=[pltpu.VMEM((NT, 64, 256), F32)],
        compiler_params=params(),
        name="norm",
    )(ka, ra, kb, *rb, cot, gain)


def grad_kernel(go_ref, gp_ref, xo_ref, xp_ref, ho_ref, hp_ref, *rest):
    out = rest[-1]
    go, gp = go_ref[...], gp_ref[...]
    for s in range(3):
        if s < 2:
            cols = slice(s * 256, (s + 1) * 256)
            a, b = xo_ref[:, cols], xp_ref[:, cols]
        else:
            a, b = ho_ref[...], hp_ref[...]
        out[s] = tn(go, a) + tn(gp, b)


def grad(which, go, gp, xo, xp, ho, hp, into=None):
    tile = 512
    steps = HALF // tile
    base = which * steps
    whole = lambda a: pl.BlockSpec(a.shape, lambda j: (0, 0))
    gspec = pl.BlockSpec((512, tile), lambda j: (0, j))
    specs = [gspec, gspec, whole(xo), whole(xp), whole(ho), whole(hp)]
    args = [go, gp, xo, xp, ho, hp]
    if into is not None:
        specs.append(pl.BlockSpec(memory_space=pl.ANY))
        args.append(into)
    return pl.pallas_call(
        grad_kernel,
        grid=(steps,),
        in_specs=specs,
        out_specs=pl.BlockSpec((3, tile, 256), lambda j: (0, base + j, 0)),
        out_shape=jax.ShapeDtypeStruct((3, DOUT, 256), F32),
        input_output_aliases={} if into is None else {6: 0},
        compiler_params=params(),
        name="grad",
    )(*args)


def local(
    attn_out,
    o_proj,
    high_resid,
    low_hidden,
    mid_hidden,
    route_list,
    fc_weight,
    norm_gain,
    cotangent,
):
    trainers = lax.axis_size("dp")
    toks = route_list.shape[0]
    cap = toks // 2
    slots = trainers * cap
    t = lax.axis_index("tensor")
    pos = jnp.stack([t // 4, t // 2 % 2, t % 2]).astype(jnp.int32)

    w = jnp.transpose(fc_weight[0], (1, 0, 2))
    w_other = send(w, dc=1)

    here = jnp.arange(toks, dtype=jnp.int32)
    same = (route_list[:, None] == route_list[None, :]) & (here[None, :] < here[:, None])
    slot = route_list * cap + jnp.sum(same.astype(jnp.int32), axis=1)
    pick = (slot[:, None] == jnp.arange(slots, dtype=jnp.int32)[None, :]).astype(BF16)

    def packed(v):
        rows = lax.dot_general(pick, v, (((0,), (1,)), ((), ())), preferred_element_type=BF16)
        return lax.all_to_all(rows.reshape(trainers, cap, -1), "dp", 0, 0)

    own, oth = oproj_partial(pos, o_proj, attn_out)
    own = own + send(oth, dc=1)
    narrow = own.astype(BF16)
    high = own[0, 0]
    for dx in range(NX):
        for dz in range(NZ):
            if dx or dz:
                high = high + send(narrow[dx, dz], dx, dz).astype(F32)
    high_hidden = (high_resid.astype(F32) + high).astype(BF16)

    early = packed(jnp.concatenate([low_hidden, mid_hidden, cotangent], axis=0))
    early = early.reshape(slots, -1)
    xo, xs = reorder(pos, early[:, :512])
    xp = send(xs, dc=1)
    cot = lax.all_to_all(early[:, 512:].reshape(NT, 64, 256), "tensor", 0, 0)
    gain = lax.all_gather(norm_gain[0], "tensor", axis=0)

    ho, hs = reorder(pos, packed(high_hidden).reshape(slots, -1))
    hp = send(hs, dc=1)

    a = join(0, xo, xp, ho, hp, w, w_other)
    ax = a[0]
    for dx in range(1, NX):
        ax = ax + send(a[dx], dx).astype(F32)
    b = join(1, xo, xp, ho, hp, w, w_other)
    bz = b[0] + send(b[1], dz=1).astype(F32)
    az = send(ax[64:].astype(BF16), dz=1)
    bx = [send(bz[dx * 64 : (dx + 1) * 64].astype(BF16), dx) for dx in range(1, NX)]

    outputs, ga, gb = norm(ax[:64], az, bz[:64], bx, cot, gain)

    def spread_z_first(v):
        far = send(v, dz=1)
        pieces = [v, far]
        for dx in range(1, NX):
            pieces += [send(v, -dx), send(far, -dx)]
        return jnp.concatenate(pieces, axis=0)

    def spread_x_first(v):
        pieces = []
        for dx in range(NX):
            near = send(v, -dx) if dx else v
            pieces += [near, send(near, dz=1)]
        return jnp.concatenate(pieces, axis=0)

    ga = spread_z_first(ga)
    gap = send(ga, dc=1)
    gb = spread_x_first(gb)
    gbp = send(gb, dc=1)
    fc = grad(0, ga, gap, xo, xs, ho, hs)
    fc = grad(1, gb, gbp, xo, xs, ho, hs, fc)
    fc_grad = jnp.transpose(fc, (1, 0, 2))[None]

    returned = lax.all_to_all(outputs, "tensor", 0, 0)
    gain_grad = jnp.sum(returned[:, 64:66].astype(F32), axis=(0, 1))[None, :]
    back = lax.all_to_all(returned[:, :64].reshape(trainers, cap, 256), "dp", 0, 0)
    draft_hidden = lax.dot_general(
        back.reshape(slots, 256), pick, (((0,), (1,)), ((), ())), preferred_element_type=BF16
    )
    return (draft_hidden, fc_grad, gain_grad)


def solution(mesh):
    return jax.shard_map(
        local,
        mesh=mesh,
        in_specs=(
            P("tensor", "dp"),
            P(None, "tensor"),
            P("tensor", "dp"),
            P("tensor", "dp"),
            P("tensor", "dp"),
            P("dp"),
            P("dp", None, None, "tensor"),
            P("dp", "tensor"),
            P("tensor", "dp"),
        ),
        out_specs=(P("tensor", "dp"), P("dp", None, None, "tensor"), P("dp", "tensor")),
        check_vma=False,
    )
```

time: 473 us -> 269 us (0.57)
  waiting for transfers between devices: 293 us -> 79.6 us
  starting transfers between devices: 9.01 us -> 74.3 us
  Pallas kernels: 0 us -> 36.5 us
  blocking collectives: 76.6 us -> 48.4 us
  matrix products: 30.8 us -> 5.34 us
  between operations: 14 us -> 0.89 us
  local copies, waits for them, and re-layouts: 29 us -> 15.9 us
  other arithmetic: 19 us -> 7.17 us
    reduce_scatter x2 -> x0, waiting for transfers between devices: 202 us -> none  [the longest x1 124 us: local(): lax.psum_scatter(jnp.dot(block, rows_flat, preferred_element_type=jnp.flo...]
    ppermute x0 -> x35, waiting for transfers between devices: none -> 67.3 us  [send(): return lax.ppermute(v, 'tensor', shift(dx, dz, dc))]
    psum x2 -> x0, blocking collectives: 66.8 us -> none  [the longest x1 33.7 us: local(): square_total = lax.psum(jnp.sum(draft_pre * draft_pre, axis=0), 'tensor')]
    all_gather x1 -> x0, waiting for transfers between devices: 62 us -> none  [local(): lax.all_gather(pre_grad, 'tensor', axis=0, tiled=True)]
    ppermute x0 -> x35, starting transfers between devices: none -> 53.4 us  [send(): return lax.ppermute(v, 'tensor', shift(dx, dz, dc))]
    pallas_call x0 -> x8, Pallas kernels: none -> 36.5 us  [the longest x2 14.3 us: grad(): pl.pallas_call(grad_kernel, grid=(steps,), in_specs=specs, out_specs=pl.B...]
    dot_general x3 -> x1, matrix products: 30.8 us -> 2.16 us  [local(): lax.dot_general(back.reshape(slots, 256), pick, (((0,), (1,)), ((), ())),...]
    all_gather x0 -> x1, blocking collectives: none -> 27.5 us  [local(): gain = lax.all_gather(norm_gain[0], 'tensor', axis=0)]
  transfers between devices with their start and end apart: 5 -> 39, of which waited for: 5 -> 18; matrix products, arithmetic and copies ran while one was open for 5% -> 9% of each run, Pallas kernels for 0% -> 8%
where the time goes in v1:
time: 269 us; the launch traced here: 268 us
  waiting for transfers between devices  79.6 us (30%)
  starting transfers between devices  74.3 us (28%)
  blocking collectives  48.4 us (18%)
  Pallas kernels  36.5 us (14%)
  local copies, waits for them, and re-layouts  15.9 us (6%)
  other arithmetic  7.17 us (3%)
  matrix products  5.34 us (2%)
    ppermute x35, waiting for transfers between devices, send(): return lax.ppermute(v, 'tensor', shift(dx, dz, dc))  67.3 us
    ppermute x35, starting transfers between devices, send(): return lax.ppermute(v, 'tensor', shift(dx, dz, dc))  53.4 us
    all_gather x1, blocking collectives, local(): gain = lax.all_gather(norm_gain[0], 'tensor', axis=0)  27.5 us
    all_to_all x1, blocking collectives, local(): returned = lax.all_to_all(outputs, 'tensor', 0, 0)  20.9 us
    pallas_call x2, Pallas kernels, grad(): pl.pallas_call(grad_kernel, grid=(steps,), in_specs=specs, out_specs=pl.B...  14.3 us
    pallas_call x2, Pallas kernels, join(): pl.pallas_call(functools.partial(join_kernel, which), grid=(steps,), in_s...  13.6 us
    all_to_all x2, starting transfers between devices, packed(): return lax.all_to_all(rows.reshape(trainers, cap, -1), 'dp', 0, 0)  11.2 us
    unnamed x38, local copies, waits for them, and re-layouts  9.31 us
  transfers between devices with their start and end apart: 39, of which 18 were waited for; matrix products, arithmetic and copies ran while one was open for 9% of the time, Pallas kernels for 8%

profile of v1, /device:TPU:1, one launch (start us, length us, event | category | flops | bytes accessed | tf_op | source)
XLA Modules:
  0.0 268.0 jit_solution(10548007570139722904)
XLA Ops:
  3.2 5.5 %oproj_partial.1 = (f32[4,2,256,256]{3,2,1,0:T(8,128)S(1)}, f32[4,2,256,256]{3,2,1,0:T(8,128)}) custom-call(s32[3]{0:T(128)S(1)} %pad_add_fusion.pos, bf16[4096,512]{1,0:T(8,128)(2,1)} %o_ref.1, bf16[512,256]{1,0:T(8,128)(2,1)S(1)} %copy-done.4), custom_call_target="tpu_custom_call" | custom-call | tf_op jit(solution)/shard_map/oproj_partial/pallas_call | solution.py:56
  10.9 5.6 %all-to-all-start = ((bf16[8,128,768]{2,1,0:T(8,128)(2,1)}), bf16[8,128,768]{2,1,0:T(8,128)(2,1)}, u32[]{:S(2)}, u32[]{:S(2)}) async-start(bf16[8,128,768]{2,1,0:T(8,128)(2,1)} %bitcast.66), calls=%async_computation | async-start | bytes 3145728 | tf_op jit(solution)/shard_map/all_to_all | solution.py:249
  18.6 3.4 %collective-permute-start.2 = (bf16[256,256]{1,0:T(8,128)(2,1)S(1)}, bf16[256,256]{1,0:T(8,128)(2,1)S(1)}, u32[]{:S(2)}, u32[]{:S(2)}) collective-permute-start(bf16[256,256]{1,0:T(8,128)(2,1)S(1)} %get-tuple-element.40), channel_id=1, source_target_pairs={{0,2},{1,3},{2,0},{3,1},{4,6},{5,7},{6,4},{7,5},{8,10},{9,11},{10,... | collective-permute-start | bytes 393224 | tf_op jit(solution)/shard_map/ppermute | solution.py:29
  24.8 2.8 %collective-permute-start.6 = (bf16[256,256]{1,0:T(8,128)(2,1)S(1)}, bf16[256,256]{1,0:T(8,128)(2,1)S(1)}, u32[]{:S(2)}, u32[]{:S(2)}) collective-permute-start(bf16[256,256]{1,0:T(8,128)(2,1)S(1)} %get-tuple-element.43), channel_id=1, source_target_pairs={{0,10},{1,11},{2,8},{3,9},{4,14},{5,15},{6,12},{7,13},{8,2},{9,3},... | collective-permute-start | bytes 393224 | tf_op jit(solution)/shard_map/ppermute | solution.py:29
  27.6 18.0 %collective-permute-done.2 = bf16[256,256]{1,0:T(8,128)(2,1)S(1)} collective-permute-done((bf16[256,256]{1,0:T(8,128)(2,1)S(1)}, bf16[256,256]{1,0:T(8,128)(2,1)S(1)}, u32[]{:S(2)}, u32[]{:S(2)}) %collective-permute-start.2) | collective-permute-done | bytes 131104 | tf_op jit(solution)/shard_map/ppermute | solution.py:29
  45.6 2.7 %collective-permute-start.5 = (bf16[256,256]{1,0:T(8,128)(2,1)S(1)}, bf16[256,256]{1,0:T(8,128)(2,1)S(1)}, u32[]{:S(2)}, u32[]{:S(2)}) collective-permute-start(bf16[256,256]{1,0:T(8,128)(2,1)S(1)} %get-tuple-element.44), channel_id=1, source_target_pairs={{0,8},{1,9},{2,10},{3,11},{4,12},{5,13},{6,14},{7,15},{8,0},{9,1},... | collective-permute-start | bytes 393224 | tf_op jit(solution)/shard_map/ppermute | solution.py:29
  51.0 4.8 %collective-permute-done.4 = bf16[256,256]{1,0:T(8,128)(2,1)S(1)} collective-permute-done((bf16[256,256]{1,0:T(8,128)(2,1)S(1)}, bf16[256,256]{1,0:T(8,128)(2,1)S(1)}, u32[]{:S(2)}, u32[]{:S(2)}) %collective-permute-start.4) | collective-permute-done | bytes 131104 | tf_op jit(solution)/shard_map/ppermute | solution.py:29
  58.9 5.6 %all-to-all-start.1 = ((bf16[8,128,256]{2,1,0:T(8,128)(2,1)}), bf16[8,128,256]{2,1,0:T(8,128)(2,1)S(1)}, u32[]{:S(2)}, u32[]{:S(2)}) async-start(bf16[8,128,256]{2,1,0:T(8,128)(2,1)} %bitcast.14), calls=%async_computation.1 | async-start | bytes 1048576 | tf_op jit(solution)/shard_map/all_to_all | solution.py:249
  68.1 4.4 %all-to-all-done.1 = bf16[8,128,256]{2,1,0:T(8,128)(2,1)S(1)} async-done(((bf16[8,128,256]{2,1,0:T(8,128)(2,1)}), bf16[8,128,256]{2,1,0:T(8,128)(2,1)S(1)}, u32[]{:S(2)}, u32[]{:S(2)}) %all-to-all-start.1) | async-done | bytes 524320 | tf_op jit(solution)/shard_map/all_to_all | solution.py:249
  73.1 2.6 collective-permute-start.9
  76.8 6.8 %join.2 = (f32[128,2048]{1,0:T(8,128)S(1)}, bf16[128,2048]{1,0:T(8,128)(2,1)}, bf16[128,2048]{1,0:T(8,128)(2,1)}, bf16[128,2048]{1,0:T(8,128)(2,1)S(1)}) custom-call(bf16[512,512]{1,0:T(8,128)(2,1)S(1)} %get-tuple-element.18.xo_ref, bf16[512,512]{1,0:T(8,128)(2,1)S(1)} %collective-permute-done.xp_ref, bf16[512,256]{1,0:T(8,128)(2,1)S(1)} %get-tuple-element.22.ho_ref, ...), custom_call_target="tpu_custom_call" | custom-call | tf_op jit(solution)/shard_map/join/pallas_call | solution.py:120
  86.9 6.8 %join.3 = (f32[256,2048]{1,0:T(8,128)S(1)}, bf16[256,2048]{1,0:T(8,128)(2,1)}) custom-call(bf16[512,512]{1,0:T(8,128)(2,1)S(1)} %get-tuple-element.18.xo_ref, bf16[512,512]{1,0:T(8,128)(2,1)S(1)} %collective-permute-done.xp_ref, bf16[512,256]{1,0:T(8,128)(2,1)S(1)} %get-tuple-element.22.ho_ref, bf16[512,256]{1,0:T(8,128)(2,1)S(1)} %collective-permute-done.9.hp_ref, ...), custom_call_target="tpu_custom_call" | custom-call | tf_op jit(solution)/shard_map/join/pallas_call | solution.py:120
  95.1 2.6 collective-permute-start.15
  99.6 5.5 %all-to-all-start.2 = ((bf16[16,64,256]{2,1,0:T(8,128)(2,1)}), bf16[16,64,256]{2,1,0:T(8,128)(2,1)}, u32[]{:S(2)}, u32[]{:S(2)}) async-start(bf16[16,64,256]{2,1,0:T(8,128)(2,1)} %bitcast.19), calls=%async_computation.2 | async-start | bytes 1048576 | tf_op jit(solution)/shard_map/all_to_all | solution.py:265
  105.0 4.4 %collective-permute-done.11 = bf16[128,2048]{1,0:T(8,128)(2,1)} collective-permute-done((bf16[128,2048]{1,0:T(8,128)(2,1)}, bf16[128,2048]{1,0:T(8,128)(2,1)}, u32[]{:S(2)}, u32[]{:S(2)}) %collective-permute-start.11) | collective-permute-done | bytes 524320 | tf_op jit(solution)/shard_map/ppermute | solution.py:29
  114.9 9.7 %collective-permute-done.15 = bf16[256,2048]{1,0:T(8,128)(2,1)} collective-permute-done((bf16[256,2048]{1,0:T(8,128)(2,1)}, bf16[256,2048]{1,0:T(8,128)(2,1)}, u32[]{:S(2)}, u32[]{:S(2)}) %collective-permute-start.15) | collective-permute-done | bytes 1048608 | tf_op jit(solution)/shard_map/ppermute | solution.py:29
  129.7 27.5 %all-gather = f32[16,1,256]{2,1,0:T(1,128)S(1)} all-gather(f32[1,1,256]{2,1,0:T(1,128)S(1)} %bitcast.67), channel_id=1, replica_groups=mesh['dp'=8,'tensor'=16] {'tensor'}, dimensions={0}, use_global_device_ids=true | all-gather | bytes 17408 | tf_op jit(solution)/shard_map/all_gather | solution.py:266
  159.2 2.9 %collective-permute-start.19 = (bf16[64,2048]{1,0:T(8,128)(2,1)S(1)}, bf16[64,2048]{1,0:T(8,128)(2,1)S(1)}, u32[]{:S(2)}, u32[]{:S(2)}) collective-permute-start(bf16[64,2048]{1,0:T(8,128)(2,1)S(1)} %get-tuple-element.31), channel_id=1, source_target_pairs={{0,2},{1,3},{2,0},{3,1},{4,6},{5,7},{6,4},{7,5},{8,10},{9,11},{10,... | collective-permute-start | bytes 786440 | tf_op jit(solution)/shard_map/ppermute | solution.py:29
  165.7 2.8 %collective-permute-done.19 = bf16[64,2048]{1,0:T(8,128)(2,1)S(1)} collective-permute-done((bf16[64,2048]{1,0:T(8,128)(2,1)S(1)}, bf16[64,2048]{1,0:T(8,128)(2,1)S(1)}, u32[]{:S(2)}, u32[]{:S(2)}) %collective-permute-start.19) | collective-permute-done | bytes 262176 | tf_op jit(solution)/shard_map/ppermute | solution.py:29
  169.2 4.1 %collective-permute-done.27 = bf16[64,2048]{1,0:T(8,128)(2,1)S(1)} collective-permute-done((bf16[64,2048]{1,0:T(8,128)(2,1)S(1)}, bf16[64,2048]{1,0:T(8,128)(2,1)S(1)}, u32[]{:S(2)}, u32[]{:S(2)}) %collective-permute-start.27) | collective-permute-done | bytes 262176 | tf_op jit(solution)/shard_map/ppermute | solution.py:29
  173.6 3.0 %collective-permute-done.20 = bf16[64,2048]{1,0:T(8,128)(2,1)S(1)} collective-permute-done((bf16[64,2048]{1,0:T(8,128)(2,1)S(1)}, bf16[64,2048]{1,0:T(8,128)(2,1)S(1)}, u32[]{:S(2)}, u32[]{:S(2)}) %collective-permute-start.20) | collective-permute-done | bytes 262176 | tf_op jit(solution)/shard_map/ppermute | solution.py:29
  176.6 2.8 %collective-permute-start.29 = (bf16[64,2048]{1,0:T(8,128)(2,1)S(1)}, bf16[64,2048]{1,0:T(8,128)(2,1)S(1)}, u32[]{:S(2)}, u32[]{:S(2)}) collective-permute-start(bf16[64,2048]{1,0:T(8,128)(2,1)S(1)} %collective-permute-done.27), channel_id=1, source_target_pairs={{0,12},{1,13},{2,14},{3,15},{4,0},{5,1},{6,2},{7,3},{8,4},{9,5},{1... | collective-permute-start | bytes 786440 | tf_op jit(solution)/shard_map/ppermute | solution.py:29
  182.3 5.6 %collective-permute-done.29 = bf16[64,2048]{1,0:T(8,128)(2,1)S(1)} collective-permute-done((bf16[64,2048]{1,0:T(8,128)(2,1)S(1)}, bf16[64,2048]{1,0:T(8,128)(2,1)S(1)}, u32[]{:S(2)}, u32[]{:S(2)}) %collective-permute-start.29) | collective-permute-done | bytes 262176 | tf_op jit(solution)/shard_map/ppermute | solution.py:29
  190.5 3.9 %collective-permute-start.33 = (bf16[64,2048]{1,0:T(8,128)(2,1)S(1)}, bf16[64,2048]{1,0:T(8,128)(2,1)S(1)}, u32[]{:S(2)}, u32[]{:S(2)}) collective-permute-start(bf16[64,2048]{1,0:T(8,128)(2,1)S(1)} %collective-permute-done.27), channel_id=1, source_target_pairs={{0,4},{1,5},{2,6},{3,7},{4,8},{5,9},{6,10},{7,11},{8,12},{9,13},{1... | collective-permute-start | bytes 786440 | tf_op jit(solution)/shard_map/ppermute | solution.py:29
  197.4 4.1 %collective-permute-done.33 = bf16[64,2048]{1,0:T(8,128)(2,1)S(1)} collective-permute-done((bf16[64,2048]{1,0:T(8,128)(2,1)S(1)}, bf16[64,2048]{1,0:T(8,128)(2,1)S(1)}, u32[]{:S(2)}, u32[]{:S(2)}) %collective-permute-start.33) | collective-permute-done | bytes 262176 | tf_op jit(solution)/shard_map/ppermute | solution.py:29
  201.5 4.4 %collective-permute-start.34 = (bf16[512,2048]{1,0:T(8,128)(2,1)S(1)}, bf16[512,2048]{1,0:T(8,128)(2,1)}, u32[]{:S(2)}, u32[]{:S(2)}) collective-permute-start(bf16[512,2048]{1,0:T(8,128)(2,1)S(1)} %constant_dynamic-update-slice_fusion.8.go_ref), channel_id=1, source_target_pairs={{0,1},{1,0},{2,3},{3,2},{4,5},{5,4},{6,7},{7,6},{8,9},{9,8},{10,11... | collective-permute-start | bytes 6291464 | tf_op jit(solution)/shard_map/ppermute | solution.py:29
  211.7 2.9 %collective-permute-start.26 = (bf16[512,2048]{1,0:T(8,128)(2,1)}, bf16[512,2048]{1,0:T(8,128)(2,1)}, u32[]{:S(2)}, u32[]{:S(2)}) collective-permute-start(bf16[512,2048]{1,0:T(8,128)(2,1)} %constant_dynamic-update-slice_fusion.go_ref), channel_id=1, source_target_pairs={{0,1},{1,0},{2,3},{3,2},{4,5},{5,4},{6,7},{7,6},{8,9},{9,8},{10,11... | collective-permute-start | bytes 6291464 | tf_op jit(solution)/shard_map/ppermute | solution.py:29
  214.6 20.9 %all_to_all.25 = bf16[16,80,256]{2,1,0:T(8,128)(2,1)S(1)} all-to-all(bf16[16,80,256]{2,1,0:T(8,128)(2,1)S(1)} %get-tuple-element.30), channel_id=1, replica_groups=mesh['dp'=8,'tensor'=16] {'tensor'}, dimensions={0} | all-to-all | bytes 1310720 | tf_op jit(solution)/shard_map/all_to_all | solution.py:304
  237.2 4.1 %all-to-all-start.4 = ((bf16[8,128,256]{2,1,0:T(8,128)(2,1)}), bf16[8,128,256]{2,1,0:T(8,128)(2,1)}, u32[]{:S(2)}, u32[]{:S(2)}) async-start(bf16[8,128,256]{2,1,0:T(8,128)(2,1)} %bitcast.65), calls=%async_computation.4 | async-start | bytes 1048576 | tf_op jit(solution)/shard_map/all_to_all | solution.py:306
  242.8 7.8 %all-to-all-done.4 = bf16[8,128,256]{2,1,0:T(8,128)(2,1)} async-done(((bf16[8,128,256]{2,1,0:T(8,128)(2,1)}), bf16[8,128,256]{2,1,0:T(8,128)(2,1)}, u32[]{:S(2)}, u32[]{:S(2)}) %all-to-all-start.4) | async-done | bytes 524320 | tf_op jit(solution)/shard_map/all_to_all | solution.py:306
  253.8 6.9 %grad.2.rest_0_ = f32[3,4096,256]{2,1,0:T(8,128)} custom-call(bf16[512,2048]{1,0:T(8,128)(2,1)S(1)} %constant_dynamic-update-slice_fusion.8.go_ref, bf16[512,2048]{1,0:T(8,128)(2,1)} %collective-permute-done.34.gp_ref, bf16[512,512]{1,0:T(8,128)(2,1)S(1)} %get-tuple-element.18.xo_ref, bf16[512,512]{1,0:T(8,128)(2,1)S(1)} %get-tuple-element.19.xp_ref, ...), custom_call_target="tpu_custom_call" | custom-call | tf_op jit(solution)/shard_map/grad/pallas_call | solution.py:209
  260.7 7.3 %grad.3 = f32[3,4096,256]{2,1,0:T(8,128)} custom-call(bf16[512,2048]{1,0:T(8,128)(2,1)} %constant_dynamic-update-slice_fusion.go_ref, bf16[512,2048]{1,0:T(8,128)(2,1)} %collective-permute-done.26.gp_ref, bf16[512,512]{1,0:T(8,128)(2,1)S(1)} %get-tuple-element.18.xo_ref, ...), custom_call_target="tpu_custom_call", output_to_operand_aliasing={{}: (6, {})} | custom-call | tf_op jit(solution)/shard_map/grad/pallas_call | solution.py:209
  (114 shorter events, 64.7 us)
Async XLA Ops:
  0.6 76.2 %collective-permute-start.10 = (bf16[3,4096,256]{2,1,0:T(8,128)(2,1)}, bf16[3,4096,256]{2,1,0:T(8,128)(2,1)}, u32[]{:S(2)}, u32[]{:S(2)}) collective-permute-start(bf16[3,4096,256]{2,1,0:T(8,128)(2,1)} %bitcast.62), channel_id=1, source_target_pairs={{0,1},{1,0},{2,3},{3,2},{4,5},{5,4},{6,7},{7,6},{8,9},{9,8},{10,11... | collective-permute-start | bytes 18874376 | tf_op jit(solution)/shard_map/ppermute | solution.py:29
  10.9 48.0 %all-to-all-start = ((bf16[8,128,768]{2,1,0:T(8,128)(2,1)}), bf16[8,128,768]{2,1,0:T(8,128)(2,1)}, u32[]{:S(2)}, u32[]{:S(2)}) async-start(bf16[8,128,768]{2,1,0:T(8,128)(2,1)} %bitcast.66), calls=%async_computation | async-start | bytes 3145728 | tf_op jit(solution)/shard_map/all_to_all | solution.py:249
  18.6 27.0 %collective-permute-start.2 = (bf16[256,256]{1,0:T(8,128)(2,1)S(1)}, bf16[256,256]{1,0:T(8,128)(2,1)S(1)}, u32[]{:S(2)}, u32[]{:S(2)}) collective-permute-start(bf16[256,256]{1,0:T(8,128)(2,1)S(1)} %get-tuple-element.40), channel_id=1, source_target_pairs={{0,2},{1,3},{2,0},{3,1},{4,6},{5,7},{6,4},{7,5},{8,10},{9,11},{10,... | collective-permute-start | bytes 393224 | tf_op jit(solution)/shard_map/ppermute | solution.py:29
  22.0 26.4 %collective-permute-start.8 = (bf16[256,256]{1,0:T(8,128)(2,1)S(1)}, bf16[256,256]{1,0:T(8,128)(2,1)S(1)}, u32[]{:S(2)}, u32[]{:S(2)}) collective-permute-start(bf16[256,256]{1,0:T(8,128)(2,1)S(1)} %get-tuple-element.41), channel_id=1, source_target_pairs={{0,14},{1,15},{2,12},{3,13},{4,2},{5,3},{6,0},{7,1},{8,6},{9,7},{1... | collective-permute-start | bytes 393224 | tf_op jit(solution)/shard_map/ppermute | solution.py:29
  24.3 24.1 %collective-permute-start.7 = (bf16[256,256]{1,0:T(8,128)(2,1)S(1)}, bf16[256,256]{1,0:T(8,128)(2,1)S(1)}, u32[]{:S(2)}, u32[]{:S(2)}) collective-permute-start(bf16[256,256]{1,0:T(8,128)(2,1)S(1)} %get-tuple-element.42), channel_id=1, source_target_pairs={{0,12},{1,13},{2,14},{3,15},{4,0},{5,1},{6,2},{7,3},{8,4},{9,5},{1... | collective-permute-start | bytes 393224 | tf_op jit(solution)/shard_map/ppermute | solution.py:29
  24.8 24.0 %collective-permute-start.6 = (bf16[256,256]{1,0:T(8,128)(2,1)S(1)}, bf16[256,256]{1,0:T(8,128)(2,1)S(1)}, u32[]{:S(2)}, u32[]{:S(2)}) collective-permute-start(bf16[256,256]{1,0:T(8,128)(2,1)S(1)} %get-tuple-element.43), channel_id=1, source_target_pairs={{0,10},{1,11},{2,8},{3,9},{4,14},{5,15},{6,12},{7,13},{8,2},{9,3},... | collective-permute-start | bytes 393224 | tf_op jit(solution)/shard_map/ppermute | solution.py:29
  48.4 9.2 %collective-permute-start.3 = (bf16[256,256]{1,0:T(8,128)(2,1)S(1)}, bf16[256,256]{1,0:T(8,128)(2,1)S(1)}, u32[]{:S(2)}, u32[]{:S(2)}) collective-permute-start(bf16[256,256]{1,0:T(8,128)(2,1)S(1)} %get-tuple-element.46), channel_id=1, source_target_pairs={{0,4},{1,5},{2,6},{3,7},{4,8},{5,9},{6,10},{7,11},{8,12},{9,13},{1... | collective-permute-start | bytes 393224 | tf_op jit(solution)/shard_map/ppermute | solution.py:29
  58.9 13.6 %all-to-all-start.1 = ((bf16[8,128,256]{2,1,0:T(8,128)(2,1)}), bf16[8,128,256]{2,1,0:T(8,128)(2,1)S(1)}, u32[]{:S(2)}, u32[]{:S(2)}) async-start(bf16[8,128,256]{2,1,0:T(8,128)(2,1)} %bitcast.14), calls=%async_computation.1 | async-start | bytes 1048576 | tf_op jit(solution)/shard_map/all_to_all | solution.py:249
  66.5 9.2 %collective-permute-start = (bf16[512,512]{1,0:T(8,128)(2,1)S(1)}, bf16[512,512]{1,0:T(8,128)(2,1)S(1)}, u32[]{:S(2)}, u32[]{:S(2)}) collective-permute-start(bf16[512,512]{1,0:T(8,128)(2,1)S(1)} %get-tuple-element.19.xp_ref), channel_id=1, source_target_pairs={{0,1},{1,0},{2,3},{3,2},{4,5},{5,4},{6,7},{7,6},{8,9},{9,8},{10,11... | collective-permute-start | bytes 1572872 | tf_op jit(solution)/shard_map/ppermute | solution.py:29
  83.6 25.9 %collective-permute-start.11 = (bf16[128,2048]{1,0:T(8,128)(2,1)}, bf16[128,2048]{1,0:T(8,128)(2,1)}, u32[]{:S(2)}, u32[]{:S(2)}) collective-permute-start(bf16[128,2048]{1,0:T(8,128)(2,1)} %get-tuple-element.25), channel_id=1, source_target_pairs={{0,4},{1,5},{2,6},{3,7},{4,8},{5,9},{6,10},{7,11},{8,12},{9,13},{1... | collective-permute-start | bytes 1572872 | tf_op jit(solution)/shard_map/ppermute | solution.py:29
  84.3 25.2 %collective-permute-start.12 = (bf16[128,2048]{1,0:T(8,128)(2,1)}, bf16[128,2048]{1,0:T(8,128)(2,1)}, u32[]{:S(2)}, u32[]{:S(2)}) collective-permute-start(bf16[128,2048]{1,0:T(8,128)(2,1)} %get-tuple-element.26), channel_id=1, source_target_pairs={{0,8},{1,9},{2,10},{3,11},{4,12},{5,13},{6,14},{7,15},{8,0},{9,1},... | collective-permute-start | bytes 1572872 | tf_op jit(solution)/shard_map/ppermute | solution.py:29
  85.0 25.2 %collective-permute-start.13 = (bf16[128,2048]{1,0:T(8,128)(2,1)S(1)}, bf16[128,2048]{1,0:T(8,128)(2,1)}, u32[]{:S(2)}, u32[]{:S(2)}) collective-permute-start(bf16[128,2048]{1,0:T(8,128)(2,1)S(1)} %get-tuple-element.27), channel_id=1, source_target_pairs={{0,12},{1,13},{2,14},{3,15},{4,0},{5,1},{6,2},{7,3},{8,4},{9,5},{1... | collective-permute-start | bytes 1572872 | tf_op jit(solution)/shard_map/ppermute | solution.py:29
  95.1 29.5 %collective-permute-start.15 = (bf16[256,2048]{1,0:T(8,128)(2,1)}, bf16[256,2048]{1,0:T(8,128)(2,1)}, u32[]{:S(2)}, u32[]{:S(2)}) collective-permute-start(bf16[256,2048]{1,0:T(8,128)(2,1)} %get-tuple-element.29), channel_id=1, source_target_pairs={{0,2},{1,3},{2,0},{3,1},{4,6},{5,7},{6,4},{7,5},{8,10},{9,11},{10,... | collective-permute-start | bytes 3145736 | tf_op jit(solution)/shard_map/ppermute | solution.py:29
  99.6 57.7 %all-to-all-start.2 = ((bf16[16,64,256]{2,1,0:T(8,128)(2,1)}), bf16[16,64,256]{2,1,0:T(8,128)(2,1)}, u32[]{:S(2)}, u32[]{:S(2)}) async-start(bf16[16,64,256]{2,1,0:T(8,128)(2,1)} %bitcast.19), calls=%async_computation.2 | async-start | bytes 1048576 | tf_op jit(solution)/shard_map/all_to_all | solution.py:265
  112.7 44.6 %collective-permute-start.14 = (bf16[64,2048]{1,0:T(8,128)(2,1)}, bf16[64,2048]{1,0:T(8,128)(2,1)S(1)}, u32[]{:S(2)}, u32[]{:S(2)}) collective-permute-start(bf16[64,2048]{1,0:T(8,128)(2,1)} %slice.123), channel_id=1, source_target_pairs={{0,2},{1,3},{2,0},{3,1},{4,6},{5,7},{6,4},{7,5},{8,10},{9,11},{10,... | collective-permute-start | bytes 786440 | tf_op jit(solution)/shard_map/ppermute | solution.py:29
  127.2 30.1 %collective-permute-start.18 = (bf16[64,2048]{1,0:T(8,128)(2,1)}, bf16[64,2048]{1,0:T(8,128)(2,1)S(1)}, u32[]{:S(2)}, u32[]{:S(2)}) collective-permute-start(bf16[64,2048]{1,0:T(8,128)(2,1)} %get-tuple-element.37), channel_id=1, source_target_pairs={{0,12},{1,13},{2,14},{3,15},{4,0},{5,1},{6,2},{7,3},{8,4},{9,5},{1... | collective-permute-start | bytes 786440 | tf_op jit(solution)/shard_map/ppermute | solution.py:29
  127.7 29.6 %collective-permute-start.17 = (bf16[64,2048]{1,0:T(8,128)(2,1)}, bf16[64,2048]{1,0:T(8,128)(2,1)S(1)}, u32[]{:S(2)}, u32[]{:S(2)}) collective-permute-start(bf16[64,2048]{1,0:T(8,128)(2,1)} %get-tuple-element.38), channel_id=1, source_target_pairs={{0,8},{1,9},{2,10},{3,11},{4,12},{5,13},{6,14},{7,15},{8,0},{9,1},... | collective-permute-start | bytes 786440 | tf_op jit(solution)/shard_map/ppermute | solution.py:29
  129.1 28.2 %collective-permute-start.16 = (bf16[64,2048]{1,0:T(8,128)(2,1)}, bf16[64,2048]{1,0:T(8,128)(2,1)S(1)}, u32[]{:S(2)}, u32[]{:S(2)}) collective-permute-start(bf16[64,2048]{1,0:T(8,128)(2,1)} %get-tuple-element.39), channel_id=1, source_target_pairs={{0,4},{1,5},{2,6},{3,7},{4,8},{5,9},{6,10},{7,11},{8,12},{9,13},{1... | collective-permute-start | bytes 786440 | tf_op jit(solution)/shard_map/ppermute | solution.py:29
  159.2 9.3 %collective-permute-start.19 = (bf16[64,2048]{1,0:T(8,128)(2,1)S(1)}, bf16[64,2048]{1,0:T(8,128)(2,1)S(1)}, u32[]{:S(2)}, u32[]{:S(2)}) collective-permute-start(bf16[64,2048]{1,0:T(8,128)(2,1)S(1)} %get-tuple-element.31), channel_id=1, source_target_pairs={{0,2},{1,3},{2,0},{3,1},{4,6},{5,7},{6,4},{7,5},{8,10},{9,11},{10,... | collective-permute-start | bytes 786440 | tf_op jit(solution)/shard_map/ppermute | solution.py:29
  162.1 28.4 %collective-permute-start.24 = (bf16[64,2048]{1,0:T(8,128)(2,1)S(1)}, bf16[64,2048]{1,0:T(8,128)(2,1)S(1)}, u32[]{:S(2)}, u32[]{:S(2)}) collective-permute-start(bf16[64,2048]{1,0:T(8,128)(2,1)S(1)} %get-tuple-element.31), channel_id=1, source_target_pairs={{0,4},{1,5},{2,6},{3,7},{4,8},{5,9},{6,10},{7,11},{8,12},{9,13},{1... | collective-permute-start | bytes 786440 | tf_op jit(solution)/shard_map/ppermute | solution.py:29
  162.1 32.3 %collective-permute-start.22 = (bf16[64,2048]{1,0:T(8,128)(2,1)S(1)}, bf16[64,2048]{1,0:T(8,128)(2,1)S(1)}, u32[]{:S(2)}, u32[]{:S(2)}) collective-permute-start(bf16[64,2048]{1,0:T(8,128)(2,1)S(1)} %get-tuple-element.31), channel_id=1, source_target_pairs={{0,8},{1,9},{2,10},{3,11},{4,12},{5,13},{6,14},{7,15},{8,0},{9,1},... | collective-permute-start | bytes 786440 | tf_op jit(solution)/shard_map/ppermute | solution.py:29
  163.5 13.1 %collective-permute-start.20 = (bf16[64,2048]{1,0:T(8,128)(2,1)S(1)}, bf16[64,2048]{1,0:T(8,128)(2,1)S(1)}, u32[]{:S(2)}, u32[]{:S(2)}) collective-permute-start(bf16[64,2048]{1,0:T(8,128)(2,1)S(1)} %get-tuple-element.31), channel_id=1, source_target_pairs={{0,12},{1,13},{2,14},{3,15},{4,0},{5,1},{6,2},{7,3},{8,4},{9,5},{1... | collective-permute-start | bytes 786440 | tf_op jit(solution)/shard_map/ppermute | solution.py:29
  168.5 28.8 %collective-permute-start.32 = (bf16[64,2048]{1,0:T(8,128)(2,1)S(1)}, bf16[64,2048]{1,0:T(8,128)(2,1)S(1)}, u32[]{:S(2)}, u32[]{:S(2)}) collective-permute-start(bf16[64,2048]{1,0:T(8,128)(2,1)S(1)} %get-tuple-element.32), channel_id=1, source_target_pairs={{0,4},{1,5},{2,6},{3,7},{4,8},{5,9},{6,10},{7,11},{8,12},{9,13},{1... | collective-permute-start | bytes 786440 | tf_op jit(solution)/shard_map/ppermute | solution.py:29
  173.3 9.0 %collective-permute-start.28 = (bf16[64,2048]{1,0:T(8,128)(2,1)S(1)}, bf16[64,2048]{1,0:T(8,128)(2,1)S(1)}, u32[]{:S(2)}, u32[]{:S(2)}) collective-permute-start(bf16[64,2048]{1,0:T(8,128)(2,1)S(1)} %get-tuple-element.32), channel_id=1, source_target_pairs={{0,12},{1,13},{2,14},{3,15},{4,0},{5,1},{6,2},{7,3},{8,4},{9,5},{1... | collective-permute-start | bytes 786440 | tf_op jit(solution)/shard_map/ppermute | solution.py:29
  176.6 11.2 %collective-permute-start.29 = (bf16[64,2048]{1,0:T(8,128)(2,1)S(1)}, bf16[64,2048]{1,0:T(8,128)(2,1)S(1)}, u32[]{:S(2)}, u32[]{:S(2)}) collective-permute-start(bf16[64,2048]{1,0:T(8,128)(2,1)S(1)} %collective-permute-done.27), channel_id=1, source_target_pairs={{0,12},{1,13},{2,14},{3,15},{4,0},{5,1},{6,2},{7,3},{8,4},{9,5},{1... | collective-permute-start | bytes 786440 | tf_op jit(solution)/shard_map/ppermute | solution.py:29
  189.0 16.9 %collective-permute-start.21 = (bf16[64,2048]{1,0:T(8,128)(2,1)S(1)}, bf16[64,2048]{1,0:T(8,128)(2,1)S(1)}, u32[]{:S(2)}, u32[]{:S(2)}) collective-permute-start(bf16[64,2048]{1,0:T(8,128)(2,1)S(1)} %collective-permute-done.20), channel_id=1, source_target_pairs={{0,2},{1,3},{2,0},{3,1},{4,6},{5,7},{6,4},{7,5},{8,10},{9,11},{10,... | collective-permute-start | bytes 786440 | tf_op jit(solution)/shard_map/ppermute | solution.py:29
  190.5 11.0 %collective-permute-start.33 = (bf16[64,2048]{1,0:T(8,128)(2,1)S(1)}, bf16[64,2048]{1,0:T(8,128)(2,1)S(1)}, u32[]{:S(2)}, u32[]{:S(2)}) collective-permute-start(bf16[64,2048]{1,0:T(8,128)(2,1)S(1)} %collective-permute-done.27), channel_id=1, source_target_pairs={{0,4},{1,5},{2,6},{3,7},{4,8},{5,9},{6,10},{7,11},{8,12},{9,13},{1... | collective-permute-start | bytes 786440 | tf_op jit(solution)/shard_map/ppermute | solution.py:29
  194.3 16.6 %collective-permute-start.25 = (bf16[64,2048]{1,0:T(8,128)(2,1)S(1)}, bf16[64,2048]{1,0:T(8,128)(2,1)S(1)}, u32[]{:S(2)}, u32[]{:S(2)}) collective-permute-start(bf16[64,2048]{1,0:T(8,128)(2,1)S(1)} %collective-permute-done.24), channel_id=1, source_target_pairs={{0,2},{1,3},{2,0},{3,1},{4,6},{5,7},{6,4},{7,5},{8,10},{9,11},{10,... | collective-permute-start | bytes 786440 | tf_op jit(solution)/shard_map/ppermute | solution.py:29
  195.8 13.6 %collective-permute-start.23 = (bf16[64,2048]{1,0:T(8,128)(2,1)S(1)}, bf16[64,2048]{1,0:T(8,128)(2,1)S(1)}, u32[]{:S(2)}, u32[]{:S(2)}) collective-permute-start(bf16[64,2048]{1,0:T(8,128)(2,1)S(1)} %collective-permute-done.22), channel_id=1, source_target_pairs={{0,2},{1,3},{2,0},{3,1},{4,6},{5,7},{6,4},{7,5},{8,10},{9,11},{10,... | collective-permute-start | bytes 786440 | tf_op jit(solution)/shard_map/ppermute | solution.py:29
  201.5 51.3 %collective-permute-start.34 = (bf16[512,2048]{1,0:T(8,128)(2,1)S(1)}, bf16[512,2048]{1,0:T(8,128)(2,1)}, u32[]{:S(2)}, u32[]{:S(2)}) collective-permute-start(bf16[512,2048]{1,0:T(8,128)(2,1)S(1)} %constant_dynamic-update-slice_fusion.8.go_ref), channel_id=1, source_target_pairs={{0,1},{1,0},{2,3},{3,2},{4,5},{5,4},{6,7},{7,6},{8,9},{9,8},{10,11... | collective-permute-start | bytes 6291464 | tf_op jit(solution)/shard_map/ppermute | solution.py:29
  211.7 49.0 %collective-permute-start.26 = (bf16[512,2048]{1,0:T(8,128)(2,1)}, bf16[512,2048]{1,0:T(8,128)(2,1)}, u32[]{:S(2)}, u32[]{:S(2)}) collective-permute-start(bf16[512,2048]{1,0:T(8,128)(2,1)} %constant_dynamic-update-slice_fusion.go_ref), channel_id=1, source_target_pairs={{0,1},{1,0},{2,3},{3,2},{4,5},{5,4},{6,7},{7,6},{8,9},{9,8},{10,11... | collective-permute-start | bytes 6291464 | tf_op jit(solution)/shard_map/ppermute | solution.py:29
  237.2 13.4 %all-to-all-start.4 = ((bf16[8,128,256]{2,1,0:T(8,128)(2,1)}), bf16[8,128,256]{2,1,0:T(8,128)(2,1)}, u32[]{:S(2)}, u32[]{:S(2)}) async-start(bf16[8,128,256]{2,1,0:T(8,128)(2,1)} %bitcast.65), calls=%async_computation.4 | async-start | bytes 1048576 | tf_op jit(solution)/shard_map/all_to_all | solution.py:306
  (19 other events, 145.8 us)

commit v2 on v1

v2 whole, which is shorter than its diff:
```python
import functools

import jax
import jax.numpy as jnp
from jax import lax
from jax.experimental import pallas as pl
from jax.experimental.pallas import tpu as pltpu
from jax.sharding import PartitionSpec as P

NX, NZ, NC = 4, 2, 2
NT = NX * NZ * NC
DOUT = 4096
HALF = DOUT // 2
X_FIRST = 2048
EPS = 1e-05
F32, BF16 = jnp.float32, jnp.bfloat16
VMEM = 48 * 1024 * 1024
BIG = 40 * 1024 * 1024


def shift(dx, dz, dc):
    pairs = []
    for x in range(NX):
        for z in range(NZ):
            for c in range(NC):
                pairs.append((x * 4 + z * 2 + c, (x + dx) % NX * 4 + (z ^ dz) * 2 + (c ^ dc)))
    return pairs


def send(v, dx=0, dz=0, dc=0):
    return lax.ppermute(v, "tensor", shift(dx, dz, dc))


def params(limit=VMEM):
    return pltpu.CompilerParams(vmem_limit_bytes=limit)


def cost(macs, nbytes):
    return pl.CostEstimate(flops=2 * macs, bytes_accessed=nbytes, transcendentals=0)


def nt(a, b):
    return lax.dot_general(a, b, (((1,), (1,)), ((), ())), preferred_element_type=F32)


def tn(a, b):
    return lax.dot_general(a, b, (((0,), (0,)), ((), ())), preferred_element_type=F32)


def oproj_kernel(pos, o_ref, a_ref, own_ref, oth_ref):
    z, c = pos[1], pos[2]
    for dz in range(NZ):
        for dc, out in ((0, own_ref), (1, oth_ref)):
            block = (z ^ dz) * 2 + (c ^ dc)
            rows = o_ref[pl.ds(pl.multiple_of(block * 256, 256), 256), :]
            out[0, dz] = jnp.dot(rows, a_ref[...], preferred_element_type=F32)


def oproj_partial(pos, o_proj, attn):
    k, n = attn.shape
    return pl.pallas_call(
        oproj_kernel,
        grid_spec=pltpu.PrefetchScalarGridSpec(
            num_scalar_prefetch=1,
            grid=(NX,),
            in_specs=[
                pl.BlockSpec((1024, k), lambda i, p: ((p[0] + i) % NX, 0)),
                pl.BlockSpec((k, n), lambda i, p: (0, 0)),
            ],
            out_specs=[pl.BlockSpec((1, NZ, 256, n), lambda i, p: (i, 0, 0, 0))] * 2,
        ),
        out_shape=[jax.ShapeDtypeStruct((NX, NZ, 256, n), F32)] * 2,
        compiler_params=params(),
        cost_estimate=cost(DOUT * k * n, 9 << 20),
        name="oproj_partial",
    )(pos, o_proj, attn)


def join_kernel(which, xo_ref, xp_ref, ho_ref, hp_ref, w_ref, v_ref, *outs):
    acc = nt(ho_ref[...], w_ref[2]) + nt(hp_ref[...], v_ref[2])
    for s in range(2):
        cols = slice(s * 256, (s + 1) * 256)
        acc += nt(xo_ref[:, cols], w_ref[s]) + nt(xp_ref[:, cols], v_ref[s])
    if which == 0:
        for dx in range(NX):
            outs[dx][...] = acc[dx * 128 : (dx + 1) * 128].astype(outs[dx].dtype)
    else:
        for dx in range(NX):
            for dz in range(NZ):
                at = dx * 128 + dz * 64
                outs[dz][dx * 64 : (dx + 1) * 64, :] = acc[at : at + 64].astype(outs[dz].dtype)


def join(which, xo, xp, ho, hp, w, v):
    tile = 512
    width = X_FIRST if which == 0 else DOUT - X_FIRST
    base = X_FIRST // tile * which
    whole = lambda a: pl.BlockSpec(a.shape, lambda j: (0, 0))
    wspec = pl.BlockSpec((3, tile, 256), lambda j: (0, base + j, 0))
    if which == 0:
        shapes = [(128, F32)] + [(128, BF16)] * 3
    else:
        shapes = [(256, F32), (256, BF16)]
    return pl.pallas_call(
        functools.partial(join_kernel, which),
        grid=(width // tile,),
        in_specs=[whole(xo), whole(xp), whole(ho), whole(hp), wspec, wspec],
        out_specs=[pl.BlockSpec((n, tile), lambda j: (0, j)) for n, _ in shapes],
        out_shape=[jax.ShapeDtypeStruct((n, width), t) for n, t in shapes],
        compiler_params=params(),
        cost_estimate=cost(512 * 1536 * width, width * 4608),
        name="join",
    )(xo, xp, ho, hp, w, v)


def norm_kernel(
    ka, ra, kb, rb1, rb2, rb3, cot_ref, out_ref, pga_ref, pgb_ref, gg_ref, pre
):
    first, half = X_FIRST // 256, HALF // 256

    def gain_of(t):
        parts = cot_ref[t, 64:, :].astype(F32)
        return (parts[0:1] + parts[1:2]) + parts[2:3]

    square = jnp.zeros((64, 1), F32)
    inner = jnp.zeros((64, 1), F32)
    for t in range(NT):
        at = t if t < first else t - first
        cols = slice(at * 256, (at + 1) * 256)
        if t < first:
            d = ka[:, cols] + ra[:, cols].astype(F32)
        else:
            d = kb[:, cols] + rb1[:, cols].astype(F32)
            d += rb2[:, cols].astype(F32) + rb3[:, cols].astype(F32)
        pre[t] = d
        up = gain_of(t) * cot_ref[t, :64, :].astype(F32)
        square += jnp.sum(d * d, axis=1, keepdims=True)
        inner += jnp.sum(up * d, axis=1, keepdims=True)
    inv = 1.0 / jnp.sqrt(square / DOUT + EPS)
    slope = inner * inv
    row = lax.broadcasted_iota(jnp.int32, (16, 256), 0)
    for t in range(NT):
        cols = slice(t % half * 256, (t % half + 1) * 256)
        raw = cot_ref[t, :64, :].astype(F32)
        gain = gain_of(t)
        normed = pre[t] * inv
        grad = ((gain * raw - normed * (slope / DOUT)) * inv).astype(BF16)
        if t < half:
            pga_ref[:, cols] = grad
        else:
            pgb_ref[:, cols] = grad
        total = jnp.sum(raw * normed, axis=0, keepdims=True)
        hi = total.astype(BF16).astype(F32)
        extra = jnp.where(row == 0, hi, jnp.where(row == 1, total - hi, 0.0))
        gg_ref[t] = extra.astype(BF16)
        out_ref[t] = (gain * normed).astype(BF16)


def norm(ka, ra, kb, rb, cot):
    whole = pl.BlockSpec(memory_space=pltpu.VMEM)
    return pl.pallas_call(
        norm_kernel,
        in_specs=[whole] * 7,
        out_specs=[whole] * 4,
        out_shape=[
            jax.ShapeDtypeStruct((NT, 64, 256), BF16),
            jax.ShapeDtypeStruct((64, HALF), BF16),
            jax.ShapeDtypeStruct((64, HALF), BF16),
            jax.ShapeDtypeStruct((NT, 16, 256), BF16),
        ],
        scratch_shapes=[pltpu.VMEM((NT, 64, 256), F32)],
        compiler_params=params(),
        cost_estimate=cost(0, 6 << 20),
        name="norm",
    )(ka, ra, kb, *rb, cot)


def grad_kernel(ng, *refs):
    out = refs[-1]
    g = jnp.concatenate([g[...] for g in refs[:ng]], axis=0)
    both = tn(g, refs[ng][...])
    for s in range(3):
        out[s] = both[:, s * 256 : (s + 1) * 256]


def grad(which, gs, x, into=None):
    tile = 512
    steps = HALF // tile
    base = which * steps
    specs = [pl.BlockSpec((g.shape[0], tile), lambda j: (0, j)) for g in gs]
    specs.append(pl.BlockSpec(x.shape, lambda j: (0, 0)))
    args = list(gs) + [x]
    if into is not None:
        specs.append(pl.BlockSpec(memory_space=pl.ANY))
        args.append(into)
    return pl.pallas_call(
        functools.partial(grad_kernel, len(gs)),
        grid=(steps,),
        in_specs=specs,
        out_specs=pl.BlockSpec((3, tile, 256), lambda j: (0, base + j, 0)),
        out_shape=jax.ShapeDtypeStruct((3, DOUT, 256), F32),
        input_output_aliases={} if into is None else {len(args) - 1: 0},
        compiler_params=params(BIG),
        cost_estimate=cost(1024 * 768 * HALF, 12 << 20),
        name="grad",
    )(*args)


def local(
    attn_out,
    o_proj,
    high_resid,
    low_hidden,
    mid_hidden,
    route_list,
    fc_weight,
    norm_gain,
    cotangent,
):
    trainers = lax.axis_size("dp")
    toks = route_list.shape[0]
    cap = toks // 2
    slots = trainers * cap
    t = lax.axis_index("tensor")
    x, z, c = t // 4, t // 2 % 2, t % 2
    pos = jnp.stack([x, z, c]).astype(jnp.int32)

    here = jnp.arange(toks, dtype=jnp.int32)
    same = (route_list[:, None] == route_list[None, :]) & (here[None, :] < here[:, None])
    within = jnp.sum(same.astype(jnp.int32), axis=1)

    def onehot(slot, n):
        return (slot[:, None] == jnp.arange(n, dtype=jnp.int32)[None, :]).astype(BF16)

    pick = onehot(route_list * cap + within, slots)
    back_pick = onehot(within // 8 * 80 + route_list * 8 + within % 8, NT * 80)

    at = jnp.arange(slots, dtype=jnp.int32)
    inner = at // 8 % 8 * cap + at % 8
    block = at // 64

    def device(dc, dx, dz):
        return (x + dx) % 4 * 4 + (z ^ dz) * 2 + (c ^ dc)

    straight = onehot(inner + block * 8, slots)
    from_a = device(block // 8, block // 2 % 4, block % 2) * 8
    order_a = onehot(inner + from_a, slots)
    y, zl = lax.axis_index("dp") // 2, lax.axis_index("dp") % 2
    replica = at // 8 % 8
    apart = (y - replica // 2 + 4) % 4 * 2 + (replica % 2 ^ zl)
    near_order = onehot(apart * cap + at % 8 + from_a, slots)
    towards = (route_list % 2 ^ zl) * 4 + (route_list // 2 - y + 4) % 4
    near_pick = onehot(towards * cap + within, slots)
    order_b = onehot((block // 8 * 8 + block % 4 * 2 + block // 4 % 2) * 64 + at % 64, slots)

    def moved(order, v):
        return jnp.dot(order, v, preferred_element_type=BF16)

    def packed(pick, v):
        return lax.dot_general(pick, v, (((0,), (1,)), ((), ())), preferred_element_type=BF16)

    early = packed(pick, jnp.concatenate([low_hidden, mid_hidden, cotangent], axis=0))
    early = lax.all_to_all(early.reshape(trainers, cap, -1), "dp", 0, 0).reshape(slots, -1)

    own, oth = oproj_partial(pos, o_proj, attn_out)
    own = own + send(oth, dc=1)
    w = jnp.transpose(fc_weight[0], (1, 0, 2))
    w, own = lax.optimization_barrier((w, own))
    w_other = send(w, dc=1)
    narrow = own.astype(BF16)
    sums = own[0]
    for dx in range(1, NX):
        sums = sums + send(narrow[dx], dx).astype(F32)
    term = sums[0] + send(sums[1], dz=1)
    high_hidden = (high_resid.astype(F32) + term).astype(BF16)

    early, high_hidden = lax.optimization_barrier((early, high_hidden))

    gain = norm_gain[0]
    part0 = lax.reduce_precision(gain, 8, 7)
    part1 = lax.reduce_precision(gain - part0, 8, 7)
    part2 = gain - part0 - part1
    parts = jnp.pad(jnp.stack([part0, part1, part2]).astype(BF16), ((0, 13), (0, 0)))
    cot = jnp.concatenate(
        [
            moved(straight, early[:, 512:]).reshape(NT, 64, 256),
            jnp.broadcast_to(parts[None], (NT, 16, 256)),
        ],
        axis=1,
    )
    cot = lax.all_to_all(cot, "tensor", 0, 0)

    lowmid = early[:, :512]
    keep, other = [packed(near_pick[:, i * 512 : (i + 1) * 512], high_hidden) for i in range(2)]
    got = lax.ppermute(other, "dp", [(i, i ^ 1) for i in range(8)])
    pair = jnp.stack([keep.reshape(4, cap, -1), got.reshape(4, cap, -1)], axis=1)
    far = [
        lax.ppermute(pair[dy], "dp", [(i, (i + 2 * dy) % 8) for i in range(8)])
        for dy in range(1, 4)
    ]
    high_rows = jnp.concatenate([pair[0]] + far, axis=0).reshape(slots, -1)
    xo, xs = moved(order_a[:512], lowmid), moved(order_a[512:], lowmid)
    xp = send(xs, dc=1)
    ho, hs = moved(near_order[:512], high_rows), moved(near_order[512:], high_rows)
    hp = send(hs, dc=1)
    ho, hp, cot = lax.optimization_barrier((ho, hp, cot))

    b = join(1, xo, xp, ho, hp, w, w_other)
    bz = b[0] + send(b[1], dz=1).astype(F32)
    a = join(0, xo, xp, ho, hp, w, w_other)
    a, xs, hs = lax.optimization_barrier((a, xs, hs))
    got = [send(a[dx], dx) for dx in range(1, NX)]
    got, _ = lax.optimization_barrier((got, bz))
    ax = a[0] + got[0].astype(F32) + got[1].astype(F32) + got[2].astype(F32)
    az = send(ax[64:].astype(BF16), dz=1)
    bx = [send(bz[dx * 64 : (dx + 1) * 64].astype(BF16), dx) for dx in range(1, NX)]

    xa = jnp.concatenate(
        [jnp.concatenate([xo, xs], axis=0), jnp.concatenate([ho, hs], axis=0)], axis=1
    )
    xb = moved(order_b, xa)
    xa, xb, az = lax.optimization_barrier((xa, xb, az))

    outputs, ga, gb, gg = norm(ax[:64], az, bz[:64], bx, cot)

    far = send(ga, dz=1)
    near = [send(gb, -dx) for dx in range(1, NX)]
    outputs = outputs.reshape(NT, trainers, 8, 256).transpose(1, 0, 2, 3)
    outputs = lax.all_to_all(outputs, "dp", 0, 0)
    a0 = jnp.concatenate([ga, far], axis=0)
    near, _, outputs = lax.optimization_barrier((near, a0, outputs))
    b0 = jnp.concatenate([gb] + near, axis=0)
    a1 = [send(a0, -dx) for dx in range(1, NX)]
    b1 = send(b0, dz=1)
    a0p, b0p = send(a0, dc=1), send(b0, dc=1)
    outputs = outputs.transpose(1, 0, 2, 3).reshape(NT, 64, 256)
    outputs = jnp.concatenate([outputs, gg], axis=1)
    a1p, b1p = [send(v, dc=1) for v in a1], send(b1, dc=1)
    returned = lax.all_to_all(outputs, "tensor", 0, 0)
    fc = grad(0, [a0] + a1 + [a0p] + a1p, xa)
    fc = grad(1, (b0, b1, b0p, b1p), xb, fc)
    returned, fc = lax.optimization_barrier((returned, fc))
    gain_grad = jnp.sum(returned[:, 64:66].astype(F32), axis=(0, 1))[None, :]
    draft_hidden = lax.dot_general(
        returned.reshape(NT * 80, 256),
        back_pick,
        (((0,), (1,)), ((), ())),
        preferred_element_type=BF16,
    )
    fc_grad = jnp.transpose(fc, (1, 0, 2))[None]
    return (draft_hidden, fc_grad, gain_grad)


def solution(mesh):
    return jax.shard_map(
        local,
        mesh=mesh,
        in_specs=(
            P("tensor", "dp"),
            P(None, "tensor"),
            P("tensor", "dp"),
            P("tensor", "dp"),
            P("tensor", "dp"),
            P("dp"),
            P("dp", None, None, "tensor"),
            P("dp", "tensor"),
            P("tensor", "dp"),
        ),
        out_specs=(P("tensor", "dp"), P("dp", None, None, "tensor"), P("dp", "tensor")),
        check_vma=False,
    )
```

time: 269 us -> 217 us (0.81)
  blocking collectives: 48.4 us -> 0 us
  matrix products: 5.34 us -> 15 us
  local copies, waits for them, and re-layouts: 15.9 us -> 10.1 us
  Pallas kernels: 36.5 us -> 32.5 us
  starting transfers between devices: 74.3 us -> 70.5 us
  waiting for transfers between devices: 79.6 us -> 76.7 us
    all_gather x1 -> x0, blocking collectives: 27.5 us -> none  [local(): gain = lax.all_gather(norm_gain[0], 'tensor', axis=0)]
    all_to_all x1 -> x0, blocking collectives: 20.9 us -> none  [local(): returned = lax.all_to_all(outputs, 'tensor', 0, 0)]
    ppermute x35 -> x30, starting transfers between devices: 53.4 us -> 43 us  [send(): return lax.ppermute(v, 'tensor', shift(dx, dz, dc))]
    dot_general x1 -> x7, matrix products: 2.16 us -> 12.5 us  [the longest x6 10.2 us: moved(): return jnp.dot(order, v, preferred_element_type=BF16)]
    all_to_all x4, waiting for transfers between devices: 12.2 us -> 5.13 us  [the longest x1 5.12 us: local(): outputs = lax.all_to_all(outputs, 'dp', 0, 0)]
    ppermute x0 -> x4, starting transfers between devices: none -> 4.34 us  [the longest x3 4.25 us: local(): lax.ppermute(pair[dy], 'dp', [(i, (i + 2 * dy) % 8) for i in range(8)])]
    slice x5 -> x2, local copies, waits for them, and re-layouts: 4.14 us -> 0.07 us  [local(): outputs, ga, gb, gg = norm(ax[:64], az, bz[:64], bx, cot)]
    eq x0 -> x3, other arithmetic: none -> 3.59 us  [onehot(): slot[:, None] == jnp.arange(n, dtype=jnp.int32)[None, :]]
  transfers between devices with their start and end apart: 39 -> 38, of which waited for: 18 -> 16; matrix products, arithmetic and copies ran while one was open for 9% -> 11% of each run, Pallas kernels for 8% -> 10%
where the time goes in v2:
time: 217 us; the launch traced here: 215 us
  waiting for transfers between devices  76.7 us (35%)
  starting transfers between devices  70.5 us (32%)
  Pallas kernels  32.5 us (15%)
  matrix products  15 us (7%)
  local copies, waits for them, and re-layouts  10.1 us (5%)
  other arithmetic  9.62 us (4%)
    ppermute x30, waiting for transfers between devices, send(): return lax.ppermute(v, 'tensor', shift(dx, dz, dc))  68.8 us
    ppermute x30, starting transfers between devices, send(): return lax.ppermute(v, 'tensor', shift(dx, dz, dc))  43 us
    pallas_call x2, Pallas kernels, grad(): pl.pallas_call(functools.partial(grad_kernel, len(gs)), grid=(steps,), in...  14.4 us
    pallas_call x2, Pallas kernels, join(): pl.pallas_call(functools.partial(join_kernel, which), grid=(width // tile...  12.1 us
    dot_general x6, matrix products, moved(): return jnp.dot(order, v, preferred_element_type=BF16)  10.2 us
    all_to_all x1, starting transfers between devices, local(): returned = lax.all_to_all(outputs, 'tensor', 0, 0)  6.67 us
    all_to_all x1, starting transfers between devices, local(): cot = lax.all_to_all(cot, 'tensor', 0, 0)  6.61 us
    unnamed x32, local copies, waits for them, and re-layouts  5.97 us
  transfers between devices with their start and end apart: 38, of which 16 were waited for; matrix products, arithmetic and copies ran while one was open for 11% of the time, Pallas kernels for 10%

profile of v2, /device:TPU:1, one launch (start us, length us, event | category | flops | bytes accessed | tf_op | source)
XLA Modules:
  0.0 215.5 jit_solution(17195454453190539870)
XLA Ops:
  1.7 4.4 %oproj_partial.1 = (f32[4,2,256,256]{3,2,1,0:T(8,128)S(1)}, f32[4,2,256,256]{3,2,1,0:T(8,128)S(1)}) custom-call(s32[3]{0:T(128)S(1)} %pad_add_fusion.pos, bf16[4096,512]{1,0:T(8,128)(2,1)} %o_ref.1, bf16[512,256]{1,0:T(8,128)(2,1)S(1)} %copy-done.3), custom_call_target="tpu_custom_call" | custom-call | flops 1073741824 | bytes 9437184 | tf_op jit(solution)/shard_map/oproj_partial/pallas_call | solution.py:61
  7.6 3.8 %collective-permute-done = f32[4,2,256,256]{3,2,1,0:T(8,128)S(1)} collective-permute-done((f32[4,2,256,256]{3,2,1,0:T(8,128)S(1)}, f32[4,2,256,256]{3,2,1,0:T(8,128)S(1)}, u32[]{:S(2)}, u32[]{:S(2)}) %collective-permute-start) | collective-permute-done | bytes 2097184 | tf_op jit(solution)/shard_map/ppermute | solution.py:31
  14.3 5.8 %all-to-all-start = ((bf16[8,128,768]{2,1,0:T(8,128)(2,1)}), bf16[8,128,768]{2,1,0:T(8,128)(2,1)}, u32[]{:S(2)}, u32[]{:S(2)}) async-start(bf16[8,128,768]{2,1,0:T(8,128)(2,1)} %bitcast.70), calls=%async_computation | async-start | bytes 3145728 | tf_op jit(solution)/shard_map/all_to_all | solution.py:263
  28.0 2.6 %collective-permute-done.1 = bf16[2,256,256]{2,1,0:T(8,128)(2,1)S(1)} collective-permute-done((bf16[2,256,256]{2,1,0:T(8,128)(2,1)S(1)}, bf16[2,256,256]{2,1,0:T(8,128)(2,1)S(1)}, u32[]{:S(2)}, u32[]{:S(2)}) %collective-permute-start.1) | collective-permute-done | bytes 262176 | tf_op jit(solution)/shard_map/ppermute | solution.py:31
  30.7 6.6 %collective-permute-done.2 = bf16[2,256,256]{2,1,0:T(8,128)(2,1)S(1)} collective-permute-done((bf16[2,256,256]{2,1,0:T(8,128)(2,1)S(1)}, bf16[2,256,256]{2,1,0:T(8,128)(2,1)S(1)}, u32[]{:S(2)}, u32[]{:S(2)}) %collective-permute-start.2) | collective-permute-done | bytes 262176 | tf_op jit(solution)/shard_map/ppermute | solution.py:31
  37.4 3.4 %collective-permute-start.4 = (f32[256,256]{1,0:T(8,128)S(1)}, f32[256,256]{1,0:T(8,128)S(1)}, u32[]{:S(2)}, u32[]{:S(2)}) collective-permute-start(f32[256,256]{1,0:T(8,128)S(1)} %slice_bitcast_fusion), channel_id=1, source_target_pairs={{0,2},{1,3},{2,0},{3,1},{4,6},{5,7},{6,4},{7,5},{8,10},{9,11},{10,... | collective-permute-start | bytes 786440 | tf_op jit(solution)/shard_map/ppermute | solution.py:31
  41.0 7.2 %collective-permute-done.4 = f32[256,256]{1,0:T(8,128)S(1)} collective-permute-done((f32[256,256]{1,0:T(8,128)S(1)}, f32[256,256]{1,0:T(8,128)S(1)}, u32[]{:S(2)}, u32[]{:S(2)}) %collective-permute-start.4) | collective-permute-done | bytes 262176 | tf_op jit(solution)/shard_map/ppermute | solution.py:31
  51.5 6.6 %all-to-all-start.1 = ((bf16[16,80,256]{2,1,0:T(8,128)(2,1)}), bf16[16,80,256]{2,1,0:T(8,128)(2,1)S(1)}, u32[]{:S(2)}, u32[]{:S(2)}) async-start(bf16[16,80,256]{2,1,0:T(8,128)(2,1)} %pad_maximum_fusion), calls=%async_computation.1 | async-start | bytes 1310720 | tf_op jit(solution)/shard_map/all_to_all | solution.py:291
  62.7 2.1 fusion.8
  65.9 2.7 %collective-permute-done.8 = bf16[2,128,256]{2,1,0:T(8,128)(2,1)S(1)} collective-permute-done((bf16[2,128,256]{2,1,0:T(8,128)(2,1)S(1)}, bf16[2,128,256]{2,1,0:T(8,128)(2,1)S(1)}, u32[]{:S(2)}, u32[]{:S(2)}) %collective-permute-start.8) | collective-permute-done | bytes 131104 | tf_op jit(solution)/shard_map/ppermute | solution.py:298
  70.3 2.1 fusion.10.xo_ref
  73.0 6.1 %join.3 = (f32[256,2048]{1,0:T(8,128)S(1)}, bf16[256,2048]{1,0:T(8,128)(2,1)S(1)}) custom-call(bf16[512,512]{1,0:T(8,128)(2,1)S(1)} %fusion.10.xo_ref, bf16[512,512]{1,0:T(8,128)(2,1)S(1)} %collective-permute-done.5.xp_ref, bf16[512,256]{1,0:T(8,128)(2,1)S(1)} %fusion.6.ho_ref, bf16[512,256]{1,0:T(8,128)(2,1)S(1)} %collective-permute-done.10.hp_ref, ...), custom_call_target="tpu_custom_call" | custom-call | flops 3221225472 | bytes 9437184 | tf_op jit(solution)/shard_map/join/pallas_call | solution.py:104
  79.0 2.9 %collective-permute-start.15 = (bf16[256,2048]{1,0:T(8,128)(2,1)S(1)}, bf16[256,2048]{1,0:T(8,128)(2,1)S(1)}, u32[]{:S(2)}, u32[]{:S(2)}) collective-permute-start(bf16[256,2048]{1,0:T(8,128)(2,1)S(1)} %get-tuple-element.57), channel_id=1, source_target_pairs={{0,2},{1,3},{2,0},{3,1},{4,6},{5,7},{6,4},{7,5},{8,10},{9,11},{10,... | collective-permute-start | bytes 3145736 | tf_op jit(solution)/shard_map/ppermute | solution.py:31
  82.0 6.0 %join.2 = (f32[128,2048]{1,0:T(8,128)S(1)}, bf16[128,2048]{1,0:T(8,128)(2,1)S(1)}, bf16[128,2048]{1,0:T(8,128)(2,1)S(1)}, bf16[128,2048]{1,0:T(8,128)(2,1)S(1)}) custom-call(bf16[512,512]{1,0:T(8,128)(2,1)S(1)} %fusion.10.xo_ref, bf16[512,512]{1,0:T(8,128)(2,1)S(1)} %collective-permute-done.5.xp_ref, bf16[512,256]{1,0:T(8,128)(2,1)S(1)} %fusion.6.ho_ref, ...), custom_call_target="tpu_custom_call" | custom-call | flops 3221225472 | bytes 9437184 | tf_op jit(solution)/shard_map/join/pallas_call | solution.py:104
  89.3 2.4 %collective-permute-start.13 = (bf16[128,2048]{1,0:T(8,128)(2,1)S(1)}, bf16[128,2048]{1,0:T(8,128)(2,1)S(1)}, u32[]{:S(2)}, u32[]{:S(2)}) collective-permute-start(bf16[128,2048]{1,0:T(8,128)(2,1)S(1)} %get-tuple-element.54), channel_id=1, source_target_pairs={{0,8},{1,9},{2,10},{3,11},{4,12},{5,13},{6,14},{7,15},{8,0},{9,1},... | collective-permute-start | bytes 1572872 | tf_op jit(solution)/shard_map/ppermute | solution.py:31
  92.9 12.5 %collective-permute-done.15 = bf16[256,2048]{1,0:T(8,128)(2,1)S(1)} collective-permute-done((bf16[256,2048]{1,0:T(8,128)(2,1)S(1)}, bf16[256,2048]{1,0:T(8,128)(2,1)S(1)}, u32[]{:S(2)}, u32[]{:S(2)}) %collective-permute-start.15) | collective-permute-done | bytes 1048608 | tf_op jit(solution)/shard_map/ppermute | solution.py:31
  106.0 8.7 %collective-permute-done.13 = bf16[128,2048]{1,0:T(8,128)(2,1)S(1)} collective-permute-done((bf16[128,2048]{1,0:T(8,128)(2,1)S(1)}, bf16[128,2048]{1,0:T(8,128)(2,1)S(1)}, u32[]{:S(2)}, u32[]{:S(2)}) %collective-permute-start.13) | collective-permute-done | bytes 524320 | tf_op jit(solution)/shard_map/ppermute | solution.py:31
  115.3 2.5 %collective-permute-start.19 = (bf16[64,2048]{1,0:T(8,128)(2,1)S(1)}, bf16[64,2048]{1,0:T(8,128)(2,1)S(1)}, u32[]{:S(2)}, u32[]{:S(2)}) collective-permute-start(bf16[64,2048]{1,0:T(8,128)(2,1)S(1)} %get-tuple-element.79), channel_id=1, source_target_pairs={{0,12},{1,13},{2,14},{3,15},{4,0},{5,1},{6,2},{7,3},{8,4},{9,5},{1... | collective-permute-start | bytes 786440 | tf_op jit(solution)/shard_map/ppermute | solution.py:31
  118.5 3.1 %fusion.1.refs_4_ = bf16[1024,768]{1,0:T(8,128)(2,1)} fusion(s32[1024]{0:T(1024)S(1)} %fusion.82, bf16[512,256]{1,0:T(8,128)(2,1)S(1)} %fusion.4, bf16[512,256]{1,0:T(8,128)(2,1)S(1)} %fusion.6.ho_ref, bf16[512,512]{1,0:T(8,128)(2,1)S(1)} %fusion.8, bf16[512,512]{1,0:T(8,128)(2,1)S(1)} %fusion.10.xo_ref), kind=kOutput, calls=%fused_computation.5 | convolution fusion | flops 1617952768 | bytes 3149824 | tf_op jit(solution)/shard_map/dot_general | solution.py:257
  126.2 6.8 %collective-permute-done.17.rb1 = bf16[64,2048]{1,0:T(8,128)(2,1)S(1)} collective-permute-done((bf16[64,2048]{1,0:T(8,128)(2,1)S(1)}, bf16[64,2048]{1,0:T(8,128)(2,1)S(1)}, u32[]{:S(2)}, u32[]{:S(2)}) %collective-permute-start.17) | collective-permute-done | bytes 262176 | tf_op jit(solution)/shard_map/ppermute | solution.py:31
  135.0 2.2 %collective-permute-start.20 = (bf16[64,2048]{1,0:T(8,128)(2,1)S(1)}, bf16[64,2048]{1,0:T(8,128)(2,1)}, u32[]{:S(2)}, u32[]{:S(2)}) collective-permute-start(bf16[64,2048]{1,0:T(8,128)(2,1)S(1)} %get-tuple-element.65), channel_id=1, source_target_pairs={{0,12},{1,13},{2,14},{3,15},{4,0},{5,1},{6,2},{7,3},{8,4},{9,5},{1... | collective-permute-start | bytes 786440 | tf_op jit(solution)/shard_map/ppermute | solution.py:31
  138.1 2.9 %collective-permute-start.23 = (bf16[64,2048]{1,0:T(8,128)(2,1)}, bf16[64,2048]{1,0:T(8,128)(2,1)}, u32[]{:S(2)}, u32[]{:S(2)}) collective-permute-start(bf16[64,2048]{1,0:T(8,128)(2,1)} %get-tuple-element.66), channel_id=1, source_target_pairs={{0,2},{1,3},{2,0},{3,1},{4,6},{5,7},{6,4},{7,5},{8,10},{9,11},{10,... | collective-permute-start | bytes 786440 | tf_op jit(solution)/shard_map/ppermute | solution.py:31
  142.0 4.2 %all-to-all-start.2 = ((bf16[8,16,8,256]{3,2,1,0:T(8,128)(2,1)}), bf16[8,16,8,256]{3,2,1,0:T(8,128)(2,1)}, u32[]{:S(2)}, u32[]{:S(2)}) async-start(bf16[8,16,8,256]{3,2,1,0:T(8,128)(2,1)} %copy_bitcast_fusion.1), calls=%async_computation.2 | async-start | bytes 1048576 | tf_op jit(solution)/shard_map/all_to_all | solution.py:329
  149.1 5.1 %all-to-all-done.2 = bf16[8,16,8,256]{3,2,1,0:T(8,128)(2,1)} async-done(((bf16[8,16,8,256]{3,2,1,0:T(8,128)(2,1)}), bf16[8,16,8,256]{3,2,1,0:T(8,128)(2,1)}, u32[]{:S(2)}, u32[]{:S(2)}) %all-to-all-start.2) | async-done | bytes 524320 | tf_op jit(solution)/shard_map/all_to_all | solution.py:329
  157.3 2.6 %collective-permute-start.30 = (bf16[128,2048]{1,0:T(8,128)(2,1)S(1)}, bf16[128,2048]{1,0:T(8,128)(2,1)S(1)}, u32[]{:S(2)}, u32[]{:S(2)}) collective-permute-start(bf16[128,2048]{1,0:T(8,128)(2,1)S(1)} %constant_dynamic-update-slice_fusion.refs_0_), channel_id=1, source_target_pairs={{0,1},{1,0},{2,3},{3,2},{4,5},{5,4},{6,7},{7,6},{8,9},{9,8},{10,11... | collective-permute-start | bytes 1572872 | tf_op jit(solution)/shard_map/ppermute | solution.py:31
  166.0 15.1 %collective-permute-done.24.refs_1_ = bf16[256,2048]{1,0:T(8,128)(2,1)} collective-permute-done((bf16[256,2048]{1,0:T(8,128)(2,1)S(1)}, bf16[256,2048]{1,0:T(8,128)(2,1)}, u32[]{:S(2)}, u32[]{:S(2)}) %collective-permute-start.24) | collective-permute-done | bytes 1048608 | tf_op jit(solution)/shard_map/ppermute | solution.py:31
  181.2 3.3 %collective-permute-start.26 = (bf16[256,2048]{1,0:T(8,128)(2,1)}, bf16[256,2048]{1,0:T(8,128)(2,1)}, u32[]{:S(2)}, u32[]{:S(2)}) collective-permute-start(bf16[256,2048]{1,0:T(8,128)(2,1)} %collective-permute-done.24.refs_1_), channel_id=1, source_target_pairs={{0,1},{1,0},{2,3},{3,2},{4,5},{5,4},{6,7},{7,6},{8,9},{9,8},{10,11... | collective-permute-start | bytes 3145736 | tf_op jit(solution)/shard_map/ppermute | solution.py:31
  184.4 2.4 %collective-permute-start.33 = (bf16[128,2048]{1,0:T(8,128)(2,1)}, bf16[128,2048]{1,0:T(8,128)(2,1)}, u32[]{:S(2)}, u32[]{:S(2)}) collective-permute-start(bf16[128,2048]{1,0:T(8,128)(2,1)} %collective-permute-done.29.refs_3_), channel_id=1, source_target_pairs={{0,1},{1,0},{2,3},{3,2},{4,5},{5,4},{6,7},{7,6},{8,9},{9,8},{10,11... | collective-permute-start | bytes 1572872 | tf_op jit(solution)/shard_map/ppermute | solution.py:31
  189.4 6.7 %all-to-all-start.3 = ((bf16[16,80,256]{2,1,0:T(8,128)(2,1)}), bf16[16,80,256]{2,1,0:T(8,128)(2,1)}, u32[]{:S(2)}, u32[]{:S(2)}) async-start(bf16[16,80,256]{2,1,0:T(8,128)(2,1)} %pad_maximum_fusion.1), calls=%async_computation.3 | async-start | bytes 1310720 | tf_op jit(solution)/shard_map/all_to_all | solution.py:339
  197.3 7.3 %grad.2.refs_5_ = f32[3,4096,256]{2,1,0:T(8,128)} custom-call(bf16[128,2048]{1,0:T(8,128)(2,1)S(1)} %constant_dynamic-update-slice_fusion.refs_0_, bf16[128,2048]{1,0:T(8,128)(2,1)} %collective-permute-done.27.refs_1_, bf16[128,2048]{1,0:T(8,128)(2,1)} %collective-permute-done.28.refs_2_, bf16[128,2048]{1,0:T(8,128)(2,1)} %collective-permute-done.29.refs_3_, ...), custom_call_target="tpu_custom_call" | custom-call | flops 3221225472 | bytes 12582912 | tf_op jit(solution)/shard_map/grad/pallas_call | solution.py:196
  204.6 7.2 %grad.3 = f32[3,4096,256]{2,1,0:T(8,128)} custom-call(bf16[256,2048]{1,0:T(8,128)(2,1)S(1)} %constant_dynamic-update-slice_fusion.2.refs_0_, bf16[256,2048]{1,0:T(8,128)(2,1)} %collective-permute-done.24.refs_1_, bf16[256,2048]{1,0:T(8,128)(2,1)} %collective-permute-done.25.refs_2_, ...), custom_call_target="tpu_custom_call", output_to_operand_aliasing={{}: (5, {})} | custom-call | flops 3221225472 | bytes 12582912 | tf_op jit(solution)/shard_map/grad/pallas_call | solution.py:196
  213.2 2.2 %fusion.12 = bf16[256,256]{1,0:T(8,128)(2,1)} fusion(bf16[1280,256]{1,0:T(8,128)(2,1)} %bitcast.25, s32[256]{0:T(256)S(1)} %get-tuple-element.89), kind=kOutput, calls=%fused_computation.20 | convolution fusion | flops 168099840 | bytes 787456 | tf_op jit(solution)/shard_map/dot_general | solution.py:344
  (127 shorter events, 54.6 us)
Async XLA Ops:
  11.7 61.3 %collective-permute-start.11 = (bf16[3,4096,256]{2,1,0:T(8,128)(2,1)}, bf16[3,4096,256]{2,1,0:T(8,128)(2,1)}, u32[]{:S(2)}, u32[]{:S(2)}) collective-permute-start(bf16[3,4096,256]{2,1,0:T(8,128)(2,1)} %bitcast.3.w_ref), channel_id=1, source_target_pairs={{0,1},{1,0},{2,3},{3,2},{4,5},{5,4},{6,7},{7,6},{8,9},{9,8},{10,11... | collective-permute-start | bytes 18874376 | tf_op jit(solution)/shard_map/ppermute | solution.py:31
  14.3 33.9 %all-to-all-start = ((bf16[8,128,768]{2,1,0:T(8,128)(2,1)}), bf16[8,128,768]{2,1,0:T(8,128)(2,1)}, u32[]{:S(2)}, u32[]{:S(2)}) async-start(bf16[8,128,768]{2,1,0:T(8,128)(2,1)} %bitcast.70), calls=%async_computation | async-start | bytes 3145728 | tf_op jit(solution)/shard_map/all_to_all | solution.py:263
  22.1 8.6 %collective-permute-start.1 = (bf16[2,256,256]{2,1,0:T(8,128)(2,1)S(1)}, bf16[2,256,256]{2,1,0:T(8,128)(2,1)S(1)}, u32[]{:S(2)}, u32[]{:S(2)}) collective-permute-start(bf16[2,256,256]{2,1,0:T(8,128)(2,1)S(1)} %get-tuple-element.82), channel_id=1, source_target_pairs={{0,4},{1,5},{2,6},{3,7},{4,8},{5,9},{6,10},{7,11},{8,12},{9,13},{1... | collective-permute-start | bytes 786440 | tf_op jit(solution)/shard_map/ppermute | solution.py:31
  24.8 12.4 %collective-permute-start.2 = (bf16[2,256,256]{2,1,0:T(8,128)(2,1)S(1)}, bf16[2,256,256]{2,1,0:T(8,128)(2,1)S(1)}, u32[]{:S(2)}, u32[]{:S(2)}) collective-permute-start(bf16[2,256,256]{2,1,0:T(8,128)(2,1)S(1)} %get-tuple-element.84), channel_id=1, source_target_pairs={{0,8},{1,9},{2,10},{3,11},{4,12},{5,13},{6,14},{7,15},{8,0},{9,1},... | collective-permute-start | bytes 786440 | tf_op jit(solution)/shard_map/ppermute | solution.py:31
  37.4 10.8 %collective-permute-start.4 = (f32[256,256]{1,0:T(8,128)S(1)}, f32[256,256]{1,0:T(8,128)S(1)}, u32[]{:S(2)}, u32[]{:S(2)}) collective-permute-start(f32[256,256]{1,0:T(8,128)S(1)} %slice_bitcast_fusion), channel_id=1, source_target_pairs={{0,2},{1,3},{2,0},{3,1},{4,6},{5,7},{6,4},{7,5},{8,10},{9,11},{10,... | collective-permute-start | bytes 786440 | tf_op jit(solution)/shard_map/ppermute | solution.py:31
  48.6 9.8 %collective-permute-start.6 = (bf16[512,256]{1,0:T(8,128)(2,1)S(1)}, bf16[512,256]{1,0:T(8,128)(2,1)S(1)}, u32[]{:S(2)}, u32[]{:S(2)}) collective-permute-start(bf16[512,256]{1,0:T(8,128)(2,1)S(1)} %convolution_convert_fusion.1), channel_id=1, source_target_pairs={{0,16},{16,0},{32,48},{48,32},{64,80},{80,64},{96,112},{112,96},{1... | collective-permute-start | bytes 786440 | tf_op jit(solution)/shard_map/ppermute | solution.py:295
  51.5 21.5 %all-to-all-start.1 = ((bf16[16,80,256]{2,1,0:T(8,128)(2,1)}), bf16[16,80,256]{2,1,0:T(8,128)(2,1)S(1)}, u32[]{:S(2)}, u32[]{:S(2)}) async-start(bf16[16,80,256]{2,1,0:T(8,128)(2,1)} %pad_maximum_fusion), calls=%async_computation.1 | async-start | bytes 1310720 | tf_op jit(solution)/shard_map/all_to_all | solution.py:291
  58.5 7.4 %collective-permute-start.7 = (bf16[2,128,256]{2,1,0:T(8,128)(2,1)S(1)}, bf16[2,128,256]{2,1,0:T(8,128)(2,1)S(1)}, u32[]{:S(2)}, u32[]{:S(2)}) collective-permute-start(bf16[2,128,256]{2,1,0:T(8,128)(2,1)S(1)} %get-tuple-element.86), channel_id=1, source_target_pairs={{0,32},{16,48},{32,64},{48,80},{64,96},{80,112},{96,0},{112,16},{1... | collective-permute-start | bytes 393224 | tf_op jit(solution)/shard_map/ppermute | solution.py:298
  64.8 8.1 %collective-permute-start.5 = (bf16[512,512]{1,0:T(8,128)(2,1)S(1)}, bf16[512,512]{1,0:T(8,128)(2,1)S(1)}, u32[]{:S(2)}, u32[]{:S(2)}) collective-permute-start(bf16[512,512]{1,0:T(8,128)(2,1)S(1)} %fusion.8), channel_id=1, source_target_pairs={{0,1},{1,0},{2,3},{3,2},{4,5},{5,4},{6,7},{7,6},{8,9},{9,8},{10,11... | collective-permute-start | bytes 1572872 | tf_op jit(solution)/shard_map/ppermute | solution.py:31
  79.0 26.4 %collective-permute-start.15 = (bf16[256,2048]{1,0:T(8,128)(2,1)S(1)}, bf16[256,2048]{1,0:T(8,128)(2,1)S(1)}, u32[]{:S(2)}, u32[]{:S(2)}) collective-permute-start(bf16[256,2048]{1,0:T(8,128)(2,1)S(1)} %get-tuple-element.57), channel_id=1, source_target_pairs={{0,2},{1,3},{2,0},{3,1},{4,6},{5,7},{6,4},{7,5},{8,10},{9,11},{10,... | collective-permute-start | bytes 3145736 | tf_op jit(solution)/shard_map/ppermute | solution.py:31
  88.0 17.9 %collective-permute-start.12 = (bf16[128,2048]{1,0:T(8,128)(2,1)S(1)}, bf16[128,2048]{1,0:T(8,128)(2,1)S(1)}, u32[]{:S(2)}, u32[]{:S(2)}) collective-permute-start(bf16[128,2048]{1,0:T(8,128)(2,1)S(1)} %get-tuple-element.53), channel_id=1, source_target_pairs={{0,4},{1,5},{2,6},{3,7},{4,8},{5,9},{6,10},{7,11},{8,12},{9,13},{1... | collective-permute-start | bytes 1572872 | tf_op jit(solution)/shard_map/ppermute | solution.py:31
  89.3 25.4 %collective-permute-start.13 = (bf16[128,2048]{1,0:T(8,128)(2,1)S(1)}, bf16[128,2048]{1,0:T(8,128)(2,1)S(1)}, u32[]{:S(2)}, u32[]{:S(2)}) collective-permute-start(bf16[128,2048]{1,0:T(8,128)(2,1)S(1)} %get-tuple-element.54), channel_id=1, source_target_pairs={{0,8},{1,9},{2,10},{3,11},{4,12},{5,13},{6,14},{7,15},{8,0},{9,1},... | collective-permute-start | bytes 1572872 | tf_op jit(solution)/shard_map/ppermute | solution.py:31
  91.7 23.0 %collective-permute-start.14 = (bf16[128,2048]{1,0:T(8,128)(2,1)S(1)}, bf16[128,2048]{1,0:T(8,128)(2,1)S(1)}, u32[]{:S(2)}, u32[]{:S(2)}) collective-permute-start(bf16[128,2048]{1,0:T(8,128)(2,1)S(1)} %get-tuple-element.55), channel_id=1, source_target_pairs={{0,12},{1,13},{2,14},{3,15},{4,0},{5,1},{6,2},{7,3},{8,4},{9,5},{1... | collective-permute-start | bytes 1572872 | tf_op jit(solution)/shard_map/ppermute | solution.py:31
  115.0 8.3 %collective-permute-start.16 = (bf16[64,2048]{1,0:T(8,128)(2,1)S(1)}, bf16[64,2048]{1,0:T(8,128)(2,1)S(1)}, u32[]{:S(2)}, u32[]{:S(2)}) collective-permute-start(bf16[64,2048]{1,0:T(8,128)(2,1)S(1)} %slice.183), channel_id=1, source_target_pairs={{0,2},{1,3},{2,0},{3,1},{4,6},{5,7},{6,4},{7,5},{8,10},{9,11},{10,... | collective-permute-start | bytes 786440 | tf_op jit(solution)/shard_map/ppermute | solution.py:31
  115.3 8.9 %collective-permute-start.19 = (bf16[64,2048]{1,0:T(8,128)(2,1)S(1)}, bf16[64,2048]{1,0:T(8,128)(2,1)S(1)}, u32[]{:S(2)}, u32[]{:S(2)}) collective-permute-start(bf16[64,2048]{1,0:T(8,128)(2,1)S(1)} %get-tuple-element.79), channel_id=1, source_target_pairs={{0,12},{1,13},{2,14},{3,15},{4,0},{5,1},{6,2},{7,3},{8,4},{9,5},{1... | collective-permute-start | bytes 786440 | tf_op jit(solution)/shard_map/ppermute | solution.py:31
  117.9 8.3 %collective-permute-start.18 = (bf16[64,2048]{1,0:T(8,128)(2,1)S(1)}, bf16[64,2048]{1,0:T(8,128)(2,1)S(1)}, u32[]{:S(2)}, u32[]{:S(2)}) collective-permute-start(bf16[64,2048]{1,0:T(8,128)(2,1)S(1)} %get-tuple-element.80), channel_id=1, source_target_pairs={{0,8},{1,9},{2,10},{3,11},{4,12},{5,13},{6,14},{7,15},{8,0},{9,1},... | collective-permute-start | bytes 786440 | tf_op jit(solution)/shard_map/ppermute | solution.py:31
  118.1 14.9 %collective-permute-start.17 = (bf16[64,2048]{1,0:T(8,128)(2,1)S(1)}, bf16[64,2048]{1,0:T(8,128)(2,1)S(1)}, u32[]{:S(2)}, u32[]{:S(2)}) collective-permute-start(bf16[64,2048]{1,0:T(8,128)(2,1)S(1)} %get-tuple-element.81), channel_id=1, source_target_pairs={{0,4},{1,5},{2,6},{3,7},{4,8},{5,9},{6,10},{7,11},{8,12},{9,13},{1... | collective-permute-start | bytes 786440 | tf_op jit(solution)/shard_map/ppermute | solution.py:31
  134.6 14.2 %collective-permute-start.22 = (bf16[64,2048]{1,0:T(8,128)(2,1)S(1)}, bf16[64,2048]{1,0:T(8,128)(2,1)}, u32[]{:S(2)}, u32[]{:S(2)}) collective-permute-start(bf16[64,2048]{1,0:T(8,128)(2,1)S(1)} %get-tuple-element.65), channel_id=1, source_target_pairs={{0,4},{1,5},{2,6},{3,7},{4,8},{5,9},{6,10},{7,11},{8,12},{9,13},{1... | collective-permute-start | bytes 786440 | tf_op jit(solution)/shard_map/ppermute | solution.py:31
  134.6 14.2 %collective-permute-start.21 = (bf16[64,2048]{1,0:T(8,128)(2,1)S(1)}, bf16[64,2048]{1,0:T(8,128)(2,1)}, u32[]{:S(2)}, u32[]{:S(2)}) collective-permute-start(bf16[64,2048]{1,0:T(8,128)(2,1)S(1)} %get-tuple-element.65), channel_id=1, source_target_pairs={{0,8},{1,9},{2,10},{3,11},{4,12},{5,13},{6,14},{7,15},{8,0},{9,1},... | collective-permute-start | bytes 786440 | tf_op jit(solution)/shard_map/ppermute | solution.py:31
  135.0 14.1 %collective-permute-start.20 = (bf16[64,2048]{1,0:T(8,128)(2,1)S(1)}, bf16[64,2048]{1,0:T(8,128)(2,1)}, u32[]{:S(2)}, u32[]{:S(2)}) collective-permute-start(bf16[64,2048]{1,0:T(8,128)(2,1)S(1)} %get-tuple-element.65), channel_id=1, source_target_pairs={{0,12},{1,13},{2,14},{3,15},{4,0},{5,1},{6,2},{7,3},{8,4},{9,5},{1... | collective-permute-start | bytes 786440 | tf_op jit(solution)/shard_map/ppermute | solution.py:31
  138.1 8.5 %collective-permute-start.23 = (bf16[64,2048]{1,0:T(8,128)(2,1)}, bf16[64,2048]{1,0:T(8,128)(2,1)}, u32[]{:S(2)}, u32[]{:S(2)}) collective-permute-start(bf16[64,2048]{1,0:T(8,128)(2,1)} %get-tuple-element.66), channel_id=1, source_target_pairs={{0,2},{1,3},{2,0},{3,1},{4,6},{5,7},{6,4},{7,5},{8,10},{9,11},{10,... | collective-permute-start | bytes 786440 | tf_op jit(solution)/shard_map/ppermute | solution.py:31
  142.0 12.2 %all-to-all-start.2 = ((bf16[8,16,8,256]{3,2,1,0:T(8,128)(2,1)}), bf16[8,16,8,256]{3,2,1,0:T(8,128)(2,1)}, u32[]{:S(2)}, u32[]{:S(2)}) async-start(bf16[8,16,8,256]{3,2,1,0:T(8,128)(2,1)} %copy_bitcast_fusion.1), calls=%async_computation.2 | async-start | bytes 1048576 | tf_op jit(solution)/shard_map/all_to_all | solution.py:329
  157.2 24.0 %collective-permute-start.24 = (bf16[256,2048]{1,0:T(8,128)(2,1)S(1)}, bf16[256,2048]{1,0:T(8,128)(2,1)}, u32[]{:S(2)}, u32[]{:S(2)}) collective-permute-start(bf16[256,2048]{1,0:T(8,128)(2,1)S(1)} %constant_dynamic-update-slice_fusion.2.refs_0_), channel_id=1, source_target_pairs={{0,2},{1,3},{2,0},{3,1},{4,6},{5,7},{6,4},{7,5},{8,10},{9,11},{10,... | collective-permute-start | bytes 3145736 | tf_op jit(solution)/shard_map/ppermute | solution.py:31
  159.9 24.5 %collective-permute-start.29 = (bf16[128,2048]{1,0:T(8,128)(2,1)S(1)}, bf16[128,2048]{1,0:T(8,128)(2,1)}, u32[]{:S(2)}, u32[]{:S(2)}) collective-permute-start(bf16[128,2048]{1,0:T(8,128)(2,1)S(1)} %constant_dynamic-update-slice_fusion.refs_0_), channel_id=1, source_target_pairs={{0,4},{1,5},{2,6},{3,7},{4,8},{5,9},{6,10},{7,11},{8,12},{9,13},{1... | collective-permute-start | bytes 1572872 | tf_op jit(solution)/shard_map/ppermute | solution.py:31
  160.5 26.3 %collective-permute-start.28 = (bf16[128,2048]{1,0:T(8,128)(2,1)S(1)}, bf16[128,2048]{1,0:T(8,128)(2,1)}, u32[]{:S(2)}, u32[]{:S(2)}) collective-permute-start(bf16[128,2048]{1,0:T(8,128)(2,1)S(1)} %constant_dynamic-update-slice_fusion.refs_0_), channel_id=1, source_target_pairs={{0,8},{1,9},{2,10},{3,11},{4,12},{5,13},{6,14},{7,15},{8,0},{9,1},... | collective-permute-start | bytes 1572872 | tf_op jit(solution)/shard_map/ppermute | solution.py:31
  162.3 24.5 %collective-permute-start.27 = (bf16[128,2048]{1,0:T(8,128)(2,1)S(1)}, bf16[128,2048]{1,0:T(8,128)(2,1)}, u32[]{:S(2)}, u32[]{:S(2)}) collective-permute-start(bf16[128,2048]{1,0:T(8,128)(2,1)S(1)} %constant_dynamic-update-slice_fusion.refs_0_), channel_id=1, source_target_pairs={{0,12},{1,13},{2,14},{3,15},{4,0},{5,1},{6,2},{7,3},{8,4},{9,5},{1... | collective-permute-start | bytes 1572872 | tf_op jit(solution)/shard_map/ppermute | solution.py:31
  165.2 39.4 %collective-permute-start.25 = (bf16[256,2048]{1,0:T(8,128)(2,1)S(1)}, bf16[256,2048]{1,0:T(8,128)(2,1)}, u32[]{:S(2)}, u32[]{:S(2)}) collective-permute-start(bf16[256,2048]{1,0:T(8,128)(2,1)S(1)} %constant_dynamic-update-slice_fusion.2.refs_0_), channel_id=1, source_target_pairs={{0,1},{1,0},{2,3},{3,2},{4,5},{5,4},{6,7},{7,6},{8,9},{9,8},{10,11... | collective-permute-start | bytes 3145736 | tf_op jit(solution)/shard_map/ppermute | solution.py:31
  181.2 23.4 %collective-permute-start.26 = (bf16[256,2048]{1,0:T(8,128)(2,1)}, bf16[256,2048]{1,0:T(8,128)(2,1)}, u32[]{:S(2)}, u32[]{:S(2)}) collective-permute-start(bf16[256,2048]{1,0:T(8,128)(2,1)} %collective-permute-done.24.refs_1_), channel_id=1, source_target_pairs={{0,1},{1,0},{2,3},{3,2},{4,5},{5,4},{6,7},{7,6},{8,9},{9,8},{10,11... | collective-permute-start | bytes 3145736 | tf_op jit(solution)/shard_map/ppermute | solution.py:31
  184.4 11.7 %collective-permute-start.33 = (bf16[128,2048]{1,0:T(8,128)(2,1)}, bf16[128,2048]{1,0:T(8,128)(2,1)}, u32[]{:S(2)}, u32[]{:S(2)}) collective-permute-start(bf16[128,2048]{1,0:T(8,128)(2,1)} %collective-permute-done.29.refs_3_), channel_id=1, source_target_pairs={{0,1},{1,0},{2,3},{3,2},{4,5},{5,4},{6,7},{7,6},{8,9},{9,8},{10,11... | collective-permute-start | bytes 1572872 | tf_op jit(solution)/shard_map/ppermute | solution.py:31
  186.8 9.3 %collective-permute-start.32 = (bf16[128,2048]{1,0:T(8,128)(2,1)}, bf16[128,2048]{1,0:T(8,128)(2,1)}, u32[]{:S(2)}, u32[]{:S(2)}) collective-permute-start(bf16[128,2048]{1,0:T(8,128)(2,1)} %collective-permute-done.28.refs_2_), channel_id=1, source_target_pairs={{0,1},{1,0},{2,3},{3,2},{4,5},{5,4},{6,7},{7,6},{8,9},{9,8},{10,11... | collective-permute-start | bytes 1572872 | tf_op jit(solution)/shard_map/ppermute | solution.py:31
  186.8 9.3 %collective-permute-start.31 = (bf16[128,2048]{1,0:T(8,128)(2,1)}, bf16[128,2048]{1,0:T(8,128)(2,1)}, u32[]{:S(2)}, u32[]{:S(2)}) collective-permute-start(bf16[128,2048]{1,0:T(8,128)(2,1)} %collective-permute-done.27.refs_1_), channel_id=1, source_target_pairs={{0,1},{1,0},{2,3},{3,2},{4,5},{5,4},{6,7},{7,6},{8,9},{9,8},{10,11... | collective-permute-start | bytes 1572872 | tf_op jit(solution)/shard_map/ppermute | solution.py:31
  189.4 22.3 %all-to-all-start.3 = ((bf16[16,80,256]{2,1,0:T(8,128)(2,1)}), bf16[16,80,256]{2,1,0:T(8,128)(2,1)}, u32[]{:S(2)}, u32[]{:S(2)}) async-start(bf16[16,80,256]{2,1,0:T(8,128)(2,1)} %pad_maximum_fusion.1), calls=%async_computation.3 | async-start | bytes 1310720 | tf_op jit(solution)/shard_map/all_to_all | solution.py:339
  (20 other events, 158.4 us)

commit v3 on v2

--- a/solution.py
+++ b/solution.py
@@ -235,7 +235,26 @@
     pick = onehot(route_list * cap + within, slots)
     back_pick = onehot(within // 8 * 80 + route_list * 8 + within % 8, NT * 80)
 
+    def moved(order, v):
+        return jnp.dot(order, v, preferred_element_type=BF16)
+
+    def packed(pick, v):
+        return lax.dot_general(pick, v, (((0,), (1,)), ((), ())), preferred_element_type=BF16)
+
+    early = packed(pick, jnp.concatenate([low_hidden, mid_hidden, cotangent], axis=0))
+    early = lax.all_to_all(early.reshape(trainers, cap, -1), "dp", 0, 0).reshape(slots, -1)
+
+    own, oth = oproj_partial(pos, o_proj, attn_out)
+    own = own + send(oth, dc=1)
+    w = jnp.transpose(fc_weight[0], (1, 0, 2))
+    w, own = lax.optimization_barrier((w, own))
+    w_other = send(w, dc=1)
+    narrow = own.astype(BF16)
+    sums = own[0]
+    for dx in range(1, NX):
+        sums = sums + send(narrow[dx], dx).astype(F32)
     at = jnp.arange(slots, dtype=jnp.int32)
+    at, sums = lax.optimization_barrier((at, sums))
     inner = at // 8 % 8 * cap + at % 8
     block = at // 64
 
@@ -253,24 +272,6 @@
     near_pick = onehot(towards * cap + within, slots)
     order_b = onehot((block // 8 * 8 + block % 4 * 2 + block // 4 % 2) * 64 + at % 64, slots)
 
-    def moved(order, v):
-        return jnp.dot(order, v, preferred_element_type=BF16)
-
-    def packed(pick, v):
-        return lax.dot_general(pick, v, (((0,), (1,)), ((), ())), preferred_element_type=BF16)
-
-    early = packed(pick, jnp.concatenate([low_hidden, mid_hidden, cotangent], axis=0))
-    early = lax.all_to_all(early.reshape(trainers, cap, -1), "dp", 0, 0).reshape(slots, -1)
-
-    own, oth = oproj_partial(pos, o_proj, attn_out)
-    own = own + send(oth, dc=1)
-    w = jnp.transpose(fc_weight[0], (1, 0, 2))
-    w, own = lax.optimization_barrier((w, own))
-    w_other = send(w, dc=1)
-    narrow = own.astype(BF16)
-    sums = own[0]
-    for dx in range(1, NX):
-        sums = sums + send(narrow[dx], dx).astype(F32)
     term = sums[0] + send(sums[1], dz=1)
     high_hidden = (high_resid.astype(F32) + term).astype(BF16)
 
@@ -335,6 +336,7 @@
     a0p, b0p = send(a0, dc=1), send(b0, dc=1)
     outputs = outputs.transpose(1, 0, 2, 3).reshape(NT, 64, 256)
     outputs = jnp.concatenate([outputs, gg], axis=1)
+    a1[0], outputs = lax.optimization_barrier((a1[0], outputs))
     a1p, b1p = [send(v, dc=1) for v in a1], send(b1, dc=1)
     returned = lax.all_to_all(outputs, "tensor", 0, 0)
     fc = grad(0, [a0] + a1 + [a0p] + a1p, xa)

time: 217 us -> 212 us (0.977)
  waiting for transfers between devices: 76.7 us -> 70.7 us
    ppermute x30, waiting for transfers between devices: 68.8 us -> 63.6 us  [send(): return lax.ppermute(v, 'tensor', shift(dx, dz, dc))]
    ppermute x30, starting transfers between devices: 43 us -> 47.6 us  [send(): return lax.ppermute(v, 'tensor', shift(dx, dz, dc))]
    all_to_all x1, starting transfers between devices: 6.67 us -> 4.42 us  [local(): returned = lax.all_to_all(outputs, 'tensor', 0, 0)]
    unnamed x32 -> x30, local copies, waits for them, and re-layouts: 5.97 us -> 5.96 us
  transfers between devices with their start and end apart: 38 -> 38, of which waited for: 16 -> 16; matrix products, arithmetic and copies ran while one was open for 11% -> 12% of each run, Pallas kernels for 10% -> 10%
where the time goes in v3:
time: 212 us; the launch traced here: 211 us
  starting transfers between devices  71.1 us (34%)
  waiting for transfers between devices  70.7 us (33%)
  Pallas kernels  32.5 us (15%)
  matrix products  16.7 us (8%)
  local copies, waits for them, and re-layouts  10.1 us (5%)
  other arithmetic  8.5 us (4%)
    ppermute x30, waiting for transfers between devices, send(): return lax.ppermute(v, 'tensor', shift(dx, dz, dc))  63.6 us
    ppermute x30, starting transfers between devices, send(): return lax.ppermute(v, 'tensor', shift(dx, dz, dc))  47.6 us
    pallas_call x2, Pallas kernels, grad(): pl.pallas_call(functools.partial(grad_kernel, len(gs)), grid=(steps,), in...  14.5 us
    pallas_call x2, Pallas kernels, join(): pl.pallas_call(functools.partial(join_kernel, which), grid=(width // tile...  12 us
    dot_general x6, matrix products, moved(): return jnp.dot(order, v, preferred_element_type=BF16)  12 us
    unnamed x30, local copies, waits for them, and re-layouts  5.96 us
    all_to_all x1, starting transfers between devices, local(): lax.all_to_all(early.reshape(trainers, cap, -1), 'dp', 0, 0)  5.76 us
    all_to_all x1, starting transfers between devices, local(): cot = lax.all_to_all(cot, 'tensor', 0, 0)  5.67 us
  transfers between devices with their start and end apart: 38, of which 16 were waited for; matrix products, arithmetic and copies ran while one was open for 12% of the time, Pallas kernels for 10%

profile of v3, /device:TPU:1, one launch (start us, length us, event | category | flops | bytes accessed | tf_op | source)
XLA Modules:
  0.0 210.8 jit_solution(8131670284801461729)
XLA Ops:
  1.7 4.4 %oproj_partial.1 = (f32[4,2,256,256]{3,2,1,0:T(8,128)S(1)}, f32[4,2,256,256]{3,2,1,0:T(8,128)S(1)}) custom-call(s32[3]{0:T(128)S(1)} %pad_add_fusion.pos, bf16[4096,512]{1,0:T(8,128)(2,1)} %o_ref.1, bf16[512,256]{1,0:T(8,128)(2,1)S(1)} %copy-done.3), custom_call_target="tpu_custom_call" | custom-call | flops 1073741824 | bytes 9437184 | tf_op jit(solution)/shard_map/oproj_partial/pallas_call | solution.py:61
  7.6 3.8 %collective-permute-done = f32[4,2,256,256]{3,2,1,0:T(8,128)S(1)} collective-permute-done((f32[4,2,256,256]{3,2,1,0:T(8,128)S(1)}, f32[4,2,256,256]{3,2,1,0:T(8,128)S(1)}, u32[]{:S(2)}, u32[]{:S(2)}) %collective-permute-start) | collective-permute-done | bytes 2097184 | tf_op jit(solution)/shard_map/ppermute | solution.py:31
  14.3 5.8 %all-to-all-start = ((bf16[8,128,768]{2,1,0:T(8,128)(2,1)}), bf16[8,128,768]{2,1,0:T(8,128)(2,1)}, u32[]{:S(2)}, u32[]{:S(2)}) async-start(bf16[8,128,768]{2,1,0:T(8,128)(2,1)} %bitcast.68), calls=%async_computation | async-start | bytes 3145728 | tf_op jit(solution)/shard_map/all_to_all | solution.py:245
  24.8 4.1 %collective-permute-done.1 = bf16[2,256,256]{2,1,0:T(8,128)(2,1)S(1)} collective-permute-done((bf16[2,256,256]{2,1,0:T(8,128)(2,1)S(1)}, bf16[2,256,256]{2,1,0:T(8,128)(2,1)S(1)}, u32[]{:S(2)}, u32[]{:S(2)}) %collective-permute-start.1) | collective-permute-done | bytes 262176 | tf_op jit(solution)/shard_map/ppermute | solution.py:31
  28.9 6.6 %collective-permute-done.2 = bf16[2,256,256]{2,1,0:T(8,128)(2,1)S(1)} collective-permute-done((bf16[2,256,256]{2,1,0:T(8,128)(2,1)S(1)}, bf16[2,256,256]{2,1,0:T(8,128)(2,1)S(1)}, u32[]{:S(2)}, u32[]{:S(2)}) %collective-permute-start.2) | collective-permute-done | bytes 262176 | tf_op jit(solution)/shard_map/ppermute | solution.py:31
  35.6 3.4 %collective-permute-start.4 = (f32[256,256]{1,0:T(8,128)S(1)}, f32[256,256]{1,0:T(8,128)S(1)}, u32[]{:S(2)}, u32[]{:S(2)}) collective-permute-start(f32[256,256]{1,0:T(8,128)S(1)} %slice_bitcast_fusion.3), channel_id=1, source_target_pairs={{0,2},{1,3},{2,0},{3,1},{4,6},{5,7},{6,4},{7,5},{8,10},{9,11},{10,... | collective-permute-start | bytes 786440 | tf_op jit(solution)/shard_map/ppermute | solution.py:31
  41.4 7.5 %collective-permute-done.4 = f32[256,256]{1,0:T(8,128)S(1)} collective-permute-done((f32[256,256]{1,0:T(8,128)S(1)}, f32[256,256]{1,0:T(8,128)S(1)}, u32[]{:S(2)}, u32[]{:S(2)}) %collective-permute-start.4) | collective-permute-done | bytes 262176 | tf_op jit(solution)/shard_map/ppermute | solution.py:31
  52.1 5.7 %all-to-all-start.1 = ((bf16[16,80,256]{2,1,0:T(8,128)(2,1)}), bf16[16,80,256]{2,1,0:T(8,128)(2,1)S(1)}, u32[]{:S(2)}, u32[]{:S(2)}) async-start(bf16[16,80,256]{2,1,0:T(8,128)(2,1)} %pad_maximum_fusion), calls=%async_computation.1 | async-start | bytes 1310720 | tf_op jit(solution)/shard_map/all_to_all | solution.py:292
  58.6 2.3 %collective-permute-start.9 = (bf16[2,128,256]{2,1,0:T(8,128)(2,1)S(1)}, bf16[2,128,256]{2,1,0:T(8,128)(2,1)S(1)}, u32[]{:S(2)}, u32[]{:S(2)}) collective-permute-start(bf16[2,128,256]{2,1,0:T(8,128)(2,1)S(1)} %get-tuple-element.97), channel_id=1, source_target_pairs={{0,96},{16,112},{32,0},{48,16},{64,32},{80,48},{96,64},{112,80},{1... | collective-permute-start | bytes 393224 | tf_op jit(solution)/shard_map/ppermute | solution.py:299
  61.6 2.2 %fusion.8 = bf16[512,512]{1,0:T(8,128)(2,1)S(1)} fusion(pred[1024,1024]{1,0:T(32,128)(4,1)} %iota_compare_fusion.3, bf16[1024,768]{1,0:T(8,128)(2,1)} %bitcast.10), kind=kOutput, calls=%fused_computation.13 | convolution fusion | flops 536870912 | bytes 2097152 | tf_op jit(solution)/shard_map/dot_general | solution.py:239
  72.3 6.0 %join.3 = (f32[256,2048]{1,0:T(8,128)S(1)}, bf16[256,2048]{1,0:T(8,128)(2,1)S(1)}) custom-call(bf16[512,512]{1,0:T(8,128)(2,1)S(1)} %fusion.10.xo_ref, bf16[512,512]{1,0:T(8,128)(2,1)S(1)} %collective-permute-done.5.xp_ref, bf16[512,256]{1,0:T(8,128)(2,1)S(1)} %fusion.6.ho_ref, bf16[512,256]{1,0:T(8,128)(2,1)S(1)} %collective-permute-done.10.hp_ref, ...), custom_call_target="tpu_custom_call" | custom-call | flops 3221225472 | bytes 9437184 | tf_op jit(solution)/shard_map/join/pallas_call | solution.py:104
  78.4 3.0 %collective-permute-start.15 = (bf16[256,2048]{1,0:T(8,128)(2,1)S(1)}, bf16[256,2048]{1,0:T(8,128)(2,1)S(1)}, u32[]{:S(2)}, u32[]{:S(2)}) collective-permute-start(bf16[256,2048]{1,0:T(8,128)(2,1)S(1)} %get-tuple-element.63), channel_id=1, source_target_pairs={{0,2},{1,3},{2,0},{3,1},{4,6},{5,7},{6,4},{7,5},{8,10},{9,11},{10,... | collective-permute-start | bytes 3145736 | tf_op jit(solution)/shard_map/ppermute | solution.py:31
  81.3 6.0 %join.2 = (f32[128,2048]{1,0:T(8,128)S(1)}, bf16[128,2048]{1,0:T(8,128)(2,1)S(1)}, bf16[128,2048]{1,0:T(8,128)(2,1)S(1)}, bf16[128,2048]{1,0:T(8,128)(2,1)S(1)}) custom-call(bf16[512,512]{1,0:T(8,128)(2,1)S(1)} %fusion.10.xo_ref, bf16[512,512]{1,0:T(8,128)(2,1)S(1)} %collective-permute-done.5.xp_ref, bf16[512,256]{1,0:T(8,128)(2,1)S(1)} %fusion.6.ho_ref, ...), custom_call_target="tpu_custom_call" | custom-call | flops 3221225472 | bytes 9437184 | tf_op jit(solution)/shard_map/join/pallas_call | solution.py:104
  88.6 2.4 %collective-permute-start.13 = (bf16[128,2048]{1,0:T(8,128)(2,1)S(1)}, bf16[128,2048]{1,0:T(8,128)(2,1)S(1)}, u32[]{:S(2)}, u32[]{:S(2)}) collective-permute-start(bf16[128,2048]{1,0:T(8,128)(2,1)S(1)} %get-tuple-element.60), channel_id=1, source_target_pairs={{0,8},{1,9},{2,10},{3,11},{4,12},{5,13},{6,14},{7,15},{8,0},{9,1},... | collective-permute-start | bytes 1572872 | tf_op jit(solution)/shard_map/ppermute | solution.py:31
  92.2 12.5 %collective-permute-done.15 = bf16[256,2048]{1,0:T(8,128)(2,1)S(1)} collective-permute-done((bf16[256,2048]{1,0:T(8,128)(2,1)S(1)}, bf16[256,2048]{1,0:T(8,128)(2,1)S(1)}, u32[]{:S(2)}, u32[]{:S(2)}) %collective-permute-start.15) | collective-permute-done | bytes 1048608 | tf_op jit(solution)/shard_map/ppermute | solution.py:31
  105.2 8.7 %collective-permute-done.13 = bf16[128,2048]{1,0:T(8,128)(2,1)S(1)} collective-permute-done((bf16[128,2048]{1,0:T(8,128)(2,1)S(1)}, bf16[128,2048]{1,0:T(8,128)(2,1)S(1)}, u32[]{:S(2)}, u32[]{:S(2)}) %collective-permute-start.13) | collective-permute-done | bytes 524320 | tf_op jit(solution)/shard_map/ppermute | solution.py:31
  114.6 2.6 %collective-permute-start.19 = (bf16[64,2048]{1,0:T(8,128)(2,1)S(1)}, bf16[64,2048]{1,0:T(8,128)(2,1)S(1)}, u32[]{:S(2)}, u32[]{:S(2)}) collective-permute-start(bf16[64,2048]{1,0:T(8,128)(2,1)S(1)} %get-tuple-element.89), channel_id=1, source_target_pairs={{0,12},{1,13},{2,14},{3,15},{4,0},{5,1},{6,2},{7,3},{8,4},{9,5},{1... | collective-permute-start | bytes 786440 | tf_op jit(solution)/shard_map/ppermute | solution.py:31
  117.8 4.1 %fusion.1.refs_4_ = bf16[1024,768]{1,0:T(8,128)(2,1)} fusion(s32[1024]{0:T(1024)S(1)} %get-tuple-element.99, bf16[512,256]{1,0:T(8,128)(2,1)} %fusion.4, bf16[512,256]{1,0:T(8,128)(2,1)S(1)} %fusion.6.ho_ref, bf16[512,512]{1,0:T(8,128)(2,1)S(1)} %fusion.8, bf16[512,512]{1,0:T(8,128)(2,1)S(1)} %fusion.10.xo_ref), kind=kOutput, calls=%fused_computation.5 | convolution fusion | flops 1617952768 | bytes 3149824 | tf_op jit(solution)/shard_map/dot_general | solution.py:239
  125.5 6.7 %collective-permute-done.17.rb1 = bf16[64,2048]{1,0:T(8,128)(2,1)S(1)} collective-permute-done((bf16[64,2048]{1,0:T(8,128)(2,1)S(1)}, bf16[64,2048]{1,0:T(8,128)(2,1)S(1)}, u32[]{:S(2)}, u32[]{:S(2)}) %collective-permute-start.17) | collective-permute-done | bytes 262176 | tf_op jit(solution)/shard_map/ppermute | solution.py:31
  134.3 2.2 %collective-permute-start.22 = (bf16[64,2048]{1,0:T(8,128)(2,1)S(1)}, bf16[64,2048]{1,0:T(8,128)(2,1)}, u32[]{:S(2)}, u32[]{:S(2)}) collective-permute-start(bf16[64,2048]{1,0:T(8,128)(2,1)S(1)} %get-tuple-element.72), channel_id=1, source_target_pairs={{0,12},{1,13},{2,14},{3,15},{4,0},{5,1},{6,2},{7,3},{8,4},{9,5},{1... | collective-permute-start | bytes 786440 | tf_op jit(solution)/shard_map/ppermute | solution.py:31
  137.3 2.9 %collective-permute-start.20 = (bf16[64,2048]{1,0:T(8,128)(2,1)}, bf16[64,2048]{1,0:T(8,128)(2,1)}, u32[]{:S(2)}, u32[]{:S(2)}) collective-permute-start(bf16[64,2048]{1,0:T(8,128)(2,1)} %get-tuple-element.71), channel_id=1, source_target_pairs={{0,2},{1,3},{2,0},{3,1},{4,6},{5,7},{6,4},{7,5},{8,10},{9,11},{10,... | collective-permute-start | bytes 786440 | tf_op jit(solution)/shard_map/ppermute | solution.py:31
  141.3 4.2 %all-to-all-start.2 = ((bf16[8,16,8,256]{3,2,1,0:T(8,128)(2,1)}), bf16[8,16,8,256]{3,2,1,0:T(8,128)(2,1)}, u32[]{:S(2)}, u32[]{:S(2)}) async-start(bf16[8,16,8,256]{3,2,1,0:T(8,128)(2,1)} %copy_bitcast_fusion.1), calls=%async_computation.2 | async-start | bytes 1048576 | tf_op jit(solution)/shard_map/all_to_all | solution.py:330
  148.3 5.1 %all-to-all-done.2 = bf16[8,16,8,256]{3,2,1,0:T(8,128)(2,1)} async-done(((bf16[8,16,8,256]{3,2,1,0:T(8,128)(2,1)}), bf16[8,16,8,256]{3,2,1,0:T(8,128)(2,1)}, u32[]{:S(2)}, u32[]{:S(2)}) %all-to-all-start.2) | async-done | bytes 524320 | tf_op jit(solution)/shard_map/all_to_all | solution.py:330
  160.1 4.0 %collective-permute-start.30 = (bf16[128,2048]{1,0:T(8,128)(2,1)S(1)}, bf16[128,2048]{1,0:T(8,128)(2,1)S(1)}, u32[]{:S(2)}, u32[]{:S(2)}) collective-permute-start(bf16[128,2048]{1,0:T(8,128)(2,1)S(1)} %constant_dynamic-update-slice_fusion.refs_0_), channel_id=1, source_target_pairs={{0,1},{1,0},{2,3},{3,2},{4,5},{5,4},{6,7},{7,6},{8,9},{9,8},{10,11... | collective-permute-start | bytes 1572872 | tf_op jit(solution)/shard_map/ppermute | solution.py:31
  164.1 3.3 %collective-permute-done.21.refs_1_ = bf16[128,2048]{1,0:T(8,128)(2,1)} collective-permute-done((bf16[128,2048]{1,0:T(8,128)(2,1)S(1)}, bf16[128,2048]{1,0:T(8,128)(2,1)}, u32[]{:S(2)}, u32[]{:S(2)}) %collective-permute-start.21) | collective-permute-done | bytes 524320 | tf_op jit(solution)/shard_map/ppermute | solution.py:31
  167.3 6.9 %collective-permute-start.26 = (bf16[256,2048]{1,0:T(8,128)(2,1)S(1)}, bf16[256,2048]{1,0:T(8,128)(2,1)}, u32[]{:S(2)}, u32[]{:S(2)}) collective-permute-start(bf16[256,2048]{1,0:T(8,128)(2,1)S(1)} %constant_dynamic-update-slice_fusion.2.refs_0_), channel_id=1, source_target_pairs={{0,1},{1,0},{2,3},{3,2},{4,5},{5,4},{6,7},{7,6},{8,9},{9,8},{10,11... | collective-permute-start | bytes 3145736 | tf_op jit(solution)/shard_map/ppermute | solution.py:31
  174.2 6.1 %collective-permute-done.25.refs_1_ = bf16[256,2048]{1,0:T(8,128)(2,1)} collective-permute-done((bf16[256,2048]{1,0:T(8,128)(2,1)S(1)}, bf16[256,2048]{1,0:T(8,128)(2,1)}, u32[]{:S(2)}, u32[]{:S(2)}) %collective-permute-start.25) | collective-permute-done | bytes 1048608 | tf_op jit(solution)/shard_map/ppermute | solution.py:31
  180.3 3.3 %collective-permute-start.27 = (bf16[256,2048]{1,0:T(8,128)(2,1)}, bf16[256,2048]{1,0:T(8,128)(2,1)}, u32[]{:S(2)}, u32[]{:S(2)}) collective-permute-start(bf16[256,2048]{1,0:T(8,128)(2,1)} %collective-permute-done.25.refs_1_), channel_id=1, source_target_pairs={{0,1},{1,0},{2,3},{3,2},{4,5},{5,4},{6,7},{7,6},{8,9},{9,8},{10,11... | collective-permute-start | bytes 3145736 | tf_op jit(solution)/shard_map/ppermute | solution.py:31
  187.0 4.4 %all-to-all-start.3 = ((bf16[16,80,256]{2,1,0:T(8,128)(2,1)}), bf16[16,80,256]{2,1,0:T(8,128)(2,1)}, u32[]{:S(2)}, u32[]{:S(2)}) async-start(bf16[16,80,256]{2,1,0:T(8,128)(2,1)} %pad_maximum_fusion.1), calls=%async_computation.3 | async-start | bytes 1310720 | tf_op jit(solution)/shard_map/all_to_all | solution.py:341
  192.6 7.3 %grad.2.refs_5_ = f32[3,4096,256]{2,1,0:T(8,128)} custom-call(bf16[128,2048]{1,0:T(8,128)(2,1)S(1)} %constant_dynamic-update-slice_fusion.refs_0_, bf16[128,2048]{1,0:T(8,128)(2,1)} %collective-permute-done.21.refs_1_, bf16[128,2048]{1,0:T(8,128)(2,1)} %collective-permute-done.28.refs_2_, bf16[128,2048]{1,0:T(8,128)(2,1)} %collective-permute-done.29.refs_3_, ...), custom_call_target="tpu_custom_call" | custom-call | flops 3221225472 | bytes 12582912 | tf_op jit(solution)/shard_map/grad/pallas_call | solution.py:196
  199.9 7.2 %grad.3 = f32[3,4096,256]{2,1,0:T(8,128)} custom-call(bf16[256,2048]{1,0:T(8,128)(2,1)S(1)} %constant_dynamic-update-slice_fusion.2.refs_0_, bf16[256,2048]{1,0:T(8,128)(2,1)} %collective-permute-done.25.refs_1_, bf16[256,2048]{1,0:T(8,128)(2,1)} %collective-permute-done.26.refs_2_, ...), custom_call_target="tpu_custom_call", output_to_operand_aliasing={{}: (5, {})} | custom-call | flops 3221225472 | bytes 12582912 | tf_op jit(solution)/shard_map/grad/pallas_call | solution.py:196
  208.5 2.3 %fusion.12 = bf16[256,256]{1,0:T(8,128)(2,1)} fusion(bf16[1280,256]{1,0:T(8,128)(2,1)} %bitcast.25, s32[256]{0:T(256)S(1)} %get-tuple-element.102), kind=kOutput, calls=%fused_computation.20 | convolution fusion | flops 168099840 | bytes 787456 | tf_op jit(solution)/shard_map/dot_general | solution.py:346
  (124 shorter events, 52.9 us)
Async XLA Ops:
  11.7 60.6 %collective-permute-start.11 = (bf16[3,4096,256]{2,1,0:T(8,128)(2,1)}, bf16[3,4096,256]{2,1,0:T(8,128)(2,1)}, u32[]{:S(2)}, u32[]{:S(2)}) collective-permute-start(bf16[3,4096,256]{2,1,0:T(8,128)(2,1)} %bitcast.1.w_ref), channel_id=1, source_target_pairs={{0,1},{1,0},{2,3},{3,2},{4,5},{5,4},{6,7},{7,6},{8,9},{9,8},{10,11... | collective-permute-start | bytes 18874376 | tf_op jit(solution)/shard_map/ppermute | solution.py:31
  14.3 34.6 %all-to-all-start = ((bf16[8,128,768]{2,1,0:T(8,128)(2,1)}), bf16[8,128,768]{2,1,0:T(8,128)(2,1)}, u32[]{:S(2)}, u32[]{:S(2)}) async-start(bf16[8,128,768]{2,1,0:T(8,128)(2,1)} %bitcast.68), calls=%async_computation | async-start | bytes 3145728 | tf_op jit(solution)/shard_map/all_to_all | solution.py:245
  20.3 8.6 %collective-permute-start.1 = (bf16[2,256,256]{2,1,0:T(8,128)(2,1)S(1)}, bf16[2,256,256]{2,1,0:T(8,128)(2,1)S(1)}, u32[]{:S(2)}, u32[]{:S(2)}) collective-permute-start(bf16[2,256,256]{2,1,0:T(8,128)(2,1)S(1)} %get-tuple-element.92), channel_id=1, source_target_pairs={{0,4},{1,5},{2,6},{3,7},{4,8},{5,9},{6,10},{7,11},{8,12},{9,13},{1... | collective-permute-start | bytes 786440 | tf_op jit(solution)/shard_map/ppermute | solution.py:31
  21.6 7.3 %collective-permute-start.3 = (bf16[2,256,256]{2,1,0:T(8,128)(2,1)S(1)}, bf16[2,256,256]{2,1,0:T(8,128)(2,1)S(1)}, u32[]{:S(2)}, u32[]{:S(2)}) collective-permute-start(bf16[2,256,256]{2,1,0:T(8,128)(2,1)S(1)} %get-tuple-element.93), channel_id=1, source_target_pairs={{0,12},{1,13},{2,14},{3,15},{4,0},{5,1},{6,2},{7,3},{8,4},{9,5},{1... | collective-permute-start | bytes 786440 | tf_op jit(solution)/shard_map/ppermute | solution.py:31
  23.0 12.4 %collective-permute-start.2 = (bf16[2,256,256]{2,1,0:T(8,128)(2,1)S(1)}, bf16[2,256,256]{2,1,0:T(8,128)(2,1)S(1)}, u32[]{:S(2)}, u32[]{:S(2)}) collective-permute-start(bf16[2,256,256]{2,1,0:T(8,128)(2,1)S(1)} %get-tuple-element.94), channel_id=1, source_target_pairs={{0,8},{1,9},{2,10},{3,11},{4,12},{5,13},{6,14},{7,15},{8,0},{9,1},... | collective-permute-start | bytes 786440 | tf_op jit(solution)/shard_map/ppermute | solution.py:31
  35.6 13.2 %collective-permute-start.4 = (f32[256,256]{1,0:T(8,128)S(1)}, f32[256,256]{1,0:T(8,128)S(1)}, u32[]{:S(2)}, u32[]{:S(2)}) collective-permute-start(f32[256,256]{1,0:T(8,128)S(1)} %slice_bitcast_fusion.3), channel_id=1, source_target_pairs={{0,2},{1,3},{2,0},{3,1},{4,6},{5,7},{6,4},{7,5},{8,10},{9,11},{10,... | collective-permute-start | bytes 786440 | tf_op jit(solution)/shard_map/ppermute | solution.py:31
  49.2 8.9 %collective-permute-start.6 = (bf16[512,256]{1,0:T(8,128)(2,1)S(1)}, bf16[512,256]{1,0:T(8,128)(2,1)S(1)}, u32[]{:S(2)}, u32[]{:S(2)}) collective-permute-start(bf16[512,256]{1,0:T(8,128)(2,1)S(1)} %convolution_convert_fusion.1), channel_id=1, source_target_pairs={{0,16},{16,0},{32,48},{48,32},{64,80},{80,64},{96,112},{112,96},{1... | collective-permute-start | bytes 786440 | tf_op jit(solution)/shard_map/ppermute | solution.py:296
  52.1 20.2 %all-to-all-start.1 = ((bf16[16,80,256]{2,1,0:T(8,128)(2,1)}), bf16[16,80,256]{2,1,0:T(8,128)(2,1)S(1)}, u32[]{:S(2)}, u32[]{:S(2)}) async-start(bf16[16,80,256]{2,1,0:T(8,128)(2,1)} %pad_maximum_fusion), calls=%async_computation.1 | async-start | bytes 1310720 | tf_op jit(solution)/shard_map/all_to_all | solution.py:292
  58.2 6.7 %collective-permute-start.7 = (bf16[2,128,256]{2,1,0:T(8,128)(2,1)S(1)}, bf16[2,128,256]{2,1,0:T(8,128)(2,1)S(1)}, u32[]{:S(2)}, u32[]{:S(2)}) collective-permute-start(bf16[2,128,256]{2,1,0:T(8,128)(2,1)S(1)} %get-tuple-element.96), channel_id=1, source_target_pairs={{0,32},{16,48},{32,64},{48,80},{64,96},{80,112},{96,0},{112,16},{1... | collective-permute-start | bytes 393224 | tf_op jit(solution)/shard_map/ppermute | solution.py:299
  58.6 6.2 %collective-permute-start.9 = (bf16[2,128,256]{2,1,0:T(8,128)(2,1)S(1)}, bf16[2,128,256]{2,1,0:T(8,128)(2,1)S(1)}, u32[]{:S(2)}, u32[]{:S(2)}) collective-permute-start(bf16[2,128,256]{2,1,0:T(8,128)(2,1)S(1)} %get-tuple-element.97), channel_id=1, source_target_pairs={{0,96},{16,112},{32,0},{48,16},{64,32},{80,48},{96,64},{112,80},{1... | collective-permute-start | bytes 393224 | tf_op jit(solution)/shard_map/ppermute | solution.py:299
  63.8 8.4 %collective-permute-start.5 = (bf16[512,512]{1,0:T(8,128)(2,1)S(1)}, bf16[512,512]{1,0:T(8,128)(2,1)S(1)}, u32[]{:S(2)}, u32[]{:S(2)}) collective-permute-start(bf16[512,512]{1,0:T(8,128)(2,1)S(1)} %fusion.8), channel_id=1, source_target_pairs={{0,1},{1,0},{2,3},{3,2},{4,5},{5,4},{6,7},{7,6},{8,9},{9,8},{10,11... | collective-permute-start | bytes 1572872 | tf_op jit(solution)/shard_map/ppermute | solution.py:31
  78.4 26.3 %collective-permute-start.15 = (bf16[256,2048]{1,0:T(8,128)(2,1)S(1)}, bf16[256,2048]{1,0:T(8,128)(2,1)S(1)}, u32[]{:S(2)}, u32[]{:S(2)}) collective-permute-start(bf16[256,2048]{1,0:T(8,128)(2,1)S(1)} %get-tuple-element.63), channel_id=1, source_target_pairs={{0,2},{1,3},{2,0},{3,1},{4,6},{5,7},{6,4},{7,5},{8,10},{9,11},{10,... | collective-permute-start | bytes 3145736 | tf_op jit(solution)/shard_map/ppermute | solution.py:31
  87.4 17.9 %collective-permute-start.12 = (bf16[128,2048]{1,0:T(8,128)(2,1)S(1)}, bf16[128,2048]{1,0:T(8,128)(2,1)S(1)}, u32[]{:S(2)}, u32[]{:S(2)}) collective-permute-start(bf16[128,2048]{1,0:T(8,128)(2,1)S(1)} %get-tuple-element.59), channel_id=1, source_target_pairs={{0,4},{1,5},{2,6},{3,7},{4,8},{5,9},{6,10},{7,11},{8,12},{9,13},{1... | collective-permute-start | bytes 1572872 | tf_op jit(solution)/shard_map/ppermute | solution.py:31
  88.6 25.3 %collective-permute-start.13 = (bf16[128,2048]{1,0:T(8,128)(2,1)S(1)}, bf16[128,2048]{1,0:T(8,128)(2,1)S(1)}, u32[]{:S(2)}, u32[]{:S(2)}) collective-permute-start(bf16[128,2048]{1,0:T(8,128)(2,1)S(1)} %get-tuple-element.60), channel_id=1, source_target_pairs={{0,8},{1,9},{2,10},{3,11},{4,12},{5,13},{6,14},{7,15},{8,0},{9,1},... | collective-permute-start | bytes 1572872 | tf_op jit(solution)/shard_map/ppermute | solution.py:31
  91.0 22.9 %collective-permute-start.14 = (bf16[128,2048]{1,0:T(8,128)(2,1)S(1)}, bf16[128,2048]{1,0:T(8,128)(2,1)S(1)}, u32[]{:S(2)}, u32[]{:S(2)}) collective-permute-start(bf16[128,2048]{1,0:T(8,128)(2,1)S(1)} %get-tuple-element.61), channel_id=1, source_target_pairs={{0,12},{1,13},{2,14},{3,15},{4,0},{5,1},{6,2},{7,3},{8,4},{9,5},{1... | collective-permute-start | bytes 1572872 | tf_op jit(solution)/shard_map/ppermute | solution.py:31
  114.3 8.8 %collective-permute-start.16 = (bf16[64,2048]{1,0:T(8,128)(2,1)S(1)}, bf16[64,2048]{1,0:T(8,128)(2,1)S(1)}, u32[]{:S(2)}, u32[]{:S(2)}) collective-permute-start(bf16[64,2048]{1,0:T(8,128)(2,1)S(1)} %slice.175), channel_id=1, source_target_pairs={{0,2},{1,3},{2,0},{3,1},{4,6},{5,7},{6,4},{7,5},{8,10},{9,11},{10,... | collective-permute-start | bytes 786440 | tf_op jit(solution)/shard_map/ppermute | solution.py:31
  114.6 9.1 %collective-permute-start.19 = (bf16[64,2048]{1,0:T(8,128)(2,1)S(1)}, bf16[64,2048]{1,0:T(8,128)(2,1)S(1)}, u32[]{:S(2)}, u32[]{:S(2)}) collective-permute-start(bf16[64,2048]{1,0:T(8,128)(2,1)S(1)} %get-tuple-element.89), channel_id=1, source_target_pairs={{0,12},{1,13},{2,14},{3,15},{4,0},{5,1},{6,2},{7,3},{8,4},{9,5},{1... | collective-permute-start | bytes 786440 | tf_op jit(solution)/shard_map/ppermute | solution.py:31
  117.2 8.3 %collective-permute-start.18 = (bf16[64,2048]{1,0:T(8,128)(2,1)S(1)}, bf16[64,2048]{1,0:T(8,128)(2,1)S(1)}, u32[]{:S(2)}, u32[]{:S(2)}) collective-permute-start(bf16[64,2048]{1,0:T(8,128)(2,1)S(1)} %get-tuple-element.90), channel_id=1, source_target_pairs={{0,8},{1,9},{2,10},{3,11},{4,12},{5,13},{6,14},{7,15},{8,0},{9,1},... | collective-permute-start | bytes 786440 | tf_op jit(solution)/shard_map/ppermute | solution.py:31
  117.3 14.9 %collective-permute-start.17 = (bf16[64,2048]{1,0:T(8,128)(2,1)S(1)}, bf16[64,2048]{1,0:T(8,128)(2,1)S(1)}, u32[]{:S(2)}, u32[]{:S(2)}) collective-permute-start(bf16[64,2048]{1,0:T(8,128)(2,1)S(1)} %get-tuple-element.91), channel_id=1, source_target_pairs={{0,4},{1,5},{2,6},{3,7},{4,8},{5,9},{6,10},{7,11},{8,12},{9,13},{1... | collective-permute-start | bytes 786440 | tf_op jit(solution)/shard_map/ppermute | solution.py:31
  133.8 14.2 %collective-permute-start.24 = (bf16[64,2048]{1,0:T(8,128)(2,1)S(1)}, bf16[64,2048]{1,0:T(8,128)(2,1)}, u32[]{:S(2)}, u32[]{:S(2)}) collective-permute-start(bf16[64,2048]{1,0:T(8,128)(2,1)S(1)} %get-tuple-element.72), channel_id=1, source_target_pairs={{0,4},{1,5},{2,6},{3,7},{4,8},{5,9},{6,10},{7,11},{8,12},{9,13},{1... | collective-permute-start | bytes 786440 | tf_op jit(solution)/shard_map/ppermute | solution.py:31
  133.8 14.2 %collective-permute-start.23 = (bf16[64,2048]{1,0:T(8,128)(2,1)S(1)}, bf16[64,2048]{1,0:T(8,128)(2,1)}, u32[]{:S(2)}, u32[]{:S(2)}) collective-permute-start(bf16[64,2048]{1,0:T(8,128)(2,1)S(1)} %get-tuple-element.72), channel_id=1, source_target_pairs={{0,8},{1,9},{2,10},{3,11},{4,12},{5,13},{6,14},{7,15},{8,0},{9,1},... | collective-permute-start | bytes 786440 | tf_op jit(solution)/shard_map/ppermute | solution.py:31
  134.3 14.1 %collective-permute-start.22 = (bf16[64,2048]{1,0:T(8,128)(2,1)S(1)}, bf16[64,2048]{1,0:T(8,128)(2,1)}, u32[]{:S(2)}, u32[]{:S(2)}) collective-permute-start(bf16[64,2048]{1,0:T(8,128)(2,1)S(1)} %get-tuple-element.72), channel_id=1, source_target_pairs={{0,12},{1,13},{2,14},{3,15},{4,0},{5,1},{6,2},{7,3},{8,4},{9,5},{1... | collective-permute-start | bytes 786440 | tf_op jit(solution)/shard_map/ppermute | solution.py:31
  137.3 8.4 %collective-permute-start.20 = (bf16[64,2048]{1,0:T(8,128)(2,1)}, bf16[64,2048]{1,0:T(8,128)(2,1)}, u32[]{:S(2)}, u32[]{:S(2)}) collective-permute-start(bf16[64,2048]{1,0:T(8,128)(2,1)} %get-tuple-element.71), channel_id=1, source_target_pairs={{0,2},{1,3},{2,0},{3,1},{4,6},{5,7},{6,4},{7,5},{8,10},{9,11},{10,... | collective-permute-start | bytes 786440 | tf_op jit(solution)/shard_map/ppermute | solution.py:31
  141.3 12.2 %all-to-all-start.2 = ((bf16[8,16,8,256]{3,2,1,0:T(8,128)(2,1)}), bf16[8,16,8,256]{3,2,1,0:T(8,128)(2,1)}, u32[]{:S(2)}, u32[]{:S(2)}) async-start(bf16[8,16,8,256]{3,2,1,0:T(8,128)(2,1)} %copy_bitcast_fusion.1), calls=%async_computation.2 | async-start | bytes 1048576 | tf_op jit(solution)/shard_map/all_to_all | solution.py:330
  156.4 23.9 %collective-permute-start.25 = (bf16[256,2048]{1,0:T(8,128)(2,1)S(1)}, bf16[256,2048]{1,0:T(8,128)(2,1)}, u32[]{:S(2)}, u32[]{:S(2)}) collective-permute-start(bf16[256,2048]{1,0:T(8,128)(2,1)S(1)} %constant_dynamic-update-slice_fusion.2.refs_0_), channel_id=1, source_target_pairs={{0,2},{1,3},{2,0},{3,1},{4,6},{5,7},{6,4},{7,5},{8,10},{9,11},{10,... | collective-permute-start | bytes 3145736 | tf_op jit(solution)/shard_map/ppermute | solution.py:31
  156.5 10.9 %collective-permute-start.21 = (bf16[128,2048]{1,0:T(8,128)(2,1)S(1)}, bf16[128,2048]{1,0:T(8,128)(2,1)}, u32[]{:S(2)}, u32[]{:S(2)}) collective-permute-start(bf16[128,2048]{1,0:T(8,128)(2,1)S(1)} %constant_dynamic-update-slice_fusion.refs_0_), channel_id=1, source_target_pairs={{0,12},{1,13},{2,14},{3,15},{4,0},{5,1},{6,2},{7,3},{8,4},{9,5},{1... | collective-permute-start | bytes 1572872 | tf_op jit(solution)/shard_map/ppermute | solution.py:31
  157.3 28.3 %collective-permute-start.29 = (bf16[128,2048]{1,0:T(8,128)(2,1)S(1)}, bf16[128,2048]{1,0:T(8,128)(2,1)}, u32[]{:S(2)}, u32[]{:S(2)}) collective-permute-start(bf16[128,2048]{1,0:T(8,128)(2,1)S(1)} %constant_dynamic-update-slice_fusion.refs_0_), channel_id=1, source_target_pairs={{0,4},{1,5},{2,6},{3,7},{4,8},{5,9},{6,10},{7,11},{8,12},{9,13},{1... | collective-permute-start | bytes 1572872 | tf_op jit(solution)/shard_map/ppermute | solution.py:31
  158.0 27.6 %collective-permute-start.28 = (bf16[128,2048]{1,0:T(8,128)(2,1)S(1)}, bf16[128,2048]{1,0:T(8,128)(2,1)}, u32[]{:S(2)}, u32[]{:S(2)}) collective-permute-start(bf16[128,2048]{1,0:T(8,128)(2,1)S(1)} %constant_dynamic-update-slice_fusion.refs_0_), channel_id=1, source_target_pairs={{0,8},{1,9},{2,10},{3,11},{4,12},{5,13},{6,14},{7,15},{8,0},{9,1},... | collective-permute-start | bytes 1572872 | tf_op jit(solution)/shard_map/ppermute | solution.py:31
  160.1 26.1 %collective-permute-start.30 = (bf16[128,2048]{1,0:T(8,128)(2,1)S(1)}, bf16[128,2048]{1,0:T(8,128)(2,1)S(1)}, u32[]{:S(2)}, u32[]{:S(2)}) collective-permute-start(bf16[128,2048]{1,0:T(8,128)(2,1)S(1)} %constant_dynamic-update-slice_fusion.refs_0_), channel_id=1, source_target_pairs={{0,1},{1,0},{2,3},{3,2},{4,5},{5,4},{6,7},{7,6},{8,9},{9,8},{10,11... | collective-permute-start | bytes 1572872 | tf_op jit(solution)/shard_map/ppermute | solution.py:31
  167.3 32.5 %collective-permute-start.26 = (bf16[256,2048]{1,0:T(8,128)(2,1)S(1)}, bf16[256,2048]{1,0:T(8,128)(2,1)}, u32[]{:S(2)}, u32[]{:S(2)}) collective-permute-start(bf16[256,2048]{1,0:T(8,128)(2,1)S(1)} %constant_dynamic-update-slice_fusion.2.refs_0_), channel_id=1, source_target_pairs={{0,1},{1,0},{2,3},{3,2},{4,5},{5,4},{6,7},{7,6},{8,9},{9,8},{10,11... | collective-permute-start | bytes 3145736 | tf_op jit(solution)/shard_map/ppermute | solution.py:31
  180.3 19.6 %collective-permute-start.27 = (bf16[256,2048]{1,0:T(8,128)(2,1)}, bf16[256,2048]{1,0:T(8,128)(2,1)}, u32[]{:S(2)}, u32[]{:S(2)}) collective-permute-start(bf16[256,2048]{1,0:T(8,128)(2,1)} %collective-permute-done.25.refs_1_), channel_id=1, source_target_pairs={{0,1},{1,0},{2,3},{3,2},{4,5},{5,4},{6,7},{7,6},{8,9},{9,8},{10,11... | collective-permute-start | bytes 3145736 | tf_op jit(solution)/shard_map/ppermute | solution.py:31
  187.0 20.1 %all-to-all-start.3 = ((bf16[16,80,256]{2,1,0:T(8,128)(2,1)}), bf16[16,80,256]{2,1,0:T(8,128)(2,1)}, u32[]{:S(2)}, u32[]{:S(2)}) async-start(bf16[16,80,256]{2,1,0:T(8,128)(2,1)} %pad_maximum_fusion.1), calls=%async_computation.3 | async-start | bytes 1310720 | tf_op jit(solution)/shard_map/all_to_all | solution.py:341
  (19 other events, 113.1 us)

commit v4 on v3

--- a/solution.py
+++ b/solution.py
@@ -272,7 +272,7 @@
     near_pick = onehot(towards * cap + within, slots)
     order_b = onehot((block // 8 * 8 + block % 4 * 2 + block // 4 % 2) * 64 + at % 64, slots)
 
-    term = sums[0] + send(sums[1], dz=1)
+    term = sums[0] + send(sums[1].astype(BF16), dz=1).astype(F32)
     high_hidden = (high_resid.astype(F32) + term).astype(BF16)
 
     early, high_hidden = lax.optimization_barrier((early, high_hidden))

time: 212 us -> 210 us (level)
  waiting for transfers between devices: 70.7 us -> 66.7 us
  starting transfers between devices: 71.1 us -> 73.4 us
    ppermute x30, waiting for transfers between devices: 63.6 us -> 59.3 us  [send(): return lax.ppermute(v, 'tensor', shift(dx, dz, dc))]
  transfers between devices with their start and end apart: 38 -> 38, of which waited for: 16 -> 18; matrix products, arithmetic and copies ran while one was open for 12% -> 12% of each run, Pallas kernels for 10% -> 10%
where the time goes in v4:
time: 210 us; the launch traced here: 209 us
  starting transfers between devices  73.4 us (35%)
  waiting for transfers between devices  66.7 us (32%)
  Pallas kernels  32.5 us (15%)
  matrix products  16.7 us (8%)
  local copies, waits for them, and re-layouts  10.1 us (5%)
  other arithmetic  8.5 us (4%)
    ppermute x30, waiting for transfers between devices, send(): return lax.ppermute(v, 'tensor', shift(dx, dz, dc))  59.3 us
    ppermute x30, starting transfers between devices, send(): return lax.ppermute(v, 'tensor', shift(dx, dz, dc))  49.1 us
    pallas_call x2, Pallas kernels, grad(): pl.pallas_call(functools.partial(grad_kernel, len(gs)), grid=(steps,), in...  14.4 us
    pallas_call x2, Pallas kernels, join(): pl.pallas_call(functools.partial(join_kernel, which), grid=(width // tile...  12.1 us
    dot_general x6, matrix products, moved(): return jnp.dot(order, v, preferred_element_type=BF16)  12 us
    all_to_all x1, starting transfers between devices, local(): cot = lax.all_to_all(cot, 'tensor', 0, 0)  6.73 us
    unnamed x30, local copies, waits for them, and re-layouts  5.96 us
    all_to_all x1, starting transfers between devices, local(): lax.all_to_all(early.reshape(trainers, cap, -1), 'dp', 0, 0)  5.76 us
  transfers between devices with their start and end apart: 38, of which 18 were waited for; matrix products, arithmetic and copies ran while one was open for 12% of the time, Pallas kernels for 10%

profile of v4, /device:TPU:1, one launch (start us, length us, event | category | flops | bytes accessed | tf_op | source)
XLA Modules:
  0.0 209.0 jit_solution(3679961707432111448)
XLA Ops:
  1.7 4.4 %oproj_partial.1 = (f32[4,2,256,256]{3,2,1,0:T(8,128)S(1)}, f32[4,2,256,256]{3,2,1,0:T(8,128)S(1)}) custom-call(s32[3]{0:T(128)S(1)} %pad_add_fusion.pos, bf16[4096,512]{1,0:T(8,128)(2,1)} %o_ref.1, bf16[512,256]{1,0:T(8,128)(2,1)S(1)} %copy-done.3), custom_call_target="tpu_custom_call" | custom-call | flops 1073741824 | bytes 9437184 | tf_op jit(solution)/shard_map/oproj_partial/pallas_call | solution.py:61
  7.6 3.8 %collective-permute-done = f32[4,2,256,256]{3,2,1,0:T(8,128)S(1)} collective-permute-done((f32[4,2,256,256]{3,2,1,0:T(8,128)S(1)}, f32[4,2,256,256]{3,2,1,0:T(8,128)S(1)}, u32[]{:S(2)}, u32[]{:S(2)}) %collective-permute-start) | collective-permute-done | bytes 2097184 | tf_op jit(solution)/shard_map/ppermute | solution.py:31
  14.3 5.8 %all-to-all-start = ((bf16[8,128,768]{2,1,0:T(8,128)(2,1)}), bf16[8,128,768]{2,1,0:T(8,128)(2,1)}, u32[]{:S(2)}, u32[]{:S(2)}) async-start(bf16[8,128,768]{2,1,0:T(8,128)(2,1)} %bitcast.68), calls=%async_computation | async-start | bytes 3145728 | tf_op jit(solution)/shard_map/all_to_all | solution.py:245
  24.8 4.1 %collective-permute-done.1 = bf16[2,256,256]{2,1,0:T(8,128)(2,1)S(1)} collective-permute-done((bf16[2,256,256]{2,1,0:T(8,128)(2,1)S(1)}, bf16[2,256,256]{2,1,0:T(8,128)(2,1)S(1)}, u32[]{:S(2)}, u32[]{:S(2)}) %collective-permute-start.1) | collective-permute-done | bytes 262176 | tf_op jit(solution)/shard_map/ppermute | solution.py:31
  28.9 6.6 %collective-permute-done.2 = bf16[2,256,256]{2,1,0:T(8,128)(2,1)S(1)} collective-permute-done((bf16[2,256,256]{2,1,0:T(8,128)(2,1)S(1)}, bf16[2,256,256]{2,1,0:T(8,128)(2,1)S(1)}, u32[]{:S(2)}, u32[]{:S(2)}) %collective-permute-start.2) | collective-permute-done | bytes 262176 | tf_op jit(solution)/shard_map/ppermute | solution.py:31
  35.6 3.4 %collective-permute-start.4 = (bf16[256,256]{1,0:T(8,128)(2,1)S(1)}, bf16[256,256]{1,0:T(8,128)(2,1)S(1)}, u32[]{:S(2)}, u32[]{:S(2)}) collective-permute-start(bf16[256,256]{1,0:T(8,128)(2,1)S(1)} %fusion.30), channel_id=1, source_target_pairs={{0,2},{1,3},{2,0},{3,1},{4,6},{5,7},{6,4},{7,5},{8,10},{9,11},{10,... | collective-permute-start | bytes 393224 | tf_op jit(solution)/shard_map/ppermute | solution.py:31
  41.4 4.7 %collective-permute-done.4 = bf16[256,256]{1,0:T(8,128)(2,1)S(1)} collective-permute-done((bf16[256,256]{1,0:T(8,128)(2,1)S(1)}, bf16[256,256]{1,0:T(8,128)(2,1)S(1)}, u32[]{:S(2)}, u32[]{:S(2)}) %collective-permute-start.4) | collective-permute-done | bytes 131104 | tf_op jit(solution)/shard_map/ppermute | solution.py:31
  49.3 6.7 %all-to-all-start.1 = ((bf16[16,80,256]{2,1,0:T(8,128)(2,1)}), bf16[16,80,256]{2,1,0:T(8,128)(2,1)S(1)}, u32[]{:S(2)}, u32[]{:S(2)}) async-start(bf16[16,80,256]{2,1,0:T(8,128)(2,1)} %pad_maximum_fusion), calls=%async_computation.1 | async-start | bytes 1310720 | tf_op jit(solution)/shard_map/all_to_all | solution.py:292
  56.5 2.7 %collective-permute-start.9 = (bf16[2,128,256]{2,1,0:T(8,128)(2,1)S(1)}, bf16[2,128,256]{2,1,0:T(8,128)(2,1)S(1)}, u32[]{:S(2)}, u32[]{:S(2)}) collective-permute-start(bf16[2,128,256]{2,1,0:T(8,128)(2,1)S(1)} %get-tuple-element.97), channel_id=1, source_target_pairs={{0,96},{16,112},{32,0},{48,16},{64,32},{80,48},{96,64},{112,80},{1... | collective-permute-start | bytes 393224 | tf_op jit(solution)/shard_map/ppermute | solution.py:299
  59.5 2.2 %fusion.8 = bf16[512,512]{1,0:T(8,128)(2,1)S(1)} fusion(pred[1024,1024]{1,0:T(32,128)(4,1)} %iota_compare_fusion.3, bf16[1024,768]{1,0:T(8,128)(2,1)} %bitcast.10), kind=kOutput, calls=%fused_computation.13 | convolution fusion | flops 536870912 | bytes 2097152 | tf_op jit(solution)/shard_map/dot_general | solution.py:239
  70.6 6.1 %join.3 = (f32[256,2048]{1,0:T(8,128)S(1)}, bf16[256,2048]{1,0:T(8,128)(2,1)S(1)}) custom-call(bf16[512,512]{1,0:T(8,128)(2,1)S(1)} %fusion.10.xo_ref, bf16[512,512]{1,0:T(8,128)(2,1)S(1)} %collective-permute-done.5.xp_ref, bf16[512,256]{1,0:T(8,128)(2,1)S(1)} %fusion.6.ho_ref, bf16[512,256]{1,0:T(8,128)(2,1)S(1)} %collective-permute-done.10.hp_ref, ...), custom_call_target="tpu_custom_call" | custom-call | flops 3221225472 | bytes 9437184 | tf_op jit(solution)/shard_map/join/pallas_call | solution.py:104
  76.6 3.0 %collective-permute-start.15 = (bf16[256,2048]{1,0:T(8,128)(2,1)S(1)}, bf16[256,2048]{1,0:T(8,128)(2,1)S(1)}, u32[]{:S(2)}, u32[]{:S(2)}) collective-permute-start(bf16[256,2048]{1,0:T(8,128)(2,1)S(1)} %get-tuple-element.63), channel_id=1, source_target_pairs={{0,2},{1,3},{2,0},{3,1},{4,6},{5,7},{6,4},{7,5},{8,10},{9,11},{10,... | collective-permute-start | bytes 3145736 | tf_op jit(solution)/shard_map/ppermute | solution.py:31
  79.6 6.0 %join.2 = (f32[128,2048]{1,0:T(8,128)S(1)}, bf16[128,2048]{1,0:T(8,128)(2,1)S(1)}, bf16[128,2048]{1,0:T(8,128)(2,1)S(1)}, bf16[128,2048]{1,0:T(8,128)(2,1)S(1)}) custom-call(bf16[512,512]{1,0:T(8,128)(2,1)S(1)} %fusion.10.xo_ref, bf16[512,512]{1,0:T(8,128)(2,1)S(1)} %collective-permute-done.5.xp_ref, bf16[512,256]{1,0:T(8,128)(2,1)S(1)} %fusion.6.ho_ref, ...), custom_call_target="tpu_custom_call" | custom-call | flops 3221225472 | bytes 9437184 | tf_op jit(solution)/shard_map/join/pallas_call | solution.py:104
  86.9 2.4 %collective-permute-start.13 = (bf16[128,2048]{1,0:T(8,128)(2,1)S(1)}, bf16[128,2048]{1,0:T(8,128)(2,1)S(1)}, u32[]{:S(2)}, u32[]{:S(2)}) collective-permute-start(bf16[128,2048]{1,0:T(8,128)(2,1)S(1)} %get-tuple-element.60), channel_id=1, source_target_pairs={{0,8},{1,9},{2,10},{3,11},{4,12},{5,13},{6,14},{7,15},{8,0},{9,1},... | collective-permute-start | bytes 1572872 | tf_op jit(solution)/shard_map/ppermute | solution.py:31
  90.4 12.5 %collective-permute-done.15 = bf16[256,2048]{1,0:T(8,128)(2,1)S(1)} collective-permute-done((bf16[256,2048]{1,0:T(8,128)(2,1)S(1)}, bf16[256,2048]{1,0:T(8,128)(2,1)S(1)}, u32[]{:S(2)}, u32[]{:S(2)}) %collective-permute-start.15) | collective-permute-done | bytes 1048608 | tf_op jit(solution)/shard_map/ppermute | solution.py:31
  103.5 8.7 %collective-permute-done.13 = bf16[128,2048]{1,0:T(8,128)(2,1)S(1)} collective-permute-done((bf16[128,2048]{1,0:T(8,128)(2,1)S(1)}, bf16[128,2048]{1,0:T(8,128)(2,1)S(1)}, u32[]{:S(2)}, u32[]{:S(2)}) %collective-permute-start.13) | collective-permute-done | bytes 524320 | tf_op jit(solution)/shard_map/ppermute | solution.py:31
  112.8 2.6 %collective-permute-start.19 = (bf16[64,2048]{1,0:T(8,128)(2,1)S(1)}, bf16[64,2048]{1,0:T(8,128)(2,1)S(1)}, u32[]{:S(2)}, u32[]{:S(2)}) collective-permute-start(bf16[64,2048]{1,0:T(8,128)(2,1)S(1)} %get-tuple-element.89), channel_id=1, source_target_pairs={{0,12},{1,13},{2,14},{3,15},{4,0},{5,1},{6,2},{7,3},{8,4},{9,5},{1... | collective-permute-start | bytes 786440 | tf_op jit(solution)/shard_map/ppermute | solution.py:31
  116.1 4.1 %fusion.1.refs_4_ = bf16[1024,768]{1,0:T(8,128)(2,1)} fusion(s32[1024]{0:T(1024)S(1)} %get-tuple-element.99, bf16[512,256]{1,0:T(8,128)(2,1)} %fusion.4, bf16[512,256]{1,0:T(8,128)(2,1)S(1)} %fusion.6.ho_ref, bf16[512,512]{1,0:T(8,128)(2,1)S(1)} %fusion.8, bf16[512,512]{1,0:T(8,128)(2,1)S(1)} %fusion.10.xo_ref), kind=kOutput, calls=%fused_computation.5 | convolution fusion | flops 1617952768 | bytes 3149824 | tf_op jit(solution)/shard_map/dot_general | solution.py:239
  123.8 6.7 %collective-permute-done.17.rb1 = bf16[64,2048]{1,0:T(8,128)(2,1)S(1)} collective-permute-done((bf16[64,2048]{1,0:T(8,128)(2,1)S(1)}, bf16[64,2048]{1,0:T(8,128)(2,1)S(1)}, u32[]{:S(2)}, u32[]{:S(2)}) %collective-permute-start.17) | collective-permute-done | bytes 262176 | tf_op jit(solution)/shard_map/ppermute | solution.py:31
  132.6 2.2 %collective-permute-start.22 = (bf16[64,2048]{1,0:T(8,128)(2,1)S(1)}, bf16[64,2048]{1,0:T(8,128)(2,1)}, u32[]{:S(2)}, u32[]{:S(2)}) collective-permute-start(bf16[64,2048]{1,0:T(8,128)(2,1)S(1)} %get-tuple-element.72), channel_id=1, source_target_pairs={{0,12},{1,13},{2,14},{3,15},{4,0},{5,1},{6,2},{7,3},{8,4},{9,5},{1... | collective-permute-start | bytes 786440 | tf_op jit(solution)/shard_map/ppermute | solution.py:31
  135.6 2.9 %collective-permute-start.20 = (bf16[64,2048]{1,0:T(8,128)(2,1)}, bf16[64,2048]{1,0:T(8,128)(2,1)}, u32[]{:S(2)}, u32[]{:S(2)}) collective-permute-start(bf16[64,2048]{1,0:T(8,128)(2,1)} %get-tuple-element.71), channel_id=1, source_target_pairs={{0,2},{1,3},{2,0},{3,1},{4,6},{5,7},{6,4},{7,5},{8,10},{9,11},{10,... | collective-permute-start | bytes 786440 | tf_op jit(solution)/shard_map/ppermute | solution.py:31
  139.5 4.2 %all-to-all-start.2 = ((bf16[8,16,8,256]{3,2,1,0:T(8,128)(2,1)}), bf16[8,16,8,256]{3,2,1,0:T(8,128)(2,1)}, u32[]{:S(2)}, u32[]{:S(2)}) async-start(bf16[8,16,8,256]{3,2,1,0:T(8,128)(2,1)} %copy_bitcast_fusion.1), calls=%async_computation.2 | async-start | bytes 1048576 | tf_op jit(solution)/shard_map/all_to_all | solution.py:330
  146.6 5.0 %all-to-all-done.2 = bf16[8,16,8,256]{3,2,1,0:T(8,128)(2,1)} async-done(((bf16[8,16,8,256]{3,2,1,0:T(8,128)(2,1)}), bf16[8,16,8,256]{3,2,1,0:T(8,128)(2,1)}, u32[]{:S(2)}, u32[]{:S(2)}) %all-to-all-start.2) | async-done | bytes 524320 | tf_op jit(solution)/shard_map/all_to_all | solution.py:330
  158.5 4.6 %collective-permute-start.30 = (bf16[128,2048]{1,0:T(8,128)(2,1)S(1)}, bf16[128,2048]{1,0:T(8,128)(2,1)S(1)}, u32[]{:S(2)}, u32[]{:S(2)}) collective-permute-start(bf16[128,2048]{1,0:T(8,128)(2,1)S(1)} %constant_dynamic-update-slice_fusion.refs_0_), channel_id=1, source_target_pairs={{0,1},{1,0},{2,3},{3,2},{4,5},{5,4},{6,7},{7,6},{8,9},{9,8},{10,11... | collective-permute-start | bytes 1572872 | tf_op jit(solution)/shard_map/ppermute | solution.py:31
  163.1 2.8 %collective-permute-done.21.refs_1_ = bf16[128,2048]{1,0:T(8,128)(2,1)} collective-permute-done((bf16[128,2048]{1,0:T(8,128)(2,1)S(1)}, bf16[128,2048]{1,0:T(8,128)(2,1)}, u32[]{:S(2)}, u32[]{:S(2)}) %collective-permute-start.21) | collective-permute-done | bytes 524320 | tf_op jit(solution)/shard_map/ppermute | solution.py:31
  165.8 7.3 %collective-permute-start.26 = (bf16[256,2048]{1,0:T(8,128)(2,1)S(1)}, bf16[256,2048]{1,0:T(8,128)(2,1)}, u32[]{:S(2)}, u32[]{:S(2)}) collective-permute-start(bf16[256,2048]{1,0:T(8,128)(2,1)S(1)} %constant_dynamic-update-slice_fusion.2.refs_0_), channel_id=1, source_target_pairs={{0,1},{1,0},{2,3},{3,2},{4,5},{5,4},{6,7},{7,6},{8,9},{9,8},{10,11... | collective-permute-start | bytes 3145736 | tf_op jit(solution)/shard_map/ppermute | solution.py:31
  173.2 5.1 %collective-permute-done.25.refs_1_ = bf16[256,2048]{1,0:T(8,128)(2,1)} collective-permute-done((bf16[256,2048]{1,0:T(8,128)(2,1)S(1)}, bf16[256,2048]{1,0:T(8,128)(2,1)}, u32[]{:S(2)}, u32[]{:S(2)}) %collective-permute-start.25) | collective-permute-done | bytes 1048608 | tf_op jit(solution)/shard_map/ppermute | solution.py:31
  178.3 3.5 %collective-permute-start.27 = (bf16[256,2048]{1,0:T(8,128)(2,1)}, bf16[256,2048]{1,0:T(8,128)(2,1)}, u32[]{:S(2)}, u32[]{:S(2)}) collective-permute-start(bf16[256,2048]{1,0:T(8,128)(2,1)} %collective-permute-done.25.refs_1_), channel_id=1, source_target_pairs={{0,1},{1,0},{2,3},{3,2},{4,5},{5,4},{6,7},{7,6},{8,9},{9,8},{10,11... | collective-permute-start | bytes 3145736 | tf_op jit(solution)/shard_map/ppermute | solution.py:31
  185.2 4.4 %all-to-all-start.3 = ((bf16[16,80,256]{2,1,0:T(8,128)(2,1)}), bf16[16,80,256]{2,1,0:T(8,128)(2,1)}, u32[]{:S(2)}, u32[]{:S(2)}) async-start(bf16[16,80,256]{2,1,0:T(8,128)(2,1)} %pad_maximum_fusion.1), calls=%async_computation.3 | async-start | bytes 1310720 | tf_op jit(solution)/shard_map/all_to_all | solution.py:341
  190.8 7.3 %grad.2.refs_5_ = f32[3,4096,256]{2,1,0:T(8,128)} custom-call(bf16[128,2048]{1,0:T(8,128)(2,1)S(1)} %constant_dynamic-update-slice_fusion.refs_0_, bf16[128,2048]{1,0:T(8,128)(2,1)} %collective-permute-done.21.refs_1_, bf16[128,2048]{1,0:T(8,128)(2,1)} %collective-permute-done.28.refs_2_, bf16[128,2048]{1,0:T(8,128)(2,1)} %collective-permute-done.29.refs_3_, ...), custom_call_target="tpu_custom_call" | custom-call | flops 3221225472 | bytes 12582912 | tf_op jit(solution)/shard_map/grad/pallas_call | solution.py:196
  198.1 7.2 %grad.3 = f32[3,4096,256]{2,1,0:T(8,128)} custom-call(bf16[256,2048]{1,0:T(8,128)(2,1)S(1)} %constant_dynamic-update-slice_fusion.2.refs_0_, bf16[256,2048]{1,0:T(8,128)(2,1)} %collective-permute-done.25.refs_1_, bf16[256,2048]{1,0:T(8,128)(2,1)} %collective-permute-done.26.refs_2_, ...), custom_call_target="tpu_custom_call", output_to_operand_aliasing={{}: (5, {})} | custom-call | flops 3221225472 | bytes 12582912 | tf_op jit(solution)/shard_map/grad/pallas_call | solution.py:196
  206.7 2.2 %fusion.12 = bf16[256,256]{1,0:T(8,128)(2,1)} fusion(bf16[1280,256]{1,0:T(8,128)(2,1)} %bitcast.25, s32[256]{0:T(256)S(1)} %get-tuple-element.102), kind=kOutput, calls=%fused_computation.20 | convolution fusion | flops 168099840 | bytes 787456 | tf_op jit(solution)/shard_map/dot_general | solution.py:346
  (124 shorter events, 52.7 us)
Async XLA Ops:
  11.7 58.8 %collective-permute-start.11 = (bf16[3,4096,256]{2,1,0:T(8,128)(2,1)}, bf16[3,4096,256]{2,1,0:T(8,128)(2,1)}, u32[]{:S(2)}, u32[]{:S(2)}) collective-permute-start(bf16[3,4096,256]{2,1,0:T(8,128)(2,1)} %bitcast.1.w_ref), channel_id=1, source_target_pairs={{0,1},{1,0},{2,3},{3,2},{4,5},{5,4},{6,7},{7,6},{8,9},{9,8},{10,11... | collective-permute-start | bytes 18874376 | tf_op jit(solution)/shard_map/ppermute | solution.py:31
  14.3 31.8 %all-to-all-start = ((bf16[8,128,768]{2,1,0:T(8,128)(2,1)}), bf16[8,128,768]{2,1,0:T(8,128)(2,1)}, u32[]{:S(2)}, u32[]{:S(2)}) async-start(bf16[8,128,768]{2,1,0:T(8,128)(2,1)} %bitcast.68), calls=%async_computation | async-start | bytes 3145728 | tf_op jit(solution)/shard_map/all_to_all | solution.py:245
  20.3 8.6 %collective-permute-start.1 = (bf16[2,256,256]{2,1,0:T(8,128)(2,1)S(1)}, bf16[2,256,256]{2,1,0:T(8,128)(2,1)S(1)}, u32[]{:S(2)}, u32[]{:S(2)}) collective-permute-start(bf16[2,256,256]{2,1,0:T(8,128)(2,1)S(1)} %get-tuple-element.92), channel_id=1, source_target_pairs={{0,4},{1,5},{2,6},{3,7},{4,8},{5,9},{6,10},{7,11},{8,12},{9,13},{1... | collective-permute-start | bytes 786440 | tf_op jit(solution)/shard_map/ppermute | solution.py:31
  21.6 7.3 %collective-permute-start.3 = (bf16[2,256,256]{2,1,0:T(8,128)(2,1)S(1)}, bf16[2,256,256]{2,1,0:T(8,128)(2,1)S(1)}, u32[]{:S(2)}, u32[]{:S(2)}) collective-permute-start(bf16[2,256,256]{2,1,0:T(8,128)(2,1)S(1)} %get-tuple-element.93), channel_id=1, source_target_pairs={{0,12},{1,13},{2,14},{3,15},{4,0},{5,1},{6,2},{7,3},{8,4},{9,5},{1... | collective-permute-start | bytes 786440 | tf_op jit(solution)/shard_map/ppermute | solution.py:31
  23.0 12.4 %collective-permute-start.2 = (bf16[2,256,256]{2,1,0:T(8,128)(2,1)S(1)}, bf16[2,256,256]{2,1,0:T(8,128)(2,1)S(1)}, u32[]{:S(2)}, u32[]{:S(2)}) collective-permute-start(bf16[2,256,256]{2,1,0:T(8,128)(2,1)S(1)} %get-tuple-element.94), channel_id=1, source_target_pairs={{0,8},{1,9},{2,10},{3,11},{4,12},{5,13},{6,14},{7,15},{8,0},{9,1},... | collective-permute-start | bytes 786440 | tf_op jit(solution)/shard_map/ppermute | solution.py:31
  35.6 10.4 %collective-permute-start.4 = (bf16[256,256]{1,0:T(8,128)(2,1)S(1)}, bf16[256,256]{1,0:T(8,128)(2,1)S(1)}, u32[]{:S(2)}, u32[]{:S(2)}) collective-permute-start(bf16[256,256]{1,0:T(8,128)(2,1)S(1)} %fusion.30), channel_id=1, source_target_pairs={{0,2},{1,3},{2,0},{3,1},{4,6},{5,7},{6,4},{7,5},{8,10},{9,11},{10,... | collective-permute-start | bytes 393224 | tf_op jit(solution)/shard_map/ppermute | solution.py:31
  46.4 9.9 %collective-permute-start.6 = (bf16[512,256]{1,0:T(8,128)(2,1)S(1)}, bf16[512,256]{1,0:T(8,128)(2,1)S(1)}, u32[]{:S(2)}, u32[]{:S(2)}) collective-permute-start(bf16[512,256]{1,0:T(8,128)(2,1)S(1)} %convolution_convert_fusion.1), channel_id=1, source_target_pairs={{0,16},{16,0},{32,48},{48,32},{64,80},{80,64},{96,112},{112,96},{1... | collective-permute-start | bytes 786440 | tf_op jit(solution)/shard_map/ppermute | solution.py:296
  49.3 21.2 %all-to-all-start.1 = ((bf16[16,80,256]{2,1,0:T(8,128)(2,1)}), bf16[16,80,256]{2,1,0:T(8,128)(2,1)S(1)}, u32[]{:S(2)}, u32[]{:S(2)}) async-start(bf16[16,80,256]{2,1,0:T(8,128)(2,1)} %pad_maximum_fusion), calls=%async_computation.1 | async-start | bytes 1310720 | tf_op jit(solution)/shard_map/all_to_all | solution.py:292
  56.4 6.3 %collective-permute-start.7 = (bf16[2,128,256]{2,1,0:T(8,128)(2,1)S(1)}, bf16[2,128,256]{2,1,0:T(8,128)(2,1)S(1)}, u32[]{:S(2)}, u32[]{:S(2)}) collective-permute-start(bf16[2,128,256]{2,1,0:T(8,128)(2,1)S(1)} %get-tuple-element.96), channel_id=1, source_target_pairs={{0,32},{16,48},{32,64},{48,80},{64,96},{80,112},{96,0},{112,16},{1... | collective-permute-start | bytes 393224 | tf_op jit(solution)/shard_map/ppermute | solution.py:299
  56.5 8.0 %collective-permute-start.9 = (bf16[2,128,256]{2,1,0:T(8,128)(2,1)S(1)}, bf16[2,128,256]{2,1,0:T(8,128)(2,1)S(1)}, u32[]{:S(2)}, u32[]{:S(2)}) collective-permute-start(bf16[2,128,256]{2,1,0:T(8,128)(2,1)S(1)} %get-tuple-element.97), channel_id=1, source_target_pairs={{0,96},{16,112},{32,0},{48,16},{64,32},{80,48},{96,64},{112,80},{1... | collective-permute-start | bytes 393224 | tf_op jit(solution)/shard_map/ppermute | solution.py:299
  61.7 8.8 %collective-permute-start.5 = (bf16[512,512]{1,0:T(8,128)(2,1)S(1)}, bf16[512,512]{1,0:T(8,128)(2,1)S(1)}, u32[]{:S(2)}, u32[]{:S(2)}) collective-permute-start(bf16[512,512]{1,0:T(8,128)(2,1)S(1)} %fusion.8), channel_id=1, source_target_pairs={{0,1},{1,0},{2,3},{3,2},{4,5},{5,4},{6,7},{7,6},{8,9},{9,8},{10,11... | collective-permute-start | bytes 1572872 | tf_op jit(solution)/shard_map/ppermute | solution.py:31
  76.6 26.3 %collective-permute-start.15 = (bf16[256,2048]{1,0:T(8,128)(2,1)S(1)}, bf16[256,2048]{1,0:T(8,128)(2,1)S(1)}, u32[]{:S(2)}, u32[]{:S(2)}) collective-permute-start(bf16[256,2048]{1,0:T(8,128)(2,1)S(1)} %get-tuple-element.63), channel_id=1, source_target_pairs={{0,2},{1,3},{2,0},{3,1},{4,6},{5,7},{6,4},{7,5},{8,10},{9,11},{10,... | collective-permute-start | bytes 3145736 | tf_op jit(solution)/shard_map/ppermute | solution.py:31
  85.6 17.9 %collective-permute-start.12 = (bf16[128,2048]{1,0:T(8,128)(2,1)S(1)}, bf16[128,2048]{1,0:T(8,128)(2,1)S(1)}, u32[]{:S(2)}, u32[]{:S(2)}) collective-permute-start(bf16[128,2048]{1,0:T(8,128)(2,1)S(1)} %get-tuple-element.59), channel_id=1, source_target_pairs={{0,4},{1,5},{2,6},{3,7},{4,8},{5,9},{6,10},{7,11},{8,12},{9,13},{1... | collective-permute-start | bytes 1572872 | tf_op jit(solution)/shard_map/ppermute | solution.py:31
  86.9 25.3 %collective-permute-start.13 = (bf16[128,2048]{1,0:T(8,128)(2,1)S(1)}, bf16[128,2048]{1,0:T(8,128)(2,1)S(1)}, u32[]{:S(2)}, u32[]{:S(2)}) collective-permute-start(bf16[128,2048]{1,0:T(8,128)(2,1)S(1)} %get-tuple-element.60), channel_id=1, source_target_pairs={{0,8},{1,9},{2,10},{3,11},{4,12},{5,13},{6,14},{7,15},{8,0},{9,1},... | collective-permute-start | bytes 1572872 | tf_op jit(solution)/shard_map/ppermute | solution.py:31
  89.3 22.9 %collective-permute-start.14 = (bf16[128,2048]{1,0:T(8,128)(2,1)S(1)}, bf16[128,2048]{1,0:T(8,128)(2,1)S(1)}, u32[]{:S(2)}, u32[]{:S(2)}) collective-permute-start(bf16[128,2048]{1,0:T(8,128)(2,1)S(1)} %get-tuple-element.61), channel_id=1, source_target_pairs={{0,12},{1,13},{2,14},{3,15},{4,0},{5,1},{6,2},{7,3},{8,4},{9,5},{1... | collective-permute-start | bytes 1572872 | tf_op jit(solution)/shard_map/ppermute | solution.py:31
  112.5 8.8 %collective-permute-start.16 = (bf16[64,2048]{1,0:T(8,128)(2,1)S(1)}, bf16[64,2048]{1,0:T(8,128)(2,1)S(1)}, u32[]{:S(2)}, u32[]{:S(2)}) collective-permute-start(bf16[64,2048]{1,0:T(8,128)(2,1)S(1)} %slice.179), channel_id=1, source_target_pairs={{0,2},{1,3},{2,0},{3,1},{4,6},{5,7},{6,4},{7,5},{8,10},{9,11},{10,... | collective-permute-start | bytes 786440 | tf_op jit(solution)/shard_map/ppermute | solution.py:31
  112.8 9.1 %collective-permute-start.19 = (bf16[64,2048]{1,0:T(8,128)(2,1)S(1)}, bf16[64,2048]{1,0:T(8,128)(2,1)S(1)}, u32[]{:S(2)}, u32[]{:S(2)}) collective-permute-start(bf16[64,2048]{1,0:T(8,128)(2,1)S(1)} %get-tuple-element.89), channel_id=1, source_target_pairs={{0,12},{1,13},{2,14},{3,15},{4,0},{5,1},{6,2},{7,3},{8,4},{9,5},{1... | collective-permute-start | bytes 786440 | tf_op jit(solution)/shard_map/ppermute | solution.py:31
  115.4 8.3 %collective-permute-start.18 = (bf16[64,2048]{1,0:T(8,128)(2,1)S(1)}, bf16[64,2048]{1,0:T(8,128)(2,1)S(1)}, u32[]{:S(2)}, u32[]{:S(2)}) collective-permute-start(bf16[64,2048]{1,0:T(8,128)(2,1)S(1)} %get-tuple-element.90), channel_id=1, source_target_pairs={{0,8},{1,9},{2,10},{3,11},{4,12},{5,13},{6,14},{7,15},{8,0},{9,1},... | collective-permute-start | bytes 786440 | tf_op jit(solution)/shard_map/ppermute | solution.py:31
  115.6 14.9 %collective-permute-start.17 = (bf16[64,2048]{1,0:T(8,128)(2,1)S(1)}, bf16[64,2048]{1,0:T(8,128)(2,1)S(1)}, u32[]{:S(2)}, u32[]{:S(2)}) collective-permute-start(bf16[64,2048]{1,0:T(8,128)(2,1)S(1)} %get-tuple-element.91), channel_id=1, source_target_pairs={{0,4},{1,5},{2,6},{3,7},{4,8},{5,9},{6,10},{7,11},{8,12},{9,13},{1... | collective-permute-start | bytes 786440 | tf_op jit(solution)/shard_map/ppermute | solution.py:31
  132.1 14.2 %collective-permute-start.24 = (bf16[64,2048]{1,0:T(8,128)(2,1)S(1)}, bf16[64,2048]{1,0:T(8,128)(2,1)}, u32[]{:S(2)}, u32[]{:S(2)}) collective-permute-start(bf16[64,2048]{1,0:T(8,128)(2,1)S(1)} %get-tuple-element.72), channel_id=1, source_target_pairs={{0,4},{1,5},{2,6},{3,7},{4,8},{5,9},{6,10},{7,11},{8,12},{9,13},{1... | collective-permute-start | bytes 786440 | tf_op jit(solution)/shard_map/ppermute | solution.py:31
  132.1 14.2 %collective-permute-start.23 = (bf16[64,2048]{1,0:T(8,128)(2,1)S(1)}, bf16[64,2048]{1,0:T(8,128)(2,1)}, u32[]{:S(2)}, u32[]{:S(2)}) collective-permute-start(bf16[64,2048]{1,0:T(8,128)(2,1)S(1)} %get-tuple-element.72), channel_id=1, source_target_pairs={{0,8},{1,9},{2,10},{3,11},{4,12},{5,13},{6,14},{7,15},{8,0},{9,1},... | collective-permute-start | bytes 786440 | tf_op jit(solution)/shard_map/ppermute | solution.py:31
  132.6 14.1 %collective-permute-start.22 = (bf16[64,2048]{1,0:T(8,128)(2,1)S(1)}, bf16[64,2048]{1,0:T(8,128)(2,1)}, u32[]{:S(2)}, u32[]{:S(2)}) collective-permute-start(bf16[64,2048]{1,0:T(8,128)(2,1)S(1)} %get-tuple-element.72), channel_id=1, source_target_pairs={{0,12},{1,13},{2,14},{3,15},{4,0},{5,1},{6,2},{7,3},{8,4},{9,5},{1... | collective-permute-start | bytes 786440 | tf_op jit(solution)/shard_map/ppermute | solution.py:31
  135.6 8.4 %collective-permute-start.20 = (bf16[64,2048]{1,0:T(8,128)(2,1)}, bf16[64,2048]{1,0:T(8,128)(2,1)}, u32[]{:S(2)}, u32[]{:S(2)}) collective-permute-start(bf16[64,2048]{1,0:T(8,128)(2,1)} %get-tuple-element.71), channel_id=1, source_target_pairs={{0,2},{1,3},{2,0},{3,1},{4,6},{5,7},{6,4},{7,5},{8,10},{9,11},{10,... | collective-permute-start | bytes 786440 | tf_op jit(solution)/shard_map/ppermute | solution.py:31
  139.5 12.1 %all-to-all-start.2 = ((bf16[8,16,8,256]{3,2,1,0:T(8,128)(2,1)}), bf16[8,16,8,256]{3,2,1,0:T(8,128)(2,1)}, u32[]{:S(2)}, u32[]{:S(2)}) async-start(bf16[8,16,8,256]{3,2,1,0:T(8,128)(2,1)} %copy_bitcast_fusion.1), calls=%async_computation.2 | async-start | bytes 1048576 | tf_op jit(solution)/shard_map/all_to_all | solution.py:330
  154.6 23.7 %collective-permute-start.25 = (bf16[256,2048]{1,0:T(8,128)(2,1)S(1)}, bf16[256,2048]{1,0:T(8,128)(2,1)}, u32[]{:S(2)}, u32[]{:S(2)}) collective-permute-start(bf16[256,2048]{1,0:T(8,128)(2,1)S(1)} %constant_dynamic-update-slice_fusion.2.refs_0_), channel_id=1, source_target_pairs={{0,2},{1,3},{2,0},{3,1},{4,6},{5,7},{6,4},{7,5},{8,10},{9,11},{10,... | collective-permute-start | bytes 3145736 | tf_op jit(solution)/shard_map/ppermute | solution.py:31
  155.2 10.6 %collective-permute-start.21 = (bf16[128,2048]{1,0:T(8,128)(2,1)S(1)}, bf16[128,2048]{1,0:T(8,128)(2,1)}, u32[]{:S(2)}, u32[]{:S(2)}) collective-permute-start(bf16[128,2048]{1,0:T(8,128)(2,1)S(1)} %constant_dynamic-update-slice_fusion.refs_0_), channel_id=1, source_target_pairs={{0,12},{1,13},{2,14},{3,15},{4,0},{5,1},{6,2},{7,3},{8,4},{9,5},{1... | collective-permute-start | bytes 1572872 | tf_op jit(solution)/shard_map/ppermute | solution.py:31
  155.8 28.0 %collective-permute-start.29 = (bf16[128,2048]{1,0:T(8,128)(2,1)S(1)}, bf16[128,2048]{1,0:T(8,128)(2,1)}, u32[]{:S(2)}, u32[]{:S(2)}) collective-permute-start(bf16[128,2048]{1,0:T(8,128)(2,1)S(1)} %constant_dynamic-update-slice_fusion.refs_0_), channel_id=1, source_target_pairs={{0,4},{1,5},{2,6},{3,7},{4,8},{5,9},{6,10},{7,11},{8,12},{9,13},{1... | collective-permute-start | bytes 1572872 | tf_op jit(solution)/shard_map/ppermute | solution.py:31
  156.7 27.1 %collective-permute-start.28 = (bf16[128,2048]{1,0:T(8,128)(2,1)S(1)}, bf16[128,2048]{1,0:T(8,128)(2,1)}, u32[]{:S(2)}, u32[]{:S(2)}) collective-permute-start(bf16[128,2048]{1,0:T(8,128)(2,1)S(1)} %constant_dynamic-update-slice_fusion.refs_0_), channel_id=1, source_target_pairs={{0,8},{1,9},{2,10},{3,11},{4,12},{5,13},{6,14},{7,15},{8,0},{9,1},... | collective-permute-start | bytes 1572872 | tf_op jit(solution)/shard_map/ppermute | solution.py:31
  158.5 25.8 %collective-permute-start.30 = (bf16[128,2048]{1,0:T(8,128)(2,1)S(1)}, bf16[128,2048]{1,0:T(8,128)(2,1)S(1)}, u32[]{:S(2)}, u32[]{:S(2)}) collective-permute-start(bf16[128,2048]{1,0:T(8,128)(2,1)S(1)} %constant_dynamic-update-slice_fusion.refs_0_), channel_id=1, source_target_pairs={{0,1},{1,0},{2,3},{3,2},{4,5},{5,4},{6,7},{7,6},{8,9},{9,8},{10,11... | collective-permute-start | bytes 1572872 | tf_op jit(solution)/shard_map/ppermute | solution.py:31
  165.8 32.3 %collective-permute-start.26 = (bf16[256,2048]{1,0:T(8,128)(2,1)S(1)}, bf16[256,2048]{1,0:T(8,128)(2,1)}, u32[]{:S(2)}, u32[]{:S(2)}) collective-permute-start(bf16[256,2048]{1,0:T(8,128)(2,1)S(1)} %constant_dynamic-update-slice_fusion.2.refs_0_), channel_id=1, source_target_pairs={{0,1},{1,0},{2,3},{3,2},{4,5},{5,4},{6,7},{7,6},{8,9},{9,8},{10,11... | collective-permute-start | bytes 3145736 | tf_op jit(solution)/shard_map/ppermute | solution.py:31
  178.3 19.8 %collective-permute-start.27 = (bf16[256,2048]{1,0:T(8,128)(2,1)}, bf16[256,2048]{1,0:T(8,128)(2,1)}, u32[]{:S(2)}, u32[]{:S(2)}) collective-permute-start(bf16[256,2048]{1,0:T(8,128)(2,1)} %collective-permute-done.25.refs_1_), channel_id=1, source_target_pairs={{0,1},{1,0},{2,3},{3,2},{4,5},{5,4},{6,7},{7,6},{8,9},{9,8},{10,11... | collective-permute-start | bytes 3145736 | tf_op jit(solution)/shard_map/ppermute | solution.py:31
  185.2 20.1 %all-to-all-start.3 = ((bf16[16,80,256]{2,1,0:T(8,128)(2,1)}), bf16[16,80,256]{2,1,0:T(8,128)(2,1)}, u32[]{:S(2)}, u32[]{:S(2)}) async-start(bf16[16,80,256]{2,1,0:T(8,128)(2,1)} %pad_maximum_fusion.1), calls=%async_computation.3 | async-start | bytes 1310720 | tf_op jit(solution)/shard_map/all_to_all | solution.py:341
  (19 other events, 108.9 us)
